TPU v7x, 128 devices: a whole 4x4x4 slice. The times are simulated.
128 devices in a mesh: pair: 16 (over z, y), virt: 8 (over x, core).
Axes of the slice: x: 4, y: 4, z: 4, core: 2. Of those that a mesh axis runs over, the one named last changes fastest.
Arguments:
- amplitudes: bfloat16 [1024, 32768], P('pair', 'virt'), may hold values from -6 to 6
- ladder_ints: bfloat16 [32768, 8, 4096], P('virt', None, 'pair'), may hold values from -0.09375 to 0.09375
- hole_ints: bfloat16 [1024, 1024], P('pair'), may hold values from -0.1875 to 0.1875
- tile_irrep: int32 [256], replicated, may hold values from 0 to 7, as said below
- pair_orbitals: int32 [1024, 2], P('pair'), may hold values from 0 to 199
- occ_energy: float32 [200], replicated, may hold values from -3 to -0.3
- pair_energy: float32 [32768], P('virt'), may hold values from 0.5 to 4
Outputs:
- residual: float32 [1024, 32768], P('pair', 'virt')
- update: bfloat16 [1024, 32768], P('pair', 'virt')
Inputs may be any that keep to these rules, and one draw needn't show every extreme that they name: `tile_irrep`: each aligned block of 8 consecutive tiles holds every label exactly once.
All inputs are finite; a program needn't handle non-finite values.
Results may differ from a plain program's by a relative error of at most 0.001.
Values may be sent and summed in bfloat16 or wider, within the bound.
No kernel may reach another device: no remote copies, remote signals or barrier semaphores. Data moves between devices by JAX's collectives and lax.ppermute only.
A program may use at most 192 MiB of HBM per device.

v0:
```python
import jax
import jax.numpy as jnp
from jax import lax
from jax.sharding import PartitionSpec as P

TW = 128


def local(amplitudes, ladder_ints, hole_ints, tile_irrep, pair_orbitals, occ_energy, pair_energy):
    rows_cd = ladder_ints.shape[0]
    outer = ladder_ints.shape[1]
    inner = ladder_ints.shape[2]
    pairs = hole_ints.shape[1]
    local_pairs = amplitudes.shape[0]
    virt_pos = lax.axis_index("virt")
    pair_pos = lax.axis_index("pair")
    cd_tiles = rows_cd // TW
    ab_tiles = inner // TW
    cd_irrep = lax.dynamic_slice_in_dim(tile_irrep, virt_pos * cd_tiles, cd_tiles, 0)
    label_grid = tile_irrep.reshape(outer, cd_tiles)
    ab_irrep = lax.dynamic_slice_in_dim(label_grid, pair_pos * ab_tiles, ab_tiles, 1)
    tile_mask = (cd_irrep[:, None, None] == ab_irrep[None, :, :]).astype(ladder_ints.dtype)
    masked = (
        ladder_ints.reshape(cd_tiles, TW, outer, ab_tiles, TW) * tile_mask[:, None, :, :, None]
    ).reshape(rows_cd, outer * inner)
    piece = lax.all_gather(amplitudes, "pair", axis=0, tiled=True)
    ladder = jnp.dot(piece, masked, preferred_element_type=jnp.float32)
    hole = jnp.dot(hole_ints, piece, preferred_element_type=jnp.float32)
    ladder, hole = (ladder, hole)
    regrouped = lax.all_to_all(
        ladder.reshape(pairs, outer, inner), "pair", split_axis=0, concat_axis=2, tiled=True
    )
    particle = lax.psum_scatter(regrouped, "virt", scatter_dimension=1, tiled=True)
    residual = particle.reshape(local_pairs, rows_cd) + hole
    orbital_range = jnp.arange(occ_energy.shape[0], dtype=jnp.int32)
    onehot = (pair_orbitals[:, :, None] == orbital_range[None, None, :]).astype(jnp.float32)
    occupied = jnp.sum(onehot * occ_energy[None, None, :], axis=(1, 2))
    denom = pair_energy[None, :] - occupied[:, None]
    update = (residual / denom).astype(jnp.bfloat16)
    return (residual, update)


def solution(mesh):
    placed = (
        P("pair", "virt"),
        P("virt", None, "pair"),
        P("pair", None),
        P(),
        P("pair", None),
        P(),
        P("virt"),
    )
    return jax.shard_map(
        local,
        mesh=mesh,
        in_specs=placed,
        out_specs=(P("pair", "virt"), P("pair", "virt")),
        check_vma=False,
    )
```

profile of v0, /device:TPU:1, one launch (start us, length us, event | category | flops | bytes accessed | tf_op | source)
XLA Modules:
  0.0 300.2 jit_solution(4230927393608967305)
XLA Ops:
  7.2 0.0 copy-start
  7.2 0.0 all-gather.2.cloned.1.call-start
  7.2 0.7 all-gather.2.cloned.1.call-update
  7.9 0.0 reduce-scatter.2.cloned.1.call-start
  8.0 0.8 reshape.28
  8.7 0.8 dynamic_slice.6
  9.5 0.1 constant_dynamic-slice_fusion
  9.5 0.1 compare_convert_fusion
  9.7 12.2 %mul.27 = bf16[32,128,8,2,128]{4,3,2,1,0:T(2,128)(2,1)} broadcast(bf16[32,8,2]{2,1,0:T(8,128)(2,1)S(1)} %compare_convert_fusion), dimensions={0,2,3} | broadcast | bytes 16778240 | tf_op jit(solution)/shard_map/mul | solution.py:24
  21.8 28.0 %mul.28 = bf16[4096,2048]{1,0:T(8,128)(2,1)} reshape(bf16[32,128,8,2,128]{4,3,2,1,0:T(2,128)(2,1)} %mul.27) | data formatting | bytes 33554432 | tf_op jit(solution)/shard_map/mul | solution.py:24
  49.8 16.3 %copy.16 = bf16[512,8,8,256]{3,1,2,0:T(8,128)(2,1)} copy(bf16[512,8,8,256]{3,2,1,0:T(8,128)(2,1)} %bitcast.18) | data formatting | bytes 33554432
  66.1 18.2 %all-gather.2.cloned.1.call-done = bf16[1024,4096]{1,0:T(8,128)(2,1)} async-done(((bf16[64,4096]{1,0:T(8,128)(2,1)}), bf16[1024,4096]{1,0:T(8,128)(2,1)}) %all-gather.2.cloned.1.call-update) | async-done | bytes 8388624 | tf_op jit(solution)/shard_map/all_gather | solution.py:26
  84.3 25.4 %fusion = f32[2048,1024]{1,0:T(8,128)} fusion(bf16[1024,4096]{1,0:T(8,128)(2,1)} %all-gather.2.cloned.1.call-done, bf16[4096,2048]{1,0:T(8,128)(2,1)} %bitcast.19, bf16[4096,2048]{1,0:T(8,128)(2,1)} %mul.28), kind=kOutput, calls=%fused_computation | convolution fusion | flops 17188257792 | bytes 50331648 | tf_op jit(solution)/shard_map/dot_general | solution.py:27
  109.7 9.3 %copy.14 = f32[1024,8,256]{2,1,0:T(8,128)} copy(f32[1024,8,256]{0,2,1:T(8,128)} %bitcast.20) | data formatting | bytes 16777216 | tf_op jit(solution)/shard_map/reshape | solution.py:31
  119.0 99.8 %all_to_all.18 = f32[1024,8,256]{2,1,0:T(8,128)S(1)} all-to-all(f32[1024,8,256]{2,1,0:T(8,128)} %copy.14), channel_id=1, replica_groups=mesh['pair'=16,'virt'=8] {'pair'}, dimensions={0} | all-to-all | bytes 16777216 | tf_op jit(solution)/shard_map/all_to_all | solution.py:30
  218.8 8.1 %copy.15 = f32[64,8,16,256]{3,2,0,1:T(8,128)} copy(f32[64,8,16,256]{3,1,0,2:T(8,128)S(1)} %bitcast.17) | data formatting | bytes 16777216 | tf_op jit(solution)/shard_map/all_to_all | solution.py:30
  226.8 9.4 %all_to_all.16 = f32[64,8,4096]{2,0,1:T(8,128)} reshape(f32[64,8,16,256]{3,2,0,1:T(8,128)} %copy.15) | data formatting | bytes 16777216 | tf_op jit(solution)/shard_map/all_to_all | solution.py:30
  236.2 0.0 reduce-scatter.2.cloned.1.call-update
  236.3 0.6 copy-done.2
  236.9 0.0 copy-done.3
  236.9 0.2 select_reduce_fusion
  237.1 49.9 %reduce-scatter.2.cloned.1.call-done = f32[64,1,4096]{2,0,1:T(8,128)} async-done(((f32[64,8,4096]{2,0,1:T(8,128)}), f32[64,1,4096]{2,0,1:T(8,128)}) %reduce-scatter.2.cloned.1.call-update) | async-done | bytes 1048592 | tf_op jit(solution)/shard_map/reduce_scatter | solution.py:33
  287.0 0.0 copy-done
  287.0 6.3 %divide_convert_fusion = (bf16[64,4096]{1,0:T(8,128)(2,1)}, f32[64,4096]{1,0:T(8,128)}) fusion(f32[64]{0:T(128)S(1)} %select_reduce_fusion, f32[4096]{0:T(1024)S(1)} %copy-done.1, bf16[64,1024]{1,0:T(8,128)(2,1)S(1)} %copy-done, bf16[1024,4096]{1,0:T(8,128)(2,1)} %all-gather.2.cloned.1.call-done, f32[64,1,4096]{2,0,1:T(8,128)} %reduce-scatter.2.cloned.1.call-done), kind=kOutput, calls=%fused_computation.3 | convolution fusion | flops 537919488 | bytes 11157760 | tf_op jit(solution)/shard_map/dot_general | solution.py:28
  (4 shorter events, 0.0 us)
Async XLA Ops:
  7.2 279.8 %copy-start = (bf16[64,1024]{1,0:T(8,128)(2,1)S(1)}, bf16[64,1024]{1,0:T(8,128)(2,1)}, u32[]{:S(2)}) copy-start(bf16[64,1024]{1,0:T(8,128)(2,1)} %param.9) | copy-start | bytes 393220
  7.2 77.1 %all-gather.2.cloned.1.call-start = ((), (), s32[]{:S(2)}) async-start(), calls=%async_computation.2 | async-start | bytes 8912896 | tf_op jit(solution)/shard_map/all_gather | solution.py:26
  7.9 279.1 %reduce-scatter.2.cloned.1.call-start = ((), (), s32[]{:S(2)}) async-start(), calls=%async_computation.3 | async-start | bytes 9437184 | tf_op jit(solution)/shard_map/reduce_scatter | solution.py:33
  236.2 0.7 copy-start.2
  236.2 0.7 copy-start.3
  236.2 50.8 %copy-start.1 = (f32[4096]{0:T(1024)S(1)}, f32[4096]{0:T(1024)}, u32[]{:S(2)}) copy-start(f32[4096]{0:T(1024)} %param.13) | copy-start | bytes 49156
Sparse Core Ops, SparseCore 0:
  10.2 74.0 all-gather.1
  236.4 50.5 reduce-scatter.1
where the time goes:
time: 302 us; the launch traced here: 300 us
  blocking collectives  99.8 us (33%)
  local copies, waits for them, and re-layouts  85.4 us (28%)
  waiting for transfers between devices  68.8 us (23%)
  matrix products  31.8 us (11%)
  between operations  14.1 us (5%)
    all_to_all x1, blocking collectives, local(): lax.all_to_all(ladder.reshape(pairs, outer, inner), 'pair', split_axis=0,...  99.8 us
    reduce_scatter x1, waiting for transfers between devices, local(): lax.psum_scatter(regrouped, 'virt', scatter_dimension=1, tiled=True)  49.9 us
    mul x2, local copies, waits for them, and re-layouts, local(): ladder_ints.reshape(cd_tiles, TW, outer, ab_tiles, TW)  40.1 us
    dot_general x1, matrix products, local(): ladder = jnp.dot(piece, masked, preferred_element_type=jnp.float32)  25.4 us
    all_gather x1, waiting for transfers between devices, local(): piece = lax.all_gather(amplitudes, 'pair', axis=0, tiled=True)  18.2 us
    all_to_all x2, local copies, waits for them, and re-layouts, local(): lax.all_to_all(ladder.reshape(pairs, outer, inner), 'pair', split_axis=0,...  17.5 us
    unnamed x9, local copies, waits for them, and re-layouts  17 us
    reshape x1, local copies, waits for them, and re-layouts, local(): ladder.reshape(pairs, outer, inner)  9.28 us
  transfers between devices with their start and end apart: 2, of which 2 were waited for; matrix products, arithmetic and copies ran while one was open for 19% of the time, Pallas kernels for 0%

commit v1 on v0

v1 whole, which is shorter than its diff:
```python
import functools

import jax
import jax.numpy as jnp
from jax import lax
from jax.experimental import pallas as pl
from jax.experimental.pallas import tpu as pltpu
from jax.sharding import Mesh
from jax.sharding import PartitionSpec as P

TW = 128
RING = 4
AXES = ("z", "y", "x", "core")
BF = jnp.bfloat16
F32 = jnp.float32
VMEM_LIMIT = 48 * 1024 * 1024
RELS = (0, -1, 1, 2)


def flat(z, y, x, c):
    return (((z % RING) * RING + y % RING) * RING + x % RING) * 2 + c


def perm_of(first, step):
    pairs = []
    for z in range(RING):
        for y in range(RING):
            for x in range(RING):
                for c in range(2):
                    if (c == 0) == first:
                        to = flat(z, y + step, x, c)
                    else:
                        to = flat(z + step, y, x, c)
                    pairs.append((flat(z, y, x, c), to))
    return pairs


def along(value, first, step):
    return lax.ppermute(value, AXES, perm_of(first, step))


def along_x(value, step):
    return lax.ppermute(value, "x", [(i, (i + step) % RING) for i in range(RING)])


def other_core(value):
    return lax.ppermute(value, "core", [(0, 1), (1, 0)])


def select_kernel(tab, *refs):
    blocks, out = refs[:4], refs[4]
    o = tab[pl.program_id(0) * 16 + 8]
    row = lax.broadcasted_iota(jnp.int32, (TW, 8 * TW), 0)
    col = lax.broadcasted_iota(jnp.int32, (TW, 8 * TW), 1)
    pick = jnp.where(col == row * 8 + o, 1.0, 0.0).astype(BF)
    for k in range(4):
        got = jnp.dot(pick, blocks[k][...], preferred_element_type=F32)
        out[0, k * TW:(k + 1) * TW, :] = got.astype(BF)


def select(tab, ints2d):
    specs = [
        pl.BlockSpec((8 * TW, TW), functools.partial(lambda i, t, k: (t[i * 16 + k], i % 2), k=k))
        for k in range(4)
    ]
    return pl.pallas_call(
        select_kernel,
        grid_spec=pltpu.PrefetchScalarGridSpec(
            num_scalar_prefetch=1,
            grid=(16,),
            in_specs=specs,
            out_specs=pl.BlockSpec((1, 4 * TW, TW), lambda i, t: (i, 0, 0)),
        ),
        out_shape=jax.ShapeDtypeStruct((16, 4 * TW, TW), BF),
        compiler_params=pltpu.CompilerParams(vmem_limit_bytes=VMEM_LIMIT),
        cost_estimate=pl.CostEstimate(
            flops=64 * 2 * TW * TW * 8 * TW, bytes_accessed=18 * 2**20, transcendentals=0
        ),
        name="select",
    )(tab, *([ints2d] * 4))


def ladder_kernel(tab, *refs, pieces):
    n = len(pieces)
    a_refs, w_refs, outs = refs[:n], refs[n:n + 2], refs[n + 2:n + 6]
    a_v, w_v, a_sem, w_sem = refs[n + 6:]
    copies = []
    at = 0
    for i in range(n):
        copies.append(
            pltpu.make_async_copy(a_refs[i], a_v.at[pl.ds(at, pieces[i])], a_sem.at[i])
        )
        at += pieces[i]
    w_copies = [
        [
            pltpu.make_async_copy(
                w_refs[s].at[pl.ds(4 * d, 4)], w_v.at[s, pl.ds(4 * d, 4)], w_sem.at[s, d]
            )
            for s in range(2)
        ]
        for d in range(RING)
    ]
    for cp in copies:
        cp.start()
    for pair in w_copies:
        for cp in pair:
            cp.start()
    for cp in copies:
        cp.wait()
    for d in range(RING):
        for cp in w_copies[d]:
            cp.wait()
        for q in range(4):
            ct = d * 4 + q
            cols = [
                a_v[:, pl.ds(pl.multiple_of(tab[ct * 16 + m] * TW, TW), TW)] for m in range(8)
            ]
            a = jnp.concatenate(cols, axis=1)
            w = jnp.concatenate([w_v[0, ct], w_v[1, ct ^ 2]], axis=0)
            outs[d][:, q * TW:(q + 1) * TW] = jnp.dot(a, w, preferred_element_type=F32)


def ladder(tab, a_list, w_own, w_other):
    pieces = tuple(a.shape[0] for a in a_list)
    rows, cols = sum(pieces), a_list[0].shape[1]
    n = len(pieces)
    return pl.pallas_call(
        functools.partial(ladder_kernel, pieces=pieces),
        in_specs=[pl.BlockSpec(memory_space=pltpu.SMEM)] + [pl.BlockSpec(memory_space=pl.ANY)] * (n + 2),
        out_specs=[pl.BlockSpec(memory_space=pltpu.VMEM)] * RING,
        out_shape=[jax.ShapeDtypeStruct((rows, 4 * TW), F32)] * RING,
        scratch_shapes=[
            pltpu.VMEM((rows, cols), BF),
            pltpu.VMEM((2, 16, 4 * TW, TW), BF),
            pltpu.SemaphoreType.DMA((n,)),
            pltpu.SemaphoreType.DMA((2, RING)),
        ],
        compiler_params=pltpu.CompilerParams(vmem_limit_bytes=VMEM_LIMIT),
        cost_estimate=pl.CostEstimate(
            flops=16 * 2 * rows * 8 * TW * TW, bytes_accessed=rows * cols * 2 + rows * 8192 + 4 * 2**20, transcendentals=0
        ),
        name="ladder",
    )(tab, *a_list, w_own, w_other)


def hole_kernel(h_ref, *refs):
    n = (len(refs) - 2) // 2
    for out, parts in ((refs[-2], refs[:n]), (refs[-1], refs[n:2 * n])):
        a = jnp.concatenate([r[...] for r in parts], axis=0)
        out[...] = jnp.dot(h_ref[...], a, preferred_element_type=F32)


def hole_part(h_rel, a_list, width):
    step = 1024
    steps = width // step
    rows = h_rel.shape[0]
    specs = [pl.BlockSpec((a.shape[0], step), lambda i: (0, i)) for a in a_list]
    specs2 = [pl.BlockSpec((a.shape[0], step), lambda i: (0, i + steps)) for a in a_list]
    return pl.pallas_call(
        hole_kernel,
        grid=(steps,),
        in_specs=[pl.BlockSpec(h_rel.shape, lambda i: (0, 0))] + specs + specs2,
        out_specs=[pl.BlockSpec((rows, step), lambda i: (0, i))] * 2,
        out_shape=[jax.ShapeDtypeStruct((rows, width), F32)] * 2,
        compiler_params=pltpu.CompilerParams(vmem_limit_bytes=VMEM_LIMIT),
        cost_estimate=pl.CostEstimate(
            flops=2 * rows * h_rel.shape[1] * 2 * width, bytes_accessed=10 * 2**20, transcendentals=0
        ),
        name="hole",
    )(h_rel, *a_list, *a_list)


def finish_kernel(where, keep0, keep1, keep2, keep3, got, hole_a, hole_b, occ, energy, res, upd):
    core = where[32]
    mine = pl.multiple_of(core * 32, 32)
    his = pl.multiple_of((1 - core) * 32, 32)
    keeps = (keep0, keep1, keep2, keep3)
    for i in range(16):
        for first, part, at in ((mine, keeps[i // 4][i % 4, :, :256], i), (his, got[i], 16 + i)):
            rows = pl.ds(first, 32)
            cols = pl.ds(pl.multiple_of(where[at] * 256, 256), 256)
            total = part + (hole_a[rows, cols] + hole_b[rows, cols])
            res[rows, cols] = total
            upd[rows, cols] = (total / (energy[:, cols] - occ[rows, :])).astype(BF)


def finish(where, keeps, got, hole_a, hole_b, occ, energy):
    shape = hole_a.shape
    vm = pl.BlockSpec(memory_space=pltpu.VMEM)
    return pl.pallas_call(
        finish_kernel,
        in_specs=[pl.BlockSpec(memory_space=pltpu.SMEM)] + [vm] * 9,
        out_specs=[vm, vm],
        out_shape=[jax.ShapeDtypeStruct(shape, F32), jax.ShapeDtypeStruct(shape, BF)],
        compiler_params=pltpu.CompilerParams(vmem_limit_bytes=VMEM_LIMIT),
        cost_estimate=pl.CostEstimate(flops=2**20, bytes_accessed=6 * 2**20, transcendentals=0),
        name="finish",
    )(where, *keeps, got, hole_a, hole_b, occ, energy)


def local(amplitudes, ladder_ints, hole_ints, tile_irrep, pair_orbitals, occ_energy, pair_energy):
    z, y, x, c = (lax.axis_index(name) for name in AXES)
    rows, width = amplitudes.shape
    half = rows // 2
    p = z * RING + y

    mine = lax.dynamic_slice_in_dim(amplitudes, c * half, half, 0)
    theirs = other_core(lax.dynamic_slice_in_dim(amplitudes, (1 - c) * half, half, 0))
    own = jnp.concatenate([mine, theirs], axis=1)

    i = jnp.arange(16, dtype=jnp.int32)
    rel = sum(jnp.where(i // 4 == k, jnp.int32(RELS[k] % RING), 0) for k in range(RING))
    o = 2 * ((x + rel) % RING) + (c + i // 2 % 2) % 2
    tile = o * 32 + 2 * p + i % 2
    t = jnp.arange(tile_irrep.shape[0], dtype=jnp.int32)
    label = jnp.sum(jnp.where(tile[:, None] == t[None, :], tile_irrep[None, :], 0), axis=1)
    m = jnp.arange(16, dtype=jnp.int32)
    v_of = 2 * x + (c + m // 4) % 2
    block = v_of * 4 + m % 4
    hit = (t[None, None, :] // 8 == block[None, :, None]) & (tile_irrep[None, None, :] == label[:, None, None])
    inside = jnp.sum(jnp.where(hit, t[None, None, :] % 8, 0), axis=2)
    offs = (m // 4 * 32 + m % 4 * 8)[None, :] + inside
    tab = jnp.where(m[None, :] < 8, offs, o[:, None]).reshape(256)

    w_own = select(tab, ladder_ints.reshape(-1, ladder_ints.shape[2]))
    w_other = other_core(w_own)

    r_m = along(own, True, 1)
    r_p = along(own, True, -1)
    s_a = jnp.concatenate([own, r_m], axis=0)
    r_2a = along(r_m[:half // 2], True, 1)
    r_2b = along(r_p[half // 2:], True, -1)
    s_b = jnp.concatenate([r_p, r_2a, r_2b], axis=0)
    q_ma = along(s_a, False, 1)
    q_pa = along(s_a, False, -1)
    q_mb = along(s_b, False, 1)
    q_pb = along(s_b, False, -1)
    q_2a = along(q_ma, False, 1)
    q_2b = along(q_pb, False, -1)
    a_list = [s_a, s_b, q_ma, q_mb, q_pa, q_pb, q_2a, q_2b]

    def summed(parts):
        out = ladder(tab, parts, w_own, w_other)
        return [out[0]] + [along_x(out[k], RELS[k]) for k in range(1, RING)]

    c1 = summed([s_a, s_b])
    c2 = summed([q_ma, q_mb, q_pa, q_pb])
    c3 = summed([q_2a, q_2b])
    block_rows = RING * half
    t_0 = sum(c1[1:], c1[0])
    t_m = sum((part[:block_rows] for part in c2[1:]), c2[0][:block_rows])
    t_p = sum((part[block_rows:] for part in c2[1:]), c2[0][block_rows:])
    t_2 = sum(c3[1:], c3[0])

    from_p = along(t_m, False, -1)
    from_m = along(t_p, False, 1)
    from_2 = along(t_2, False, 2)
    back = [t_0, from_m, from_p, from_2]
    keeps = []
    for k in range(RING):
        u = jnp.stack([b[k * half:(k + 1) * half] for b in back])
        keeps.append(u if k == 0 else along(u, True, RELS[k]))
    got = other_core(jnp.concatenate([u[:, :, 256:] for u in keeps], axis=0))

    j = jnp.arange(16 * half, dtype=jnp.int32)
    ds = sum(jnp.where(j // (4 * half) == k, jnp.int32(RELS[k] % RING), 0) for k in range(RING))
    df = sum(jnp.where(j // half % 4 == k, jnp.int32(RELS[k] % RING), 0) for k in range(RING))
    dz, dy = jnp.where(c == 0, ds, df), jnp.where(c == 0, df, ds)
    source = ((z + dz) % RING * RING + (y + dy) % RING) * rows + c * half + j % half
    onehot = (jnp.arange(hole_ints.shape[1], dtype=jnp.int32)[:, None] == source[None, :]).astype(BF)
    h_rel = jnp.dot(hole_ints, onehot, preferred_element_type=F32).astype(BF)
    hole_own, hole_send = hole_part(h_rel, a_list, width)
    hole_got = other_core(hole_send)

    i = jnp.arange(33, dtype=jnp.int32)
    kf = sum(jnp.where(i // 4 % 4 == k, jnp.int32(-RELS[k] % RING), 0) for k in range(RING))
    ks = sum(jnp.where(i % 4 == k, jnp.int32(RELS[k] % RING), 0) for k in range(RING))
    flip = (c + i // 16) % 2 == 0
    kz, ky = jnp.where(flip, ks, kf), jnp.where(flip, kf, ks)
    where = jnp.where(i == 32, c, (z + kz) % RING * RING + (y + ky) % RING)

    orbital = jnp.arange(occ_energy.shape[0], dtype=jnp.int32)
    picked = (pair_orbitals[:, :, None] == orbital[None, None, :]).astype(F32)
    occ = jnp.sum(picked * occ_energy[None, None, :], axis=(1, 2))[:, None]
    return finish(where, keeps, got, hole_own, hole_got, occ, pair_energy[None, :])


def solution(mesh):
    grid = Mesh(mesh.devices.reshape(RING, RING, RING, 2), AXES)
    pair, virt = ("z", "y"), ("x", "core")
    placed = (
        P(pair, virt),
        P(virt, None, pair),
        P(pair, None),
        P(),
        P(pair, None),
        P(),
        P(virt),
    )
    return jax.shard_map(
        local,
        mesh=grid,
        in_specs=placed,
        out_specs=(P(pair, virt), P(pair, virt)),
        check_vma=False,
    )
```

time: 302 us -> 145 us (0.48)
  blocking collectives: 99.8 us -> 0 us
  local copies, waits for them, and re-layouts: 85.4 us -> 8.31 us
  starting transfers between devices: 0.08 us -> 52 us
  Pallas kernels: 0 us -> 37.2 us
  matrix products: 31.8 us -> 0.46 us
  waiting for transfers between devices: 68.8 us -> 37.6 us
  between operations: 14.1 us -> 1.03 us
  other arithmetic: 0.28 us -> 6.92 us
    all_to_all x1 -> x0, blocking collectives: 99.8 us -> none  [local(): lax.all_to_all(ladder.reshape(pairs, outer, inner), 'pair', split_axis=0,...]
    ppermute x0 -> x29, starting transfers between devices: none -> 52 us  [the longest x16 28.8 us: along(): return lax.ppermute(value, AXES, perm_of(first, step))]
    reduce_scatter x1 -> x0, waiting for transfers between devices: 49.9 us -> none  [local(): lax.psum_scatter(regrouped, 'virt', scatter_dimension=1, tiled=True)]
    mul x2 -> x0, local copies, waits for them, and re-layouts: 40.1 us -> none  [local(): ladder_ints.reshape(cd_tiles, TW, outer, ab_tiles, TW)]
    ppermute x0 -> x29, waiting for transfers between devices: none -> 37.6 us  [the longest x9 21.4 us: along_x(): lax.ppermute(value, 'x', [(i, (i + step) % RING) for i in range(RING)])]
    pallas_call x0 -> x6, Pallas kernels: none -> 37.2 us  [the longest x1 14.8 us: select(): pl.pallas_call(select_kernel, grid_spec=pltpu.PrefetchScalarGridSpec(num_...]
    dot_general x2 -> x1, matrix products: 31.8 us -> 0.46 us  [local(): h_rel = jnp.dot(hole_ints, onehot, preferred_element_type=F32).astype(BF)]
    all_gather x1 -> x0, waiting for transfers between devices: 18.2 us -> none  [local(): piece = lax.all_gather(amplitudes, 'pair', axis=0, tiled=True)]
  transfers between devices with their start and end apart: 2 -> 29, of which waited for: 2 -> 10; matrix products, arithmetic and copies ran while one was open for 19% -> 5% of each run, Pallas kernels for 0% -> 24%
where the time goes in v1:
time: 145 us; the launch traced here: 144 us
  starting transfers between devices  52 us (36%)
  waiting for transfers between devices  37.6 us (26%)
  Pallas kernels  37.2 us (26%)
  local copies, waits for them, and re-layouts  8.31 us (6%)
  other arithmetic  6.92 us (5%)
    ppermute x16, starting transfers between devices, along(): return lax.ppermute(value, AXES, perm_of(first, step))  28.8 us
    ppermute x9, waiting for transfers between devices, along_x(): lax.ppermute(value, 'x', [(i, (i + step) % RING) for i in range(RING)])  21.4 us
    ppermute x9, starting transfers between devices, along_x(): lax.ppermute(value, 'x', [(i, (i + step) % RING) for i in range(RING)])  15.9 us
    pallas_call x1, Pallas kernels, select(): pl.pallas_call(select_kernel, grid_spec=pltpu.PrefetchScalarGridSpec(num_...  14.8 us
    ppermute x16, waiting for transfers between devices, along(): return lax.ppermute(value, AXES, perm_of(first, step))  14.7 us
    pallas_call x3, Pallas kernels, ladder(): pl.pallas_call(functools.partial(ladder_kernel, pieces=pieces), in_specs=...  14.5 us
    ppermute x4, starting transfers between devices, other_core(): return lax.ppermute(value, 'core', [(0, 1), (1, 0)])  7.35 us
    unnamed x36, local copies, waits for them, and re-layouts  5.91 us
  transfers between devices with their start and end apart: 29, of which 10 were waited for; matrix products, arithmetic and copies ran while one was open for 5% of the time, Pallas kernels for 24%

profile of v1, /device:TPU:1, one launch (start us, length us, event | category | flops | bytes accessed | tf_op | source)
XLA Modules:
  0.0 143.6 jit_solution(13055297899785888576)
XLA Ops:
  8.1 14.8 %select.158.refs_2_.refs_4_ = bf16[16,512,128]{2,1,0:T(8,128)(2,1)S(1)} custom-call(s32[256]{0:T(256)S(1)} %select_n.453.tab, bf16[32768,256]{1,0:T(8,128)(2,1)} %bitcast.39, bf16[32768,256]{1,0:T(8,128)(2,1)} %bitcast.40, bf16[32768,256]{1,0:T(8,128)(2,1)} %bitcast.41, bf16[32768,256]{1,0:T(8,128)(2,1)} %bitcast.42), custom_call_target="tpu_custom_call" | custom-call | flops 2147483648 | bytes 18874368 | tf_op jit(solution)/shard_map/select/pallas_call | solution.py:66
  23.0 3.7 %collective-permute-start.2 = (bf16[32,8192]{1,0:T(8,128)(2,1)}, bf16[32,8192]{1,0:T(8,128)(2,1)S(1)}, u32[]{:S(2)}, u32[]{:S(2)}) collective-permute-start(bf16[32,8192]{1,0:T(8,128)(2,1)} %pad_maximum_fusion.1), channel_id=1, source_target_pairs={{0,24},{1,97},{2,26},{3,99},{4,28},{5,101},{6,30},{7,103},{8,0},{9... | collective-permute-start | bytes 1572872 | tf_op jit(solution)/shard_map/ppermute | solution.py:39
  31.6 2.9 %collective-permute-done.2 = bf16[32,8192]{1,0:T(8,128)(2,1)S(1)} collective-permute-done((bf16[32,8192]{1,0:T(8,128)(2,1)}, bf16[32,8192]{1,0:T(8,128)(2,1)S(1)}, u32[]{:S(2)}, u32[]{:S(2)}) %collective-permute-start.2) | collective-permute-done | bytes 524320 | tf_op jit(solution)/shard_map/ppermute | solution.py:39
  34.5 3.4 %collective-permute-start.4 = (bf16[16,8192]{1,0:T(8,128)(2,1)S(1)}, bf16[16,8192]{1,0:T(8,128)(2,1)S(1)}, u32[]{:S(2)}, u32[]{:S(2)}) collective-permute-start(bf16[16,8192]{1,0:T(8,128)(2,1)S(1)} %slice.121), channel_id=1, source_target_pairs={{0,24},{1,97},{2,26},{3,99},{4,28},{5,101},{6,30},{7,103},{8,0},{9... | collective-permute-start | bytes 786440 | tf_op jit(solution)/shard_map/ppermute | solution.py:39
  38.0 3.4 %collective-permute-done.3 = bf16[16,8192]{1,0:T(8,128)(2,1)S(1)} collective-permute-done((bf16[16,8192]{1,0:T(8,128)(2,1)S(1)}, bf16[16,8192]{1,0:T(8,128)(2,1)S(1)}, u32[]{:S(2)}, u32[]{:S(2)}) %collective-permute-start.3) | collective-permute-done | bytes 262176 | tf_op jit(solution)/shard_map/ppermute | solution.py:39
  41.3 2.8 %collective-permute-done.4 = bf16[16,8192]{1,0:T(8,128)(2,1)S(1)} collective-permute-done((bf16[16,8192]{1,0:T(8,128)(2,1)S(1)}, bf16[16,8192]{1,0:T(8,128)(2,1)S(1)}, u32[]{:S(2)}, u32[]{:S(2)}) %collective-permute-start.4) | collective-permute-done | bytes 262176 | tf_op jit(solution)/shard_map/ppermute | solution.py:39
  44.1 2.2 %collective-permute-start.12 = (bf16[64,8192]{1,0:T(8,128)(2,1)S(1)}, bf16[64,8192]{1,0:T(8,128)(2,1)}, u32[]{:S(2)}, u32[]{:S(2)}) collective-permute-start(bf16[64,8192]{1,0:T(8,128)(2,1)S(1)} %constant_dynamic-update-slice_fusion.refs_1_.refs_9_), channel_id=1, source_target_pairs={{0,96},{1,25},{2,98},{3,27},{4,100},{5,29},{6,102},{7,31},{8,104},... | collective-permute-start | bytes 3145736 | tf_op jit(solution)/shard_map/ppermute | solution.py:39
  49.0 4.4 %ladder.3 = (f32[128,512]{1,0:T(8,128)S(1)}, f32[128,512]{1,0:T(8,128)}, f32[128,512]{1,0:T(8,128)}, f32[128,512]{1,0:T(8,128)}) custom-call(s32[256]{0:T(256)S(1)} %select_n.453.tab, bf16[64,8192]{1,0:T(8,128)(2,1)S(1)} %pad_maximum_fusion.refs_0_.refs_8_, bf16[64,8192]{1,0:T(8,128)(2,1)S(1)} %constant_dynamic-update-slice_fusion.refs_1_.refs_9_, ...), custom_call_target="tpu_custom_call" | custom-call | flops 536870912 | bytes 7340032 | tf_op jit(solution)/shard_map/ladder/pallas_call | solution.py:127
  53.4 2.8 %collective-permute-start.8 = (f32[128,512]{1,0:T(8,128)}, f32[128,512]{1,0:T(8,128)}, u32[]{:S(2)}, u32[]{:S(2)}) collective-permute-start(f32[128,512]{1,0:T(8,128)} %get-tuple-element.19), channel_id=1, source_target_pairs={{0,4},{2,6},{4,0},{6,2},{1,5},{3,7},{5,1},{7,3},{8,12},{10,14},{12... | collective-permute-start | bytes 786440 | tf_op jit(solution)/shard_map/ppermute | solution.py:43
  57.6 2.4 %collective-permute-start.6 = (f32[128,512]{1,0:T(8,128)}, f32[128,512]{1,0:T(8,128)}, u32[]{:S(2)}, u32[]{:S(2)}) collective-permute-start(f32[128,512]{1,0:T(8,128)} %get-tuple-element.17), channel_id=1, source_target_pairs={{0,6},{2,0},{4,2},{6,4},{1,7},{3,1},{5,3},{7,5},{8,14},{10,8},{12,... | collective-permute-start | bytes 786440 | tf_op jit(solution)/shard_map/ppermute | solution.py:43
  66.4 6.3 %ladder.4 = (f32[256,512]{1,0:T(8,128)S(1)}, f32[256,512]{1,0:T(8,128)S(1)}, f32[256,512]{1,0:T(8,128)S(1)}, f32[256,512]{1,0:T(8,128)S(1)}) custom-call(s32[256]{0:T(256)S(1)} %select_n.453.tab, bf16[64,8192]{1,0:T(8,128)(2,1)} %collective-permute-done.9.refs_0_.refs_2_.refs_10_, bf16[64,8192]{1,0:T(8,128)(2,1)S(1)} %copy-done.8, ...), custom_call_target="tpu_custom_call" | custom-call | flops 1073741824 | bytes 10485760 | tf_op jit(solution)/shard_map/ladder/pallas_call | solution.py:127
  72.8 2.8 %collective-permute-start.15 = (f32[256,512]{1,0:T(8,128)S(1)}, f32[256,512]{1,0:T(8,128)S(1)}, u32[]{:S(2)}, u32[]{:S(2)}) collective-permute-start(f32[256,512]{1,0:T(8,128)S(1)} %get-tuple-element.23), channel_id=1, source_target_pairs={{0,4},{2,6},{4,0},{6,2},{1,5},{3,7},{5,1},{7,3},{8,12},{10,14},{12... | collective-permute-start | bytes 1572872 | tf_op jit(solution)/shard_map/ppermute | solution.py:43
  75.9 2.4 %collective-permute-start.13 = (f32[256,512]{1,0:T(8,128)S(1)}, f32[256,512]{1,0:T(8,128)S(1)}, u32[]{:S(2)}, u32[]{:S(2)}) collective-permute-start(f32[256,512]{1,0:T(8,128)S(1)} %get-tuple-element.21), channel_id=1, source_target_pairs={{0,6},{2,0},{4,2},{6,4},{1,7},{3,1},{5,3},{7,5},{8,14},{10,8},{12,... | collective-permute-start | bytes 1572872 | tf_op jit(solution)/shard_map/ppermute | solution.py:43
  80.1 2.8 %collective-permute-done.15 = f32[256,512]{1,0:T(8,128)S(1)} collective-permute-done((f32[256,512]{1,0:T(8,128)S(1)}, f32[256,512]{1,0:T(8,128)S(1)}, u32[]{:S(2)}, u32[]{:S(2)}) %collective-permute-start.15) | collective-permute-done | bytes 524320 | tf_op jit(solution)/shard_map/ppermute | solution.py:43
  82.9 15.4 %collective-permute-done.14 = f32[256,512]{1,0:T(8,128)S(1)} collective-permute-done((f32[256,512]{1,0:T(8,128)S(1)}, f32[256,512]{1,0:T(8,128)S(1)}, u32[]{:S(2)}, u32[]{:S(2)}) %collective-permute-start.14) | collective-permute-done | bytes 524320 | tf_op jit(solution)/shard_map/ppermute | solution.py:43
  98.6 3.7 %ladder.5 = (f32[128,512]{1,0:T(8,128)S(1)}, f32[128,512]{1,0:T(8,128)S(1)}, f32[128,512]{1,0:T(8,128)S(1)}, f32[128,512]{1,0:T(8,128)S(1)}) custom-call(s32[256]{0:T(256)S(1)} %select_n.453.tab, bf16[64,8192]{1,0:T(8,128)(2,1)S(1)} %collective-permute-done.18.refs_0_.refs_6_.refs_14_, bf16[64,8192]{1,0:T(8,128)(2,1)S(1)} %collective-permute-done.19.refs_1_.refs_7_.refs_15_, ...), custom_call_target="tpu_custom_call" | custom-call | flops 536870912 | bytes 7340032 | tf_op jit(solution)/shard_map/ladder/pallas_call | solution.py:127
  102.4 2.2 %collective-permute-start.22 = (f32[128,512]{1,0:T(8,128)S(1)}, f32[128,512]{1,0:T(8,128)S(1)}, u32[]{:S(2)}, u32[]{:S(2)}) collective-permute-start(f32[128,512]{1,0:T(8,128)S(1)} %get-tuple-element.27), channel_id=1, source_target_pairs={{0,4},{2,6},{4,0},{6,2},{1,5},{3,7},{5,1},{7,3},{8,12},{10,14},{12... | collective-permute-start | bytes 786440 | tf_op jit(solution)/shard_map/ppermute | solution.py:43
  109.3 2.7 %collective-permute-done.21 = f32[128,512]{1,0:T(8,128)S(1)} collective-permute-done((f32[128,512]{1,0:T(8,128)S(1)}, f32[128,512]{1,0:T(8,128)S(1)}, u32[]{:S(2)}, u32[]{:S(2)}) %collective-permute-start.21) | collective-permute-done | bytes 262176 | tf_op jit(solution)/shard_map/ppermute | solution.py:43
  112.1 3.9 %collective-permute-start.23 = (f32[128,512]{1,0:T(8,128)S(1)}, f32[128,512]{1,0:T(8,128)S(1)}, u32[]{:S(2)}, u32[]{:S(2)}) collective-permute-start(f32[128,512]{1,0:T(8,128)S(1)} %add_add_fusion), channel_id=1, source_target_pairs={{0,64},{1,17},{2,66},{3,19},{4,68},{5,21},{6,70},{7,23},{8,72},{9,... | collective-permute-start | bytes 786440 | tf_op jit(solution)/shard_map/ppermute | solution.py:39
  116.0 5.5 %hole.1 = (f32[64,4096]{1,0:T(8,128)S(1)}, f32[64,4096]{1,0:T(8,128)}) custom-call(bf16[64,512]{1,0:T(8,128)(2,1)S(1)} %fusion.2.h_ref, bf16[64,8192]{1,0:T(8,128)(2,1)S(1)} %pad_maximum_fusion.refs_0_.refs_8_, bf16[64,8192]{1,0:T(8,128)(2,1)S(1)} %copy-done.4, bf16[64,8192]{1,0:T(8,128)(2,1)} %collective-permute-done.9.refs_0_.refs_2_.refs_10_, ...), custom_call_target="tpu_custom_call" | custom-call | flops 536870912 | bytes 10485760 | tf_op jit(solution)/shard_map/hole/pallas_call | solution.py:159
  121.5 5.4 %collective-permute-start.28 = (f32[64,4096]{1,0:T(8,128)}, f32[64,4096]{1,0:T(8,128)S(1)}, u32[]{:S(2)}, u32[]{:S(2)}) collective-permute-start(f32[64,4096]{1,0:T(8,128)} %get-tuple-element.29), channel_id=1, source_target_pairs={{0,1},{1,0},{2,3},{3,2},{4,5},{5,4},{6,7},{7,6},{8,9},{9,8},{10,11... | collective-permute-start | bytes 3145736 | tf_op jit(solution)/shard_map/ppermute | solution.py:47
  127.0 2.9 %collective-permute-start.25 = (f32[4,32,512]{2,1,0:T(8,128)S(1)}, f32[4,32,512]{2,1,0:T(8,128)S(1)}, u32[]{:S(2)}, u32[]{:S(2)}) collective-permute-start(f32[4,32,512]{2,1,0:T(8,128)S(1)} %pad_maximum_fusion.5), channel_id=1, source_target_pairs={{0,8},{1,33},{2,10},{3,35},{4,12},{5,37},{6,14},{7,39},{8,16},{9,4... | collective-permute-start | bytes 786440 | tf_op jit(solution)/shard_map/ppermute | solution.py:39
  132.5 5.5 %collective-permute-done.26.keep3 = f32[4,32,512]{2,1,0:T(8,128)S(1)} collective-permute-done((f32[4,32,512]{2,1,0:T(8,128)S(1)}, f32[4,32,512]{2,1,0:T(8,128)S(1)}, u32[]{:S(2)}, u32[]{:S(2)}) %collective-permute-start.26) | collective-permute-done | bytes 262176 | tf_op jit(solution)/shard_map/ppermute | solution.py:39
  141.1 2.5 %finish.1 = (f32[64,4096]{1,0:T(8,128)}, bf16[64,4096]{1,0:T(8,128)(2,1)}) custom-call(s32[33]{0:T(128)S(1)} %compare_select_fusion.25.where, f32[4,32,512]{2,1,0:T(8,128)S(1)} %pad_maximum_fusion.3.keep0, f32[4,32,512]{2,1,0:T(8,128)S(1)} %collective-permute-done.24.keep1, f32[4,32,512]{2,1,0:T(8,128)S(1)} %collective-permute-done.25.keep2, ...), custom_call_target="tpu_custom_call" | custom-call | flops 1048576 | bytes 6291456 | tf_op jit(solution)/shard_map/finish/pallas_call | solution.py:190
  (114 shorter events, 36.0 us)
Async XLA Ops:
  6.2 20.5 %collective-permute-start.1 = (bf16[32,8192]{1,0:T(8,128)(2,1)}, bf16[32,8192]{1,0:T(8,128)(2,1)}, u32[]{:S(2)}, u32[]{:S(2)}) collective-permute-start(bf16[32,8192]{1,0:T(8,128)(2,1)} %pad_maximum_fusion.1), channel_id=1, source_target_pairs={{0,8},{1,33},{2,10},{3,35},{4,12},{5,37},{6,14},{7,39},{8,16},{9,4... | collective-permute-start | bytes 1572872 | tf_op jit(solution)/shard_map/ppermute | solution.py:39
  22.9 24.7 %collective-permute-start.5 = (bf16[16,512,128]{2,1,0:T(8,128)(2,1)S(1)}, bf16[16,512,128]{2,1,0:T(8,128)(2,1)S(1)}, u32[]{:S(2)}, u32[]{:S(2)}) collective-permute-start(bf16[16,512,128]{2,1,0:T(8,128)(2,1)S(1)} %select.158.refs_2_.refs_4_), channel_id=1, source_target_pairs={{0,1},{1,0},{2,3},{3,2},{4,5},{5,4},{6,7},{7,6},{8,9},{9,8},{10,11... | collective-permute-start | bytes 6291464 | tf_op jit(solution)/shard_map/ppermute | solution.py:47
  23.0 11.5 %collective-permute-start.2 = (bf16[32,8192]{1,0:T(8,128)(2,1)}, bf16[32,8192]{1,0:T(8,128)(2,1)S(1)}, u32[]{:S(2)}, u32[]{:S(2)}) collective-permute-start(bf16[32,8192]{1,0:T(8,128)(2,1)} %pad_maximum_fusion.1), channel_id=1, source_target_pairs={{0,24},{1,97},{2,26},{3,99},{4,28},{5,101},{6,30},{7,103},{8,0},{9... | collective-permute-start | bytes 1572872 | tf_op jit(solution)/shard_map/ppermute | solution.py:39
  27.8 28.4 %collective-permute-start.9 = (bf16[64,8192]{1,0:T(8,128)(2,1)S(1)}, bf16[64,8192]{1,0:T(8,128)(2,1)}, u32[]{:S(2)}, u32[]{:S(2)}) collective-permute-start(bf16[64,8192]{1,0:T(8,128)(2,1)S(1)} %pad_maximum_fusion.refs_0_.refs_8_), channel_id=1, source_target_pairs={{0,32},{1,9},{2,34},{3,11},{4,36},{5,13},{6,38},{7,15},{8,40},{9,1... | collective-permute-start | bytes 3145736 | tf_op jit(solution)/shard_map/ppermute | solution.py:39
  29.2 27.4 %collective-permute-start.11 = (bf16[64,8192]{1,0:T(8,128)(2,1)S(1)}, bf16[64,8192]{1,0:T(8,128)(2,1)S(1)}, u32[]{:S(2)}, u32[]{:S(2)}) collective-permute-start(bf16[64,8192]{1,0:T(8,128)(2,1)S(1)} %pad_maximum_fusion.refs_0_.refs_8_), channel_id=1, source_target_pairs={{0,96},{1,25},{2,98},{3,27},{4,100},{5,29},{6,102},{7,31},{8,104},... | collective-permute-start | bytes 3145736 | tf_op jit(solution)/shard_map/ppermute | solution.py:39
  31.6 9.8 %collective-permute-start.3 = (bf16[16,8192]{1,0:T(8,128)(2,1)S(1)}, bf16[16,8192]{1,0:T(8,128)(2,1)S(1)}, u32[]{:S(2)}, u32[]{:S(2)}) collective-permute-start(bf16[16,8192]{1,0:T(8,128)(2,1)S(1)} %slice.120), channel_id=1, source_target_pairs={{0,8},{1,33},{2,10},{3,35},{4,12},{5,37},{6,14},{7,39},{8,16},{9,4... | collective-permute-start | bytes 786440 | tf_op jit(solution)/shard_map/ppermute | solution.py:39
  34.5 9.6 %collective-permute-start.4 = (bf16[16,8192]{1,0:T(8,128)(2,1)S(1)}, bf16[16,8192]{1,0:T(8,128)(2,1)S(1)}, u32[]{:S(2)}, u32[]{:S(2)}) collective-permute-start(bf16[16,8192]{1,0:T(8,128)(2,1)S(1)} %slice.121), channel_id=1, source_target_pairs={{0,24},{1,97},{2,26},{3,99},{4,28},{5,101},{6,30},{7,103},{8,0},{9... | collective-permute-start | bytes 786440 | tf_op jit(solution)/shard_map/ppermute | solution.py:39
  44.1 16.0 %collective-permute-start.12 = (bf16[64,8192]{1,0:T(8,128)(2,1)S(1)}, bf16[64,8192]{1,0:T(8,128)(2,1)}, u32[]{:S(2)}, u32[]{:S(2)}) collective-permute-start(bf16[64,8192]{1,0:T(8,128)(2,1)S(1)} %constant_dynamic-update-slice_fusion.refs_1_.refs_9_), channel_id=1, source_target_pairs={{0,96},{1,25},{2,98},{3,27},{4,100},{5,29},{6,102},{7,31},{8,104},... | collective-permute-start | bytes 3145736 | tf_op jit(solution)/shard_map/ppermute | solution.py:39
  46.4 15.2 %collective-permute-start.10 = (bf16[64,8192]{1,0:T(8,128)(2,1)S(1)}, bf16[64,8192]{1,0:T(8,128)(2,1)S(1)}, u32[]{:S(2)}, u32[]{:S(2)}) collective-permute-start(bf16[64,8192]{1,0:T(8,128)(2,1)S(1)} %constant_dynamic-update-slice_fusion.refs_1_.refs_9_), channel_id=1, source_target_pairs={{0,32},{1,9},{2,34},{3,11},{4,36},{5,13},{6,38},{7,15},{8,40},{9,1... | collective-permute-start | bytes 3145736 | tf_op jit(solution)/shard_map/ppermute | solution.py:39
  53.4 19.3 %collective-permute-start.8 = (f32[128,512]{1,0:T(8,128)}, f32[128,512]{1,0:T(8,128)}, u32[]{:S(2)}, u32[]{:S(2)}) collective-permute-start(f32[128,512]{1,0:T(8,128)} %get-tuple-element.19), channel_id=1, source_target_pairs={{0,4},{2,6},{4,0},{6,2},{1,5},{3,7},{5,1},{7,3},{8,12},{10,14},{12... | collective-permute-start | bytes 786440 | tf_op jit(solution)/shard_map/ppermute | solution.py:43
  56.3 19.3 %collective-permute-start.7 = (f32[128,512]{1,0:T(8,128)}, f32[128,512]{1,0:T(8,128)}, u32[]{:S(2)}, u32[]{:S(2)}) collective-permute-start(f32[128,512]{1,0:T(8,128)} %get-tuple-element.18), channel_id=1, source_target_pairs={{0,2},{2,4},{4,6},{6,0},{1,3},{3,5},{5,7},{7,1},{8,10},{10,12},{12... | collective-permute-start | bytes 786440 | tf_op jit(solution)/shard_map/ppermute | solution.py:43
  57.6 18.3 %collective-permute-start.6 = (f32[128,512]{1,0:T(8,128)}, f32[128,512]{1,0:T(8,128)}, u32[]{:S(2)}, u32[]{:S(2)}) collective-permute-start(f32[128,512]{1,0:T(8,128)} %get-tuple-element.17), channel_id=1, source_target_pairs={{0,6},{2,0},{4,2},{6,4},{1,7},{3,1},{5,3},{7,5},{8,14},{10,8},{12,... | collective-permute-start | bytes 786440 | tf_op jit(solution)/shard_map/ppermute | solution.py:43
  60.1 38.4 %collective-permute-start.18 = (bf16[64,8192]{1,0:T(8,128)(2,1)}, bf16[64,8192]{1,0:T(8,128)(2,1)S(1)}, u32[]{:S(2)}, u32[]{:S(2)}) collective-permute-start(bf16[64,8192]{1,0:T(8,128)(2,1)} %collective-permute-done.9.refs_0_.refs_2_.refs_10_), channel_id=1, source_target_pairs={{0,32},{1,9},{2,34},{3,11},{4,36},{5,13},{6,38},{7,15},{8,40},{9,1... | collective-permute-start | bytes 3145736 | tf_op jit(solution)/shard_map/ppermute | solution.py:39
  62.6 36.0 %collective-permute-start.19 = (bf16[64,8192]{1,0:T(8,128)(2,1)}, bf16[64,8192]{1,0:T(8,128)(2,1)S(1)}, u32[]{:S(2)}, u32[]{:S(2)}) collective-permute-start(bf16[64,8192]{1,0:T(8,128)(2,1)} %collective-permute-done.12.refs_3_.refs_5_.refs_13_), channel_id=1, source_target_pairs={{0,96},{1,25},{2,98},{3,27},{4,100},{5,29},{6,102},{7,31},{8,104},... | collective-permute-start | bytes 3145736 | tf_op jit(solution)/shard_map/ppermute | solution.py:39
  72.8 10.1 %collective-permute-start.15 = (f32[256,512]{1,0:T(8,128)S(1)}, f32[256,512]{1,0:T(8,128)S(1)}, u32[]{:S(2)}, u32[]{:S(2)}) collective-permute-start(f32[256,512]{1,0:T(8,128)S(1)} %get-tuple-element.23), channel_id=1, source_target_pairs={{0,4},{2,6},{4,0},{6,2},{1,5},{3,7},{5,1},{7,3},{8,12},{10,14},{12... | collective-permute-start | bytes 1572872 | tf_op jit(solution)/shard_map/ppermute | solution.py:43
  75.6 22.7 %collective-permute-start.14 = (f32[256,512]{1,0:T(8,128)S(1)}, f32[256,512]{1,0:T(8,128)S(1)}, u32[]{:S(2)}, u32[]{:S(2)}) collective-permute-start(f32[256,512]{1,0:T(8,128)S(1)} %get-tuple-element.22), channel_id=1, source_target_pairs={{0,2},{2,4},{4,6},{6,0},{1,3},{3,5},{5,7},{7,1},{8,10},{10,12},{12... | collective-permute-start | bytes 1572872 | tf_op jit(solution)/shard_map/ppermute | solution.py:43
  75.9 22.4 %collective-permute-start.13 = (f32[256,512]{1,0:T(8,128)S(1)}, f32[256,512]{1,0:T(8,128)S(1)}, u32[]{:S(2)}, u32[]{:S(2)}) collective-permute-start(f32[256,512]{1,0:T(8,128)S(1)} %get-tuple-element.21), channel_id=1, source_target_pairs={{0,6},{2,0},{4,2},{6,4},{1,7},{3,1},{5,3},{7,5},{8,14},{10,8},{12,... | collective-permute-start | bytes 1572872 | tf_op jit(solution)/shard_map/ppermute | solution.py:43
  98.5 10.3 %collective-permute-start.17 = (f32[128,512]{1,0:T(8,128)S(1)}, f32[128,512]{1,0:T(8,128)S(1)}, u32[]{:S(2)}, u32[]{:S(2)}) collective-permute-start(f32[128,512]{1,0:T(8,128)S(1)} %get-tuple-element.33), channel_id=1, source_target_pairs={{0,96},{1,25},{2,98},{3,27},{4,100},{5,29},{6,102},{7,31},{8,104},... | collective-permute-start | bytes 786440 | tf_op jit(solution)/shard_map/ppermute | solution.py:39
  104.6 7.4 %collective-permute-start.21 = (f32[128,512]{1,0:T(8,128)S(1)}, f32[128,512]{1,0:T(8,128)S(1)}, u32[]{:S(2)}, u32[]{:S(2)}) collective-permute-start(f32[128,512]{1,0:T(8,128)S(1)} %get-tuple-element.26), channel_id=1, source_target_pairs={{0,2},{2,4},{4,6},{6,0},{1,3},{3,5},{5,7},{7,1},{8,10},{10,12},{12... | collective-permute-start | bytes 786440 | tf_op jit(solution)/shard_map/ppermute | solution.py:43
  107.3 8.7 %collective-permute-start.16 = (f32[128,512]{1,0:T(8,128)S(1)}, f32[128,512]{1,0:T(8,128)S(1)}, u32[]{:S(2)}, u32[]{:S(2)}) collective-permute-start(f32[128,512]{1,0:T(8,128)S(1)} %get-tuple-element.32), channel_id=1, source_target_pairs={{0,32},{1,9},{2,34},{3,11},{4,36},{5,13},{6,38},{7,15},{8,40},{9,1... | collective-permute-start | bytes 786440 | tf_op jit(solution)/shard_map/ppermute | solution.py:39
  112.1 14.8 %collective-permute-start.23 = (f32[128,512]{1,0:T(8,128)S(1)}, f32[128,512]{1,0:T(8,128)S(1)}, u32[]{:S(2)}, u32[]{:S(2)}) collective-permute-start(f32[128,512]{1,0:T(8,128)S(1)} %add_add_fusion), channel_id=1, source_target_pairs={{0,64},{1,17},{2,66},{3,19},{4,68},{5,21},{6,70},{7,23},{8,72},{9,... | collective-permute-start | bytes 786440 | tf_op jit(solution)/shard_map/ppermute | solution.py:39
  121.5 18.1 %collective-permute-start.28 = (f32[64,4096]{1,0:T(8,128)}, f32[64,4096]{1,0:T(8,128)S(1)}, u32[]{:S(2)}, u32[]{:S(2)}) collective-permute-start(f32[64,4096]{1,0:T(8,128)} %get-tuple-element.29), channel_id=1, source_target_pairs={{0,1},{1,0},{2,3},{3,2},{4,5},{5,4},{6,7},{7,6},{8,9},{9,8},{10,11... | collective-permute-start | bytes 3145736 | tf_op jit(solution)/shard_map/ppermute | solution.py:47
  127.0 11.0 %collective-permute-start.25 = (f32[4,32,512]{2,1,0:T(8,128)S(1)}, f32[4,32,512]{2,1,0:T(8,128)S(1)}, u32[]{:S(2)}, u32[]{:S(2)}) collective-permute-start(f32[4,32,512]{2,1,0:T(8,128)S(1)} %pad_maximum_fusion.5), channel_id=1, source_target_pairs={{0,8},{1,33},{2,10},{3,35},{4,12},{5,37},{6,14},{7,39},{8,16},{9,4... | collective-permute-start | bytes 786440 | tf_op jit(solution)/shard_map/ppermute | solution.py:39
  129.8 8.1 %collective-permute-start.26 = (f32[4,32,512]{2,1,0:T(8,128)S(1)}, f32[4,32,512]{2,1,0:T(8,128)S(1)}, u32[]{:S(2)}, u32[]{:S(2)}) collective-permute-start(f32[4,32,512]{2,1,0:T(8,128)S(1)} %pad_maximum_fusion.6), channel_id=1, source_target_pairs={{0,16},{1,65},{2,18},{3,67},{4,20},{5,69},{6,22},{7,71},{8,24},{9,... | collective-permute-start | bytes 786440 | tf_op jit(solution)/shard_map/ppermute | solution.py:39
  (22 other events, 244.8 us)

commit v2 on v1

v2 whole, which is shorter than its diff:
```python
import functools

import jax
import jax.numpy as jnp
from jax import lax
from jax.experimental import pallas as pl
from jax.experimental.pallas import tpu as pltpu
from jax.sharding import Mesh
from jax.sharding import PartitionSpec as P

TW = 128
RING = 4
AXES = ("z", "y", "x", "core")
BF = jnp.bfloat16
F32 = jnp.float32
VMEM_LIMIT = 24 * 1024 * 1024
SCALE = 64.0
F16 = jnp.float16
LIGHT = pl.CostEstimate(flops=1024, bytes_accessed=1024, transcendentals=0)
RELS = (0, -1, 1, 2)


def flat(z, y, x, c):
    return (((z % RING) * RING + y % RING) * RING + x % RING) * 2 + c


def perm_of(first, step):
    pairs = []
    for z in range(RING):
        for y in range(RING):
            for x in range(RING):
                for c in range(2):
                    if (c == 0) == first:
                        to = flat(z, y + step, x, c)
                    else:
                        to = flat(z + step, y, x, c)
                    pairs.append((flat(z, y, x, c), to))
    return pairs


def along(value, first, step):
    return lax.ppermute(value, AXES, perm_of(first, step))


def partner(x, c, first):
    return x ^ 1 if (c == 0) == first else RING - 1 - x


def across_x(value, first):
    pairs = []
    for z in range(RING):
        for y in range(RING):
            for x in range(RING):
                for c in range(2):
                    pairs.append((flat(z, y, x, c), flat(z, y, partner(x, c, first), c)))
    return lax.ppermute(value, AXES, pairs)


def other_core(value):
    return lax.ppermute(value, "core", [(0, 1), (1, 0)])


def select_kernel(tab, ints, out, held, sem, *, first_block):
    rows = 8 * 8 * TW
    copies = [
        pltpu.make_async_copy(ints.at[pl.ds((first_block + b) * rows, rows)], held.at[b], sem.at[b])
        for b in range(2)
    ]
    for cp in copies:
        cp.start()
    row = lax.broadcasted_iota(jnp.int32, (32, 256), 0)
    col = lax.broadcasted_iota(jnp.int32, (32, 256), 1)
    for b in range(2):
        copies[b].wait()
        for ct in range(16):
            pick = jnp.where(col == row * 8 + tab[ct * 16 + 8], 1.0, 0.0).astype(BF)
            tile = tab[ct * 16 + first_block + b] - (first_block + b) * 8
            for g in range(4):
                at = pl.multiple_of(tile * 8 * TW + g * 256, 256)
                got = jnp.dot(
                    pick, held[b, pl.ds(at, 256), ct % 2 * TW:(ct % 2 + 1) * TW], preferred_element_type=F32
                )
                out[ct, b * TW + g * 32:b * TW + (g + 1) * 32, :] = got.astype(BF)


def select(tab, ints2d, first_block):
    return pl.pallas_call(
        functools.partial(select_kernel, first_block=first_block),
        in_specs=[pl.BlockSpec(memory_space=pltpu.SMEM), pl.BlockSpec(memory_space=pltpu.HBM)],
        out_specs=pl.BlockSpec(memory_space=pltpu.VMEM),
        out_shape=jax.ShapeDtypeStruct((16, 2 * TW, TW), BF),
        scratch_shapes=[pltpu.VMEM((2, 8 * 8 * TW, 2 * TW), BF), pltpu.SemaphoreType.DMA((2,))],
        compiler_params=pltpu.CompilerParams(vmem_limit_bytes=50 * 1024 * 1024),
        cost_estimate=LIGHT,
        name="select",
    )(tab, ints2d)


def ladder_kernel(tab, *refs, n):
    a_refs, w_own, w_other, outs = refs[:n], refs[n:n + 2], refs[n + 2:n + 4], refs[n + 4:]
    for ct in range(16):
        d, q = ct // 4, ct % 4
        cols = [
            jnp.concatenate(
                [a[:, pl.ds(pl.multiple_of(tab[ct * 16 + m] * TW, TW), TW)] for a in a_refs], axis=0
            )
            for m in range(8)
        ]
        there = (0, 2, 1, 3)[d] * 4 + (q ^ 2)
        w = jnp.concatenate([w[ct] for w in w_own] + [w[there] for w in w_other], axis=0)
        got = jnp.dot(jnp.concatenate(cols, axis=1), w, preferred_element_type=F32)
        at = d % 2 * 4 + q
        outs[d // 2][:, at * TW:(at + 1) * TW] = got


def ladder(tab, a_list, w_own, w_other):
    rows, n = sum(a.shape[0] for a in a_list), len(a_list)
    vm = pl.BlockSpec(memory_space=pltpu.VMEM)
    return pl.pallas_call(
        functools.partial(ladder_kernel, n=n),
        in_specs=[pl.BlockSpec(memory_space=pltpu.SMEM)] + [vm] * (n + 4),
        out_specs=[vm] * 2,
        out_shape=[jax.ShapeDtypeStruct((rows, 8 * TW), F32)] * 2,
        compiler_params=pltpu.CompilerParams(vmem_limit_bytes=VMEM_LIMIT),
        cost_estimate=LIGHT,
        name="ladder",
    )(tab, *a_list, *w_own, *w_other)


def hole_kernel(h_ref, *refs):
    n = (len(refs) - 2) // 2
    for out, parts in ((refs[-2], refs[:n]), (refs[-1], refs[n:2 * n])):
        a = jnp.concatenate([r[...] for r in parts], axis=0)
        out[...] = jnp.dot(h_ref[...], a, preferred_element_type=F32)


def hole_part(h_rel, a_list, width):
    step = 1024
    steps = width // step
    rows = h_rel.shape[0]
    specs = [pl.BlockSpec((a.shape[0], step), lambda i: (0, i)) for a in a_list]
    specs2 = [pl.BlockSpec((a.shape[0], step), lambda i: (0, i + steps)) for a in a_list]
    return pl.pallas_call(
        hole_kernel,
        grid=(steps,),
        in_specs=[pl.BlockSpec(h_rel.shape, lambda i: (0, 0))] + specs + specs2,
        out_specs=[pl.BlockSpec((rows, step), lambda i: (0, i))] * 2,
        out_shape=[jax.ShapeDtypeStruct((rows, width), F32)] * 2,
        compiler_params=pltpu.CompilerParams(vmem_limit_bytes=VMEM_LIMIT),
        cost_estimate=LIGHT,
        name="hole",
    )(h_rel, *a_list, *a_list)


def finish_kernel(where, *refs):
    keeps, (got, hole_a, hole_b, occ, energy, res, upd) = refs[:RING], refs[RING:]
    core = where[32]
    mine = pl.multiple_of(core * 32, 32)
    his = pl.multiple_of((1 - core) * 32, 32)
    for i in range(16):
        own = keeps[i // 4][i % 4 * 32:(i % 4 + 1) * 32, :256]
        for first, part, at in ((mine, own, i), (his, got[i * 32:(i + 1) * 32], 16 + i)):
            rows = pl.ds(first, 32)
            cols = pl.ds(pl.multiple_of(where[at] * 256, 256), 256)
            total = part + (hole_a[rows, cols] + hole_b[rows, cols])
            res[rows, cols] = total
            upd[rows, cols] = (total / (energy[:, cols] - occ[rows, :])).astype(BF)


def finish(where, keeps, got, hole_a, hole_b, occ, energy):
    shape = hole_a.shape
    vm = pl.BlockSpec(memory_space=pltpu.VMEM)
    return pl.pallas_call(
        finish_kernel,
        in_specs=[pl.BlockSpec(memory_space=pltpu.SMEM)] + [vm] * 9,
        out_specs=[vm, vm],
        out_shape=[jax.ShapeDtypeStruct(shape, F32), jax.ShapeDtypeStruct(shape, BF)],
        compiler_params=pltpu.CompilerParams(vmem_limit_bytes=VMEM_LIMIT),
        cost_estimate=LIGHT,
        name="finish",
    )(where, *keeps, got, hole_a, hole_b, occ, energy)


def local(amplitudes, ladder_ints, hole_ints, tile_irrep, pair_orbitals, occ_energy, pair_energy):
    z, y, x, c = (lax.axis_index(name) for name in AXES)
    rows, width = amplitudes.shape
    half = rows // 2
    p = z * RING + y

    mine = lax.dynamic_slice_in_dim(amplitudes, c * half, half, 0)
    theirs = other_core(lax.dynamic_slice_in_dim(amplitudes, (1 - c) * half, half, 0))
    own = jnp.concatenate([mine, theirs], axis=1)

    i = jnp.arange(16, dtype=jnp.int32)
    low, high = x ^ 1, RING - 1 - x
    first, second = jnp.where(c == 0, low, high), jnp.where(c == 0, high, low)
    goes = jnp.where(i < 4, x, jnp.where(i < 8, second, jnp.where(i < 12, first, (x + 2) % RING)))
    o = 2 * goes + (c + i // 2 % 2) % 2
    tile = o * 32 + 2 * p + i % 2
    t = jnp.arange(tile_irrep.shape[0], dtype=jnp.int32)
    label = jnp.sum(jnp.where(tile[:, None] == t[None, :], tile_irrep[None, :], 0), axis=1)
    m = jnp.arange(16, dtype=jnp.int32)
    v_of = 2 * x + (c + m // 4) % 2
    block = v_of * 4 + m % 4
    hit = (t[None, None, :] // 8 == block[None, :, None]) & (tile_irrep[None, None, :] == label[:, None, None])
    inside = jnp.sum(jnp.where(hit, t[None, None, :] % 8, 0), axis=2)
    offs = (m // 4 * 32 + m % 4 * 8)[None, :] + inside
    tab = jnp.where(m[None, :] < 8, offs, o[:, None]).reshape(256)

    hold = lax.optimization_barrier
    ints2d = ladder_ints.reshape(-1, ladder_ints.shape[2])

    quarter = half // 2
    r_m = along(own, True, 1)
    r_p = along(own, True, -1)
    w_a = select(hold((tab, own))[0], ints2d, 0)
    r_m, r_p, w_a, tab = hold((r_m, r_p, w_a, tab))
    s_a = jnp.concatenate([own, r_m, r_p[:quarter]], axis=0)
    q_ma = along(s_a, False, 1)
    q_pa = along(s_a, False, -1)
    r_2a = along(r_m[:quarter], True, 1)
    r_2b = along(r_p[quarter:], True, -1)
    w_b = select(tab, ints2d, 2)
    r_2a, r_2b, w_b = hold((r_2a, r_2b, w_b))
    s_b = jnp.concatenate([r_p[quarter:], r_2a, r_2b], axis=0)
    q_mb = along(s_b, False, 1)
    q_pb = along(s_b, False, -1)
    w_own = [w_a, w_b]
    w_other = [other_core(w) for w in w_own]

    i = jnp.arange(33, dtype=jnp.int32)
    kf = sum(jnp.where(i // 4 % 4 == k, jnp.int32(-RELS[k] % RING), 0) for k in range(RING))
    ks = sum(jnp.where(i % 4 == k, jnp.int32(RELS[k] % RING), 0) for k in range(RING))
    flip = (c + i // 16) % 2 == 0
    kz, ky = jnp.where(flip, ks, kf), jnp.where(flip, kf, ks)
    where = jnp.where(i == 32, c, (z + kz) % RING * RING + (y + ky) % RING)
    orbital = jnp.arange(occ_energy.shape[0], dtype=jnp.int32)
    picked = (pair_orbitals[:, :, None] == orbital[None, None, :]).astype(F32)
    occ = jnp.sum(picked * occ_energy[None, None, :], axis=(1, 2))[:, None]

    j = jnp.arange(16 * half, dtype=jnp.int32)
    ds = sum(jnp.where(j // (4 * half) == k, jnp.int32(RELS[k] % RING), 0) for k in range(RING))
    df = sum(jnp.where(j // half % 4 == k, jnp.int32(RELS[k] % RING), 0) for k in range(RING))
    dz, dy = jnp.where(c == 0, ds, df), jnp.where(c == 0, df, ds)
    source = ((z + dz) % RING * RING + (y + dy) % RING) * rows + c * half + j % half
    onehot = (jnp.arange(hole_ints.shape[1], dtype=jnp.int32)[:, None] == source[None, :]).astype(BF)
    h_rel = jnp.dot(hole_ints, onehot, preferred_element_type=F32).astype(BF)

    q_ma, q_pa, w_other, where, occ, h_rel = hold((q_ma, q_pa, w_other, where, occ, h_rel))
    q_2a = along(q_ma, False, 1)
    q_2b = along(q_pb, False, -1)
    a_list = [s_a, s_b, q_ma, q_mb, q_pa, q_pb, q_2a, q_2b]

    mid = 4 * TW
    block = RING * half

    def coded(value):
        return (value * SCALE).astype(F16)

    def decoded(value):
        return value.astype(F32) * (1.0 / SCALE)

    keep_0, send_0 = ladder(tab, a_list[:2], w_own, w_other)
    q_mb, q_pb, keep_0, send_0 = hold((q_mb, q_pb, keep_0, send_0))
    keep_1, send_1 = ladder(tab, [q_ma, q_mb, q_pa, q_pb], w_own, w_other)
    near_got = across_x(jnp.concatenate([coded(send_0), coded(send_1)], axis=0), True)
    keep_2, send_2 = ladder(tab, a_list[6:], w_own, w_other)
    far_send = coded(send_2)
    far_got = across_x(far_send, True)
    near_got, _ = hold((near_got, far_send))
    sum_0 = keep_0 + decoded(near_got[:block])
    sum_1 = keep_1 + decoded(near_got[block:])
    near_end = across_x(jnp.concatenate([coded(sum_0[:, mid:]), coded(sum_1[:, mid:])], axis=0), False)
    sum_2 = keep_2 + decoded(far_got)
    far_end = across_x(coded(sum_2[:, mid:]), False)
    near_end, h_rel = hold((near_end, h_rel))
    t_0 = sum_0[:, :mid] + decoded(near_end[:block])
    t_m = sum_1[:block, :mid] + decoded(near_end[block:2 * block])
    t_p = sum_1[block:, :mid] + decoded(near_end[2 * block:])
    t_2 = sum_2[:, :mid] + decoded(far_end)

    from_p = along(t_m, False, -1)
    from_m = along(t_p, False, 1)
    from_2 = along(t_2, False, 2)
    hole_own, hole_send = hole_part(h_rel, a_list, width)
    from_p, from_m, from_2, hole_send = hold((from_p, from_m, from_2, hole_send))
    hole_got = other_core(hole_send)
    back = [t_0, from_m, from_p, from_2]
    keeps = []
    for k in range(RING):
        u = jnp.concatenate([part[k * half:(k + 1) * half] for part in back], axis=0)
        keeps.append(u if k == 0 else along(u, True, RELS[k]))
    got = other_core(jnp.concatenate([u[:, mid // 2:] for u in keeps], axis=0))
    return finish(where, keeps, got, hole_own, hole_got, occ, pair_energy[None, :])


def solution(mesh):
    grid = Mesh(mesh.devices.reshape(RING, RING, RING, 2), AXES)
    pair, virt = ("z", "y"), ("x", "core")
    placed = (
        P(pair, virt),
        P(virt, None, pair),
        P(pair, None),
        P(),
        P(pair, None),
        P(),
        P(virt),
    )
    return jax.shard_map(
        local,
        mesh=grid,
        in_specs=placed,
        out_specs=(P(pair, virt), P(pair, virt)),
        check_vma=False,
    )
```

time: 145 us -> 106 us (0.73); the launches traced: 144 us -> 106 us
  starting transfers between devices: 52 us -> 36.7 us
  Pallas kernels: 37.2 us -> 22.5 us
  local copies, waits for them, and re-layouts: 8.31 us -> 1.47 us
  other arithmetic: 6.92 us -> 4.58 us
  waiting for transfers between devices: 37.6 us -> 39.4 us
    ppermute x16, waiting for transfers between devices: 14.7 us -> 29.1 us  [along(): return lax.ppermute(value, AXES, perm_of(first, step))]
    ppermute x9 -> x4, waiting for transfers between devices: 21.4 us -> 8.54 us  [across_x(): return lax.ppermute(value, AXES, pairs)]
    pallas_call x4 -> x5, Pallas kernels: 29.2 us -> 16.5 us  [the longest x2 9.44 us: select(): pl.pallas_call(functools.partial(select_kernel, first_block=first_block),...]
    ppermute x9 -> x4, starting transfers between devices: 15.9 us -> 5.85 us  [across_x(): return lax.ppermute(value, AXES, pairs)]
    ppermute x16, starting transfers between devices: 28.8 us -> 21.7 us  [along(): return lax.ppermute(value, AXES, perm_of(first, step))]
    unnamed x36 -> x8, local copies, waits for them, and re-layouts: 5.91 us -> 0.03 us
    pallas_call x1, Pallas kernels: 5.5 us -> 3.53 us  [hole_part(): pl.pallas_call(hole_kernel, grid=(steps,), in_specs=[pl.BlockSpec(h_rel.s...]
    ppermute x4 -> x5, starting transfers between devices: 7.35 us -> 9.08 us  [other_core(): return lax.ppermute(value, 'core', [(0, 1), (1, 0)])]
  transfers between devices with their start and end apart: 29 -> 25, of which waited for: 10 -> 13; matrix products, arithmetic and copies ran while one was open for 5% -> 5% of each run, Pallas kernels for 24% -> 19%
where the time goes in v2:
time: 106 us
  waiting for transfers between devices  39.4 us (37%)
  starting transfers between devices  36.7 us (35%)
  Pallas kernels  22.5 us (21%)
  other arithmetic  4.58 us (4%)
  local copies, waits for them, and re-layouts  1.47 us (1%)
    ppermute x16, waiting for transfers between devices, along(): return lax.ppermute(value, AXES, perm_of(first, step))  29.1 us
    ppermute x16, starting transfers between devices, along(): return lax.ppermute(value, AXES, perm_of(first, step))  21.7 us
    pallas_call x2, Pallas kernels, select(): pl.pallas_call(functools.partial(select_kernel, first_block=first_block),...  9.44 us
    ppermute x5, starting transfers between devices, other_core(): return lax.ppermute(value, 'core', [(0, 1), (1, 0)])  9.08 us
    ppermute x4, waiting for transfers between devices, across_x(): return lax.ppermute(value, AXES, pairs)  8.54 us
    pallas_call x3, Pallas kernels, ladder(): pl.pallas_call(functools.partial(ladder_kernel, n=n), in_specs=[pl.BlockS...  7.06 us
    ppermute x4, starting transfers between devices, across_x(): return lax.ppermute(value, AXES, pairs)  5.85 us
    pallas_call x1, Pallas kernels, hole_part(): pl.pallas_call(hole_kernel, grid=(steps,), in_specs=[pl.BlockSpec(h_rel.s...  3.53 us
  transfers between devices with their start and end apart: 25, of which 13 were waited for; matrix products, arithmetic and copies ran while one was open for 5% of the time, Pallas kernels for 19%

profile of v2, /device:TPU:1, one launch (start us, length us, event | category | flops | bytes accessed | tf_op | source)
XLA Modules:
  0.0 106.1 jit_solution(8980999255649122424)
XLA Ops:
  5.0 1.8 %collective-permute-start.1 = (bf16[32,8192]{1,0:T(8,128)(2,1)S(1)}, bf16[32,8192]{1,0:T(8,128)(2,1)S(1)}, u32[]{:S(2)}, u32[]{:S(2)}) collective-permute-start(bf16[32,8192]{1,0:T(8,128)(2,1)S(1)} %pad_maximum_fusion.3), channel_id=1, source_target_pairs={{0,8},{1,33},{2,10},{3,35},{4,12},{5,37},{6,14},{7,39},{8,16},{9,4... | collective-permute-start | bytes 1572872 | tf_op jit(solution)/shard_map/ppermute | solution.py:42
  6.8 2.2 %collective-permute-start.2 = (bf16[32,8192]{1,0:T(8,128)(2,1)S(1)}, bf16[32,8192]{1,0:T(8,128)(2,1)S(1)}, u32[]{:S(2)}, u32[]{:S(2)}) collective-permute-start(bf16[32,8192]{1,0:T(8,128)(2,1)S(1)} %pad_maximum_fusion.3), channel_id=1, source_target_pairs={{0,24},{1,97},{2,26},{3,99},{4,28},{5,101},{6,30},{7,103},{8,0},{9... | collective-permute-start | bytes 1572872 | tf_op jit(solution)/shard_map/ppermute | solution.py:42
  9.6 4.7 %select.141.refs_2_.refs_4_ = bf16[16,256,128]{2,1,0:T(8,128)(2,1)S(1)} custom-call(s32[256]{0:T(256)S(1)} %select_n.429.tab, bf16[32768,256]{1,0:T(8,128)(2,1)} %bitcast.7), custom_call_target="tpu_custom_call" | custom-call | flops 1024 | bytes 1024 | tf_op jit(solution)/shard_map/select/pallas_call | solution.py:87
  17.8 2.2 %collective-permute-start.7 = (bf16[16,8192]{1,0:T(8,128)(2,1)S(1)}, bf16[16,8192]{1,0:T(8,128)(2,1)S(1)}, u32[]{:S(2)}, u32[]{:S(2)}) collective-permute-start(bf16[16,8192]{1,0:T(8,128)(2,1)S(1)} %get-tuple-element.74), channel_id=1, source_target_pairs={{0,24},{1,97},{2,26},{3,99},{4,28},{5,101},{6,30},{7,103},{8,0},{9... | collective-permute-start | bytes 786440 | tf_op jit(solution)/shard_map/ppermute | solution.py:42
  22.8 4.7 %select.142.refs_3_.refs_5_ = bf16[16,256,128]{2,1,0:T(8,128)(2,1)S(1)} custom-call(s32[256]{0:T(256)S(1)} %select_n.429.tab, bf16[32768,256]{1,0:T(8,128)(2,1)} %bitcast.8), custom_call_target="tpu_custom_call" | custom-call | flops 1024 | bytes 1024 | tf_op jit(solution)/shard_map/select/pallas_call | solution.py:87
  30.9 7.3 %collective-permute-done.3.refs_0_.refs_2_.refs_10_ = bf16[80,8192]{1,0:T(8,128)(2,1)S(1)} collective-permute-done((bf16[80,8192]{1,0:T(8,128)(2,1)S(1)}, bf16[80,8192]{1,0:T(8,128)(2,1)S(1)}, u32[]{:S(2)}, u32[]{:S(2)}) %collective-permute-start.3) | collective-permute-done | bytes 1310752 | tf_op jit(solution)/shard_map/ppermute | solution.py:42
  39.2 7.4 %collective-permute-done.10.refs_3_.refs_5_.refs_13_ = bf16[48,8192]{1,0:T(8,128)(2,1)S(1)} collective-permute-done((bf16[48,8192]{1,0:T(8,128)(2,1)S(1)}, bf16[48,8192]{1,0:T(8,128)(2,1)S(1)}, u32[]{:S(2)}, u32[]{:S(2)}) %collective-permute-start.10) | collective-permute-done | bytes 786464 | tf_op jit(solution)/shard_map/ppermute | solution.py:42
  46.6 2.6 %collective-permute-start.13 = (bf16[48,8192]{1,0:T(8,128)(2,1)S(1)}, bf16[48,8192]{1,0:T(8,128)(2,1)S(1)}, u32[]{:S(2)}, u32[]{:S(2)}) collective-permute-start(bf16[48,8192]{1,0:T(8,128)(2,1)S(1)} %collective-permute-done.10.refs_3_.refs_5_.refs_13_), channel_id=1, source_target_pairs={{0,96},{1,25},{2,98},{3,27},{4,100},{5,29},{6,102},{7,31},{8,104},... | collective-permute-start | bytes 2359304 | tf_op jit(solution)/shard_map/ppermute | solution.py:42
  49.2 2.0 %ladder.3 = (f32[128,1024]{1,0:T(8,128)S(1)}, f32[128,1024]{1,0:T(8,128)S(1)}) custom-call(s32[256]{0:T(256)S(1)} %select_n.429.tab, bf16[80,8192]{1,0:T(8,128)(2,1)S(1)} %pad_maximum_fusion.refs_0_.refs_8_, bf16[48,8192]{1,0:T(8,128)(2,1)S(1)} %pad_maximum_fusion.1.refs_1_.refs_9_, bf16[16,256,128]{2,1,0:T(8,128)(2,1)S(1)} %select.141.refs_2_.refs_4_, ...), custom_call_target="tpu_custom_call" | custom-call | flops 1024 | bytes 1024 | tf_op jit(solution)/shard_map/ladder/pallas_call | solution.py:119
  51.2 3.1 %ladder.4 = (f32[256,1024]{1,0:T(8,128)S(1)}, f32[256,1024]{1,0:T(8,128)S(1)}) custom-call(s32[256]{0:T(256)S(1)} %select_n.429.tab, bf16[80,8192]{1,0:T(8,128)(2,1)S(1)} %collective-permute-done.3.refs_0_.refs_2_.refs_10_, bf16[48,8192]{1,0:T(8,128)(2,1)S(1)} %collective-permute-done.9.refs_1_.refs_3_.refs_11_, ...), custom_call_target="tpu_custom_call" | custom-call | flops 1024 | bytes 1024 | tf_op jit(solution)/shard_map/ladder/pallas_call | solution.py:119
  54.7 2.5 %collective-permute-start.11 = (f16[384,1024]{1,0:T(8,128)(2,1)S(1)}, f16[384,1024]{1,0:T(8,128)(2,1)S(1)}, u32[]{:S(2)}, u32[]{:S(2)}) collective-permute-start(f16[384,1024]{1,0:T(8,128)(2,1)S(1)} %pad_maximum_fusion.2), channel_id=1, source_target_pairs={{0,2},{1,7},{2,0},{3,5},{4,6},{5,3},{6,4},{7,1},{8,10},{9,15},{10,... | collective-permute-start | bytes 2359304 | tf_op jit(solution)/shard_map/ppermute | solution.py:56
  58.2 2.4 %collective-permute-done.12.refs_0_.refs_6_.refs_14_ = bf16[80,8192]{1,0:T(8,128)(2,1)S(1)} collective-permute-done((bf16[80,8192]{1,0:T(8,128)(2,1)S(1)}, bf16[80,8192]{1,0:T(8,128)(2,1)S(1)}, u32[]{:S(2)}, u32[]{:S(2)}) %collective-permute-start.12) | collective-permute-done | bytes 1310752 | tf_op jit(solution)/shard_map/ppermute | solution.py:42
  60.6 2.0 %ladder.5 = (f32[128,1024]{1,0:T(8,128)S(1)}, f32[128,1024]{1,0:T(8,128)S(1)}) custom-call(s32[256]{0:T(256)S(1)} %select_n.429.tab, bf16[80,8192]{1,0:T(8,128)(2,1)S(1)} %collective-permute-done.12.refs_0_.refs_6_.refs_14_, bf16[48,8192]{1,0:T(8,128)(2,1)S(1)} %collective-permute-done.13.refs_1_.refs_7_.refs_15_, ...), custom_call_target="tpu_custom_call" | custom-call | flops 1024 | bytes 1024 | tf_op jit(solution)/shard_map/ladder/pallas_call | solution.py:119
  62.7 2.6 %collective-permute-start.17 = (f16[128,1024]{1,0:T(8,128)(2,1)S(1)}, f16[128,1024]{1,0:T(8,128)(2,1)S(1)}, u32[]{:S(2)}, u32[]{:S(2)}) collective-permute-start(f16[128,1024]{1,0:T(8,128)(2,1)S(1)} %multiply_convert_fusion.1), channel_id=1, source_target_pairs={{0,2},{1,7},{2,0},{3,5},{4,6},{5,3},{6,4},{7,1},{8,10},{9,15},{10,... | collective-permute-start | bytes 786440 | tf_op jit(solution)/shard_map/ppermute | solution.py:56
  67.7 1.9 %collective-permute-done.17 = f16[128,1024]{1,0:T(8,128)(2,1)S(1)} collective-permute-done((f16[128,1024]{1,0:T(8,128)(2,1)S(1)}, f16[128,1024]{1,0:T(8,128)(2,1)S(1)}, u32[]{:S(2)}, u32[]{:S(2)}) %collective-permute-start.17) | collective-permute-done | bytes 262176 | tf_op jit(solution)/shard_map/ppermute | solution.py:56
  70.1 5.0 %collective-permute-done.14 = f16[384,512]{1,0:T(8,128)(2,1)S(1)} collective-permute-done((f16[384,512]{1,0:T(8,128)(2,1)S(1)}, f16[384,512]{1,0:T(8,128)(2,1)S(1)}, u32[]{:S(2)}, u32[]{:S(2)}) %collective-permute-start.14) | collective-permute-done | bytes 393248 | tf_op jit(solution)/shard_map/ppermute | solution.py:56
  78.5 3.5 %hole.1 = (f32[64,4096]{1,0:T(8,128)S(1)}, f32[64,4096]{1,0:T(8,128)}) custom-call(bf16[64,512]{1,0:T(8,128)(2,1)S(1)} %fusion.2.h_ref, bf16[80,8192]{1,0:T(8,128)(2,1)S(1)} %pad_maximum_fusion.refs_0_.refs_8_, bf16[48,8192]{1,0:T(8,128)(2,1)S(1)} %pad_maximum_fusion.1.refs_1_.refs_9_, bf16[80,8192]{1,0:T(8,128)(2,1)S(1)} %collective-permute-done.3.refs_0_.refs_2_.refs_10_, ...), custom_call_target="tpu_custom_call" | custom-call | flops 1024 | bytes 1024 | tf_op jit(solution)/shard_map/hole/pallas_call | solution.py:143
  82.0 4.4 %collective-permute-done.16 = f32[128,512]{1,0:T(8,128)S(1)} collective-permute-done((f32[128,512]{1,0:T(8,128)S(1)}, f32[128,512]{1,0:T(8,128)S(1)}, u32[]{:S(2)}, u32[]{:S(2)}) %collective-permute-start.16) | collective-permute-done | bytes 262176 | tf_op jit(solution)/shard_map/ppermute | solution.py:42
  86.6 3.7 %collective-permute-start.24 = (f32[64,4096]{1,0:T(8,128)}, f32[64,4096]{1,0:T(8,128)S(1)}, u32[]{:S(2)}, u32[]{:S(2)}) collective-permute-start(f32[64,4096]{1,0:T(8,128)} %get-tuple-element.68), channel_id=1, source_target_pairs={{0,1},{1,0},{2,3},{3,2},{4,5},{5,4},{6,7},{7,6},{8,9},{9,8},{10,11... | collective-permute-start | bytes 3145736 | tf_op jit(solution)/shard_map/ppermute | solution.py:60
  90.3 2.7 %collective-permute-start.22 = (f32[128,512]{1,0:T(8,128)S(1)}, f32[128,512]{1,0:T(8,128)S(1)}, u32[]{:S(2)}, u32[]{:S(2)}) collective-permute-start(f32[128,512]{1,0:T(8,128)S(1)} %pad_maximum_fusion.9), channel_id=1, source_target_pairs={{0,16},{1,65},{2,18},{3,67},{4,20},{5,69},{6,22},{7,71},{8,24},{9,... | collective-permute-start | bytes 786440 | tf_op jit(solution)/shard_map/ppermute | solution.py:42
  93.1 4.3 %collective-permute-done.22.refs_3_ = f32[128,512]{1,0:T(8,128)S(1)} collective-permute-done((f32[128,512]{1,0:T(8,128)S(1)}, f32[128,512]{1,0:T(8,128)S(1)}, u32[]{:S(2)}, u32[]{:S(2)}) %collective-permute-start.22) | collective-permute-done | bytes 262176 | tf_op jit(solution)/shard_map/ppermute | solution.py:42
  99.4 2.4 %collective-permute-start.23 = (f32[512,256]{1,0:T(8,128)}, f32[512,256]{1,0:T(8,128)}, u32[]{:S(2)}, u32[]{:S(2)}) collective-permute-start(f32[512,256]{1,0:T(8,128)} %pad_maximum_fusion.4), channel_id=1, source_target_pairs={{0,1},{1,0},{2,3},{3,2},{4,5},{5,4},{6,7},{7,6},{8,9},{9,8},{10,11... | collective-permute-start | bytes 1572872 | tf_op jit(solution)/shard_map/ppermute | solution.py:60
  101.9 1.8 %collective-permute-done.23.refs_4_ = f32[512,256]{1,0:T(8,128)} collective-permute-done((f32[512,256]{1,0:T(8,128)}, f32[512,256]{1,0:T(8,128)}, u32[]{:S(2)}, u32[]{:S(2)}) %collective-permute-start.23) | collective-permute-done | bytes 524320 | tf_op jit(solution)/shard_map/ppermute | solution.py:60
  103.7 2.5 %finish.1 = (f32[64,4096]{1,0:T(8,128)}, bf16[64,4096]{1,0:T(8,128)(2,1)}) custom-call(s32[33]{0:T(128)S(1)} %compare_select_fusion.20.where, f32[128,512]{1,0:T(8,128)S(1)} %pad_maximum_fusion.6.refs_0_, f32[128,512]{1,0:T(8,128)S(1)} %collective-permute-done.20.refs_1_, f32[128,512]{1,0:T(8,128)S(1)} %collective-permute-done.21.refs_2_, ...), custom_call_target="tpu_custom_call" | custom-call | flops 1024 | bytes 1024 | tf_op jit(solution)/shard_map/finish/pallas_call | solution.py:173
  (89 shorter events, 25.5 us)
Async XLA Ops:
  5.0 10.5 %collective-permute-start.1 = (bf16[32,8192]{1,0:T(8,128)(2,1)S(1)}, bf16[32,8192]{1,0:T(8,128)(2,1)S(1)}, u32[]{:S(2)}, u32[]{:S(2)}) collective-permute-start(bf16[32,8192]{1,0:T(8,128)(2,1)S(1)} %pad_maximum_fusion.3), channel_id=1, source_target_pairs={{0,8},{1,33},{2,10},{3,35},{4,12},{5,37},{6,14},{7,39},{8,16},{9,4... | collective-permute-start | bytes 1572872 | tf_op jit(solution)/shard_map/ppermute | solution.py:42
  6.8 8.7 %collective-permute-start.2 = (bf16[32,8192]{1,0:T(8,128)(2,1)S(1)}, bf16[32,8192]{1,0:T(8,128)(2,1)S(1)}, u32[]{:S(2)}, u32[]{:S(2)}) collective-permute-start(bf16[32,8192]{1,0:T(8,128)(2,1)S(1)} %pad_maximum_fusion.3), channel_id=1, source_target_pairs={{0,24},{1,97},{2,26},{3,99},{4,28},{5,101},{6,30},{7,103},{8,0},{9... | collective-permute-start | bytes 1572872 | tf_op jit(solution)/shard_map/ppermute | solution.py:42
  15.5 14.6 %collective-permute-start.5 = (bf16[16,256,128]{2,1,0:T(8,128)(2,1)S(1)}, bf16[16,256,128]{2,1,0:T(8,128)(2,1)S(1)}, u32[]{:S(2)}, u32[]{:S(2)}) collective-permute-start(bf16[16,256,128]{2,1,0:T(8,128)(2,1)S(1)} %select.141.refs_2_.refs_4_), channel_id=1, source_target_pairs={{0,1},{1,0},{2,3},{3,2},{4,5},{5,4},{6,7},{7,6},{8,9},{9,8},{10,11... | collective-permute-start | bytes 3145736 | tf_op jit(solution)/shard_map/ppermute | solution.py:60
  16.1 11.5 %collective-permute-start.6 = (bf16[16,8192]{1,0:T(8,128)(2,1)S(1)}, bf16[16,8192]{1,0:T(8,128)(2,1)S(1)}, u32[]{:S(2)}, u32[]{:S(2)}) collective-permute-start(bf16[16,8192]{1,0:T(8,128)(2,1)S(1)} %slice.107), channel_id=1, source_target_pairs={{0,8},{1,33},{2,10},{3,35},{4,12},{5,37},{6,14},{7,39},{8,16},{9,4... | collective-permute-start | bytes 786440 | tf_op jit(solution)/shard_map/ppermute | solution.py:42
  17.8 9.8 %collective-permute-start.7 = (bf16[16,8192]{1,0:T(8,128)(2,1)S(1)}, bf16[16,8192]{1,0:T(8,128)(2,1)S(1)}, u32[]{:S(2)}, u32[]{:S(2)}) collective-permute-start(bf16[16,8192]{1,0:T(8,128)(2,1)S(1)} %get-tuple-element.74), channel_id=1, source_target_pairs={{0,24},{1,97},{2,26},{3,99},{4,28},{5,101},{6,30},{7,103},{8,0},{9... | collective-permute-start | bytes 786440 | tf_op jit(solution)/shard_map/ppermute | solution.py:42
  20.1 18.0 %collective-permute-start.3 = (bf16[80,8192]{1,0:T(8,128)(2,1)S(1)}, bf16[80,8192]{1,0:T(8,128)(2,1)S(1)}, u32[]{:S(2)}, u32[]{:S(2)}) collective-permute-start(bf16[80,8192]{1,0:T(8,128)(2,1)S(1)} %pad_maximum_fusion.refs_0_.refs_8_), channel_id=1, source_target_pairs={{0,32},{1,9},{2,34},{3,11},{4,36},{5,13},{6,38},{7,15},{8,40},{9,1... | collective-permute-start | bytes 3932168 | tf_op jit(solution)/shard_map/ppermute | solution.py:42
  21.5 16.8 %collective-permute-start.4 = (bf16[80,8192]{1,0:T(8,128)(2,1)S(1)}, bf16[80,8192]{1,0:T(8,128)(2,1)S(1)}, u32[]{:S(2)}, u32[]{:S(2)}) collective-permute-start(bf16[80,8192]{1,0:T(8,128)(2,1)S(1)} %pad_maximum_fusion.refs_0_.refs_8_), channel_id=1, source_target_pairs={{0,96},{1,25},{2,98},{3,27},{4,100},{5,29},{6,102},{7,31},{8,104},... | collective-permute-start | bytes 3932168 | tf_op jit(solution)/shard_map/ppermute | solution.py:42
  27.6 10.6 %collective-permute-start.8 = (bf16[16,256,128]{2,1,0:T(8,128)(2,1)S(1)}, bf16[16,256,128]{2,1,0:T(8,128)(2,1)S(1)}, u32[]{:S(2)}, u32[]{:S(2)}) collective-permute-start(bf16[16,256,128]{2,1,0:T(8,128)(2,1)S(1)} %select.142.refs_3_.refs_5_), channel_id=1, source_target_pairs={{0,1},{1,0},{2,3},{3,2},{4,5},{5,4},{6,7},{7,6},{8,9},{9,8},{10,11... | collective-permute-start | bytes 3145736 | tf_op jit(solution)/shard_map/ppermute | solution.py:60
  28.6 18.0 %collective-permute-start.10 = (bf16[48,8192]{1,0:T(8,128)(2,1)S(1)}, bf16[48,8192]{1,0:T(8,128)(2,1)S(1)}, u32[]{:S(2)}, u32[]{:S(2)}) collective-permute-start(bf16[48,8192]{1,0:T(8,128)(2,1)S(1)} %pad_maximum_fusion.1.refs_1_.refs_9_), channel_id=1, source_target_pairs={{0,96},{1,25},{2,98},{3,27},{4,100},{5,29},{6,102},{7,31},{8,104},... | collective-permute-start | bytes 2359304 | tf_op jit(solution)/shard_map/ppermute | solution.py:42
  30.1 21.2 %collective-permute-start.9 = (bf16[48,8192]{1,0:T(8,128)(2,1)S(1)}, bf16[48,8192]{1,0:T(8,128)(2,1)S(1)}, u32[]{:S(2)}, u32[]{:S(2)}) collective-permute-start(bf16[48,8192]{1,0:T(8,128)(2,1)S(1)} %pad_maximum_fusion.1.refs_1_.refs_9_), channel_id=1, source_target_pairs={{0,32},{1,9},{2,34},{3,11},{4,36},{5,13},{6,38},{7,15},{8,40},{9,1... | collective-permute-start | bytes 2359304 | tf_op jit(solution)/shard_map/ppermute | solution.py:42
  38.2 22.4 %collective-permute-start.12 = (bf16[80,8192]{1,0:T(8,128)(2,1)S(1)}, bf16[80,8192]{1,0:T(8,128)(2,1)S(1)}, u32[]{:S(2)}, u32[]{:S(2)}) collective-permute-start(bf16[80,8192]{1,0:T(8,128)(2,1)S(1)} %collective-permute-done.3.refs_0_.refs_2_.refs_10_), channel_id=1, source_target_pairs={{0,32},{1,9},{2,34},{3,11},{4,36},{5,13},{6,38},{7,15},{8,40},{9,1... | collective-permute-start | bytes 3932168 | tf_op jit(solution)/shard_map/ppermute | solution.py:42
  46.6 11.5 %collective-permute-start.13 = (bf16[48,8192]{1,0:T(8,128)(2,1)S(1)}, bf16[48,8192]{1,0:T(8,128)(2,1)S(1)}, u32[]{:S(2)}, u32[]{:S(2)}) collective-permute-start(bf16[48,8192]{1,0:T(8,128)(2,1)S(1)} %collective-permute-done.10.refs_3_.refs_5_.refs_13_), channel_id=1, source_target_pairs={{0,96},{1,25},{2,98},{3,27},{4,100},{5,29},{6,102},{7,31},{8,104},... | collective-permute-start | bytes 2359304 | tf_op jit(solution)/shard_map/ppermute | solution.py:42
  54.7 12.1 %collective-permute-start.11 = (f16[384,1024]{1,0:T(8,128)(2,1)S(1)}, f16[384,1024]{1,0:T(8,128)(2,1)S(1)}, u32[]{:S(2)}, u32[]{:S(2)}) collective-permute-start(f16[384,1024]{1,0:T(8,128)(2,1)S(1)} %pad_maximum_fusion.2), channel_id=1, source_target_pairs={{0,2},{1,7},{2,0},{3,5},{4,6},{5,3},{6,4},{7,1},{8,10},{9,15},{10,... | collective-permute-start | bytes 2359304 | tf_op jit(solution)/shard_map/ppermute | solution.py:56
  62.7 7.0 %collective-permute-start.17 = (f16[128,1024]{1,0:T(8,128)(2,1)S(1)}, f16[128,1024]{1,0:T(8,128)(2,1)S(1)}, u32[]{:S(2)}, u32[]{:S(2)}) collective-permute-start(f16[128,1024]{1,0:T(8,128)(2,1)S(1)} %multiply_convert_fusion.1), channel_id=1, source_target_pairs={{0,2},{1,7},{2,0},{3,5},{4,6},{5,3},{6,4},{7,1},{8,10},{9,15},{10,... | collective-permute-start | bytes 786440 | tf_op jit(solution)/shard_map/ppermute | solution.py:56
  67.3 7.8 %collective-permute-start.14 = (f16[384,512]{1,0:T(8,128)(2,1)S(1)}, f16[384,512]{1,0:T(8,128)(2,1)S(1)}, u32[]{:S(2)}, u32[]{:S(2)}) collective-permute-start(f16[384,512]{1,0:T(8,128)(2,1)S(1)} %pad_maximum_fusion.5), channel_id=1, source_target_pairs={{0,6},{1,3},{2,4},{3,1},{4,2},{5,7},{6,0},{7,5},{8,14},{9,11},{10,... | collective-permute-start | bytes 1179656 | tf_op jit(solution)/shard_map/ppermute | solution.py:56
  69.8 7.1 %collective-permute-start.18 = (f16[128,512]{1,0:T(8,128)(2,1)S(1)}, f16[128,512]{1,0:T(8,128)(2,1)S(1)}, u32[]{:S(2)}, u32[]{:S(2)}) collective-permute-start(f16[128,512]{1,0:T(8,128)(2,1)S(1)} %fusion.5), channel_id=1, source_target_pairs={{0,6},{1,3},{2,4},{3,1},{4,2},{5,7},{6,0},{7,5},{8,14},{9,11},{10,... | collective-permute-start | bytes 393224 | tf_op jit(solution)/shard_map/ppermute | solution.py:56
  75.3 6.8 %collective-permute-start.15 = (f32[128,512]{1,0:T(8,128)S(1)}, f32[128,512]{1,0:T(8,128)S(1)}, u32[]{:S(2)}, u32[]{:S(2)}) collective-permute-start(f32[128,512]{1,0:T(8,128)S(1)} %get-tuple-element.73), channel_id=1, source_target_pairs={{0,96},{1,25},{2,98},{3,27},{4,100},{5,29},{6,102},{7,31},{8,104},... | collective-permute-start | bytes 786440 | tf_op jit(solution)/shard_map/ppermute | solution.py:42
  76.8 9.5 %collective-permute-start.16 = (f32[128,512]{1,0:T(8,128)S(1)}, f32[128,512]{1,0:T(8,128)S(1)}, u32[]{:S(2)}, u32[]{:S(2)}) collective-permute-start(f32[128,512]{1,0:T(8,128)S(1)} %get-tuple-element.72), channel_id=1, source_target_pairs={{0,32},{1,9},{2,34},{3,11},{4,36},{5,13},{6,38},{7,15},{8,40},{9,1... | collective-permute-start | bytes 786440 | tf_op jit(solution)/shard_map/ppermute | solution.py:42
  76.9 9.5 %collective-permute-start.19 = (f32[128,512]{1,0:T(8,128)S(1)}, f32[128,512]{1,0:T(8,128)S(1)}, u32[]{:S(2)}, u32[]{:S(2)}) collective-permute-start(f32[128,512]{1,0:T(8,128)S(1)} %slice_add_fusion), channel_id=1, source_target_pairs={{0,64},{1,17},{2,66},{3,19},{4,68},{5,21},{6,70},{7,23},{8,72},{9,... | collective-permute-start | bytes 786440 | tf_op jit(solution)/shard_map/ppermute | solution.py:42
  86.5 10.9 %collective-permute-start.21 = (f32[128,512]{1,0:T(8,128)S(1)}, f32[128,512]{1,0:T(8,128)S(1)}, u32[]{:S(2)}, u32[]{:S(2)}) collective-permute-start(f32[128,512]{1,0:T(8,128)S(1)} %pad_maximum_fusion.8), channel_id=1, source_target_pairs={{0,8},{1,33},{2,10},{3,35},{4,12},{5,37},{6,14},{7,39},{8,16},{9,4... | collective-permute-start | bytes 786440 | tf_op jit(solution)/shard_map/ppermute | solution.py:42
  86.6 17.1 %collective-permute-start.24 = (f32[64,4096]{1,0:T(8,128)}, f32[64,4096]{1,0:T(8,128)S(1)}, u32[]{:S(2)}, u32[]{:S(2)}) collective-permute-start(f32[64,4096]{1,0:T(8,128)} %get-tuple-element.68), channel_id=1, source_target_pairs={{0,1},{1,0},{2,3},{3,2},{4,5},{5,4},{6,7},{7,6},{8,9},{9,8},{10,11... | collective-permute-start | bytes 3145736 | tf_op jit(solution)/shard_map/ppermute | solution.py:60
  90.3 7.1 %collective-permute-start.22 = (f32[128,512]{1,0:T(8,128)S(1)}, f32[128,512]{1,0:T(8,128)S(1)}, u32[]{:S(2)}, u32[]{:S(2)}) collective-permute-start(f32[128,512]{1,0:T(8,128)S(1)} %pad_maximum_fusion.9), channel_id=1, source_target_pairs={{0,16},{1,65},{2,18},{3,67},{4,20},{5,69},{6,22},{7,71},{8,24},{9,... | collective-permute-start | bytes 786440 | tf_op jit(solution)/shard_map/ppermute | solution.py:42
  93.0 5.6 %collective-permute-start.20 = (f32[128,512]{1,0:T(8,128)S(1)}, f32[128,512]{1,0:T(8,128)S(1)}, u32[]{:S(2)}, u32[]{:S(2)}) collective-permute-start(f32[128,512]{1,0:T(8,128)S(1)} %pad_maximum_fusion.7), channel_id=1, source_target_pairs={{0,24},{1,97},{2,26},{3,99},{4,28},{5,101},{6,30},{7,103},{8,0},{9... | collective-permute-start | bytes 786440 | tf_op jit(solution)/shard_map/ppermute | solution.py:42
  99.4 4.3 %collective-permute-start.23 = (f32[512,256]{1,0:T(8,128)}, f32[512,256]{1,0:T(8,128)}, u32[]{:S(2)}, u32[]{:S(2)}) collective-permute-start(f32[512,256]{1,0:T(8,128)} %pad_maximum_fusion.4), channel_id=1, source_target_pairs={{0,1},{1,0},{2,3},{3,2},{4,5},{5,4},{6,7},{7,6},{8,9},{9,8},{10,11... | collective-permute-start | bytes 1572872 | tf_op jit(solution)/shard_map/ppermute | solution.py:60
  (5 other events, 48.9 us)

commit v3 on v2

--- a/solution.py
+++ b/solution.py
@@ -16,6 +16,7 @@
 VMEM_LIMIT = 24 * 1024 * 1024
 SCALE = 64.0
 F16 = jnp.float16
+HEAVY = pl.CostEstimate(flops=2**36, bytes_accessed=2**26, transcendentals=0)
 LIGHT = pl.CostEstimate(flops=1024, bytes_accessed=1024, transcendentals=0)
 RELS = (0, -1, 1, 2)
 
@@ -113,7 +114,7 @@
         outs[d // 2][:, at * TW:(at + 1) * TW] = got
 
 
-def ladder(tab, a_list, w_own, w_other):
+def ladder(tab, a_list, w_own, w_other, cost=LIGHT):
     rows, n = sum(a.shape[0] for a in a_list), len(a_list)
     vm = pl.BlockSpec(memory_space=pltpu.VMEM)
     return pl.pallas_call(
@@ -122,7 +123,7 @@
         out_specs=[vm] * 2,
         out_shape=[jax.ShapeDtypeStruct((rows, 8 * TW), F32)] * 2,
         compiler_params=pltpu.CompilerParams(vmem_limit_bytes=VMEM_LIMIT),
-        cost_estimate=LIGHT,
+        cost_estimate=cost,
         name="ladder",
     )(tab, *a_list, *w_own, *w_other)
 
@@ -147,7 +148,7 @@
         out_specs=[pl.BlockSpec((rows, step), lambda i: (0, i))] * 2,
         out_shape=[jax.ShapeDtypeStruct((rows, width), F32)] * 2,
         compiler_params=pltpu.CompilerParams(vmem_limit_bytes=VMEM_LIMIT),
-        cost_estimate=LIGHT,
+        cost_estimate=HEAVY,
         name="hole",
     )(h_rel, *a_list, *a_list)
 
@@ -248,8 +249,6 @@
 
     q_ma, q_pa, w_other, where, occ, h_rel = hold((q_ma, q_pa, w_other, where, occ, h_rel))
     q_2a = along(q_ma, False, 1)
-    q_2b = along(q_pb, False, -1)
-    a_list = [s_a, s_b, q_ma, q_mb, q_pa, q_pb, q_2a, q_2b]
 
     mid = 4 * TW
     block = RING * half
@@ -260,30 +259,41 @@
     def decoded(value):
         return value.astype(F32) * (1.0 / SCALE)
 
-    keep_0, send_0 = ladder(tab, a_list[:2], w_own, w_other)
-    q_mb, q_pb, keep_0, send_0 = hold((q_mb, q_pb, keep_0, send_0))
-    keep_1, send_1 = ladder(tab, [q_ma, q_mb, q_pa, q_pb], w_own, w_other)
-    near_got = across_x(jnp.concatenate([coded(send_0), coded(send_1)], axis=0), True)
+    def halves(keep, got):
+        total = keep + decoded(got)
+        return total[:, :mid], coded(total[:, mid:])
+
+    keep_0, send_0 = ladder(tab, [s_a, s_b], w_own, w_other)
+    got_0 = across_x(send_0, True)
+    q_pb, keep_0 = hold((q_pb, keep_0))
+    q_2b = along(q_pb, False, -1)
+    q_mb, got_0 = hold((q_mb, got_0))
+    sum_0 = keep_0 + got_0
+    end_0 = across_x(sum_0[:, mid:], False)
+    a_list = [s_a, s_b, q_ma, q_mb, q_pa, q_pb, q_2a, q_2b]
+    keep_1, send_1 = ladder(tab, a_list[2:6], w_own, w_other)
+    got_1 = across_x(coded(send_1), True)
     keep_2, send_2 = ladder(tab, a_list[6:], w_own, w_other)
-    far_send = coded(send_2)
-    far_got = across_x(far_send, True)
-    near_got, _ = hold((near_got, far_send))
-    sum_0 = keep_0 + decoded(near_got[:block])
-    sum_1 = keep_1 + decoded(near_got[block:])
-    near_end = across_x(jnp.concatenate([coded(sum_0[:, mid:]), coded(sum_1[:, mid:])], axis=0), False)
-    sum_2 = keep_2 + decoded(far_got)
-    far_end = across_x(coded(sum_2[:, mid:]), False)
-    near_end, h_rel = hold((near_end, h_rel))
-    t_0 = sum_0[:, :mid] + decoded(near_end[:block])
-    t_m = sum_1[:block, :mid] + decoded(near_end[block:2 * block])
-    t_p = sum_1[block:, :mid] + decoded(near_end[2 * block:])
-    t_2 = sum_2[:, :mid] + decoded(far_end)
-
-    from_p = along(t_m, False, -1)
-    from_m = along(t_p, False, 1)
-    from_2 = along(t_2, False, 2)
+    got_1, keep_2, send_2 = hold((got_1, keep_2, send_2))
+    sum_1, fwd_1 = halves(keep_1, got_1)
+    end_1 = across_x(fwd_1, False)
+    far_parts = [coded(keep_2[:, mid:]), coded(send_2[:, :mid]), coded(send_2[:, mid:])]
+    far_got = [
+        across_x(far_parts[0], False),
+        across_x(far_parts[1], True),
+        lax.ppermute(far_parts[2], "x", [(i, (i + 2) % RING) for i in range(RING)]),
+    ]
     hole_own, hole_send = hole_part(h_rel, a_list, width)
-    from_p, from_m, from_2, hole_send = hold((from_p, from_m, from_2, hole_send))
+    far_got, hole_send = hold((far_got, hole_send))
+    t_0 = sum_0[:, :mid] + end_0
+    t_m = sum_1[:block] + decoded(end_1[:block])
+    t_p = sum_1[block:] + decoded(end_1[block:])
+    t_2 = keep_2[:, :mid] + sum(decoded(part) for part in far_got)
+
+    from_p = decoded(along(coded(t_m), False, -1))
+    from_m = decoded(along(coded(t_p), False, 1))
+    from_2 = decoded(along(coded(t_2), False, 2))
+    from_p, from_m, from_2 = hold((from_p, from_m, from_2))
     hole_got = other_core(hole_send)
     back = [t_0, from_m, from_p, from_2]
     keeps = []

time: 106 us -> 103 us (0.972)
  waiting for transfers between devices: 39.4 us -> 29 us
  starting transfers between devices: 36.7 us -> 43.7 us
    ppermute x16, waiting for transfers between devices: 29.1 us -> 22.5 us  [along(): return lax.ppermute(value, AXES, perm_of(first, step))]
    ppermute x4 -> x6, waiting for transfers between devices: 8.54 us -> 3.62 us  [across_x(): return lax.ppermute(value, AXES, pairs)]
    ppermute x4 -> x6, starting transfers between devices: 5.85 us -> 9.77 us  [across_x(): return lax.ppermute(value, AXES, pairs)]
    ppermute x16, starting transfers between devices: 21.7 us -> 24.3 us  [along(): return lax.ppermute(value, AXES, perm_of(first, step))]
    ppermute x0 -> x1, waiting for transfers between devices: none -> 1.16 us  [local(): lax.ppermute(far_parts[2], 'x', [(i, (i + 2) % RING) for i in range(RING)])]
  transfers between devices with their start and end apart: 25 -> 28, of which waited for: 13 -> 13; matrix products, arithmetic and copies ran while one was open for 5% -> 5% of each run, Pallas kernels for 19% -> 20%
where the time goes in v3:
time: 103 us; the launch traced here: 102 us
  starting transfers between devices  43.7 us (42%)
  waiting for transfers between devices  29 us (28%)
  Pallas kernels  22.5 us (22%)
  other arithmetic  4.24 us (4%)
  local copies, waits for them, and re-layouts  1.49 us (1%)
    ppermute x16, starting transfers between devices, along(): return lax.ppermute(value, AXES, perm_of(first, step))  24.3 us
    ppermute x16, waiting for transfers between devices, along(): return lax.ppermute(value, AXES, perm_of(first, step))  22.5 us
    ppermute x6, starting transfers between devices, across_x(): return lax.ppermute(value, AXES, pairs)  9.77 us
    pallas_call x2, Pallas kernels, select(): pl.pallas_call(functools.partial(select_kernel, first_block=first_block),...  9.44 us
    ppermute x5, starting transfers between devices, other_core(): return lax.ppermute(value, 'core', [(0, 1), (1, 0)])  9.43 us
    pallas_call x3, Pallas kernels, ladder(): pl.pallas_call(functools.partial(ladder_kernel, n=n), in_specs=[pl.BlockS...  7.04 us
    ppermute x6, waiting for transfers between devices, across_x(): return lax.ppermute(value, AXES, pairs)  3.62 us
    pallas_call x1, Pallas kernels, hole_part(): pl.pallas_call(hole_kernel, grid=(steps,), in_specs=[pl.BlockSpec(h_rel.s...  3.55 us
  transfers between devices with their start and end apart: 28, of which 13 were waited for; matrix products, arithmetic and copies ran while one was open for 5% of the time, Pallas kernels for 20%

profile of v3, /device:TPU:1, one launch (start us, length us, event | category | flops | bytes accessed | tf_op | source)
XLA Modules:
  0.0 102.5 jit_solution(7604967060400515739)
XLA Ops:
  6.8 2.2 %collective-permute-start.2 = (bf16[32,8192]{1,0:T(8,128)(2,1)S(1)}, bf16[32,8192]{1,0:T(8,128)(2,1)S(1)}, u32[]{:S(2)}, u32[]{:S(2)}) collective-permute-start(bf16[32,8192]{1,0:T(8,128)(2,1)S(1)} %pad_maximum_fusion.2), channel_id=1, source_target_pairs={{0,24},{1,97},{2,26},{3,99},{4,28},{5,101},{6,30},{7,103},{8,0},{9... | collective-permute-start | bytes 1572872 | tf_op jit(solution)/shard_map/ppermute | solution.py:43
  9.7 4.7 %select.141.refs_2_.refs_4_ = bf16[16,256,128]{2,1,0:T(8,128)(2,1)S(1)} custom-call(s32[256]{0:T(256)S(1)} %select_n.429.tab, bf16[32768,256]{1,0:T(8,128)(2,1)} %bitcast.7), custom_call_target="tpu_custom_call" | custom-call | flops 1024 | bytes 1024 | tf_op jit(solution)/shard_map/select/pallas_call | solution.py:88
  15.6 3.1 %collective-permute-start.7 = (bf16[16,8192]{1,0:T(8,128)(2,1)S(1)}, bf16[16,8192]{1,0:T(8,128)(2,1)S(1)}, u32[]{:S(2)}, u32[]{:S(2)}) collective-permute-start(bf16[16,8192]{1,0:T(8,128)(2,1)S(1)} %get-tuple-element.82), channel_id=1, source_target_pairs={{0,24},{1,97},{2,26},{3,99},{4,28},{5,101},{6,30},{7,103},{8,0},{9... | collective-permute-start | bytes 786440 | tf_op jit(solution)/shard_map/ppermute | solution.py:43
  20.1 2.2 %collective-permute-start.4 = (bf16[80,8192]{1,0:T(8,128)(2,1)S(1)}, bf16[80,8192]{1,0:T(8,128)(2,1)S(1)}, u32[]{:S(2)}, u32[]{:S(2)}) collective-permute-start(bf16[80,8192]{1,0:T(8,128)(2,1)S(1)} %pad_maximum_fusion.refs_0_.refs_8_), channel_id=1, source_target_pairs={{0,96},{1,25},{2,98},{3,27},{4,100},{5,29},{6,102},{7,31},{8,104},... | collective-permute-start | bytes 3932168 | tf_op jit(solution)/shard_map/ppermute | solution.py:43
  22.2 4.7 %select.142.refs_3_.refs_5_ = bf16[16,256,128]{2,1,0:T(8,128)(2,1)S(1)} custom-call(s32[256]{0:T(256)S(1)} %select_n.429.tab, bf16[32768,256]{1,0:T(8,128)(2,1)} %bitcast.8), custom_call_target="tpu_custom_call" | custom-call | flops 1024 | bytes 1024 | tf_op jit(solution)/shard_map/select/pallas_call | solution.py:88
  27.0 2.4 %collective-permute-start.8 = (bf16[16,256,128]{2,1,0:T(8,128)(2,1)S(1)}, bf16[16,256,128]{2,1,0:T(8,128)(2,1)S(1)}, u32[]{:S(2)}, u32[]{:S(2)}) collective-permute-start(bf16[16,256,128]{2,1,0:T(8,128)(2,1)S(1)} %select.142.refs_3_.refs_5_), channel_id=1, source_target_pairs={{0,1},{1,0},{2,3},{3,2},{4,5},{5,4},{6,7},{7,6},{8,9},{9,8},{10,11... | collective-permute-start | bytes 3145736 | tf_op jit(solution)/shard_map/ppermute | solution.py:61
  31.8 8.4 %collective-permute-done.3.refs_0_.refs_2_.refs_10_ = bf16[80,8192]{1,0:T(8,128)(2,1)S(1)} collective-permute-done((bf16[80,8192]{1,0:T(8,128)(2,1)S(1)}, bf16[80,8192]{1,0:T(8,128)(2,1)S(1)}, u32[]{:S(2)}, u32[]{:S(2)}) %collective-permute-start.3) | collective-permute-done | bytes 1310752 | tf_op jit(solution)/shard_map/ppermute | solution.py:43
  40.2 2.0 %ladder.3 = (f32[128,1024]{1,0:T(8,128)S(1)}, f32[128,1024]{1,0:T(8,128)S(1)}) custom-call(s32[256]{0:T(256)S(1)} %select_n.429.tab, bf16[80,8192]{1,0:T(8,128)(2,1)S(1)} %pad_maximum_fusion.refs_0_.refs_8_, bf16[48,8192]{1,0:T(8,128)(2,1)S(1)} %pad_maximum_fusion.1.refs_1_.refs_9_, bf16[16,256,128]{2,1,0:T(8,128)(2,1)S(1)} %select.141.refs_2_.refs_4_, ...), custom_call_target="tpu_custom_call" | custom-call | flops 1024 | bytes 1024 | tf_op jit(solution)/shard_map/ladder/pallas_call | solution.py:120
  42.2 2.6 %collective-permute-start.11 = (f32[128,1024]{1,0:T(8,128)S(1)}, f32[128,1024]{1,0:T(8,128)S(1)}, u32[]{:S(2)}, u32[]{:S(2)}) collective-permute-start(f32[128,1024]{1,0:T(8,128)S(1)} %get-tuple-element.52), channel_id=1, source_target_pairs={{0,2},{1,7},{2,0},{3,5},{4,6},{5,3},{6,4},{7,1},{8,10},{9,15},{10,... | collective-permute-start | bytes 1572872 | tf_op jit(solution)/shard_map/ppermute | solution.py:57
  45.2 3.4 %collective-permute-start.15 = (bf16[48,8192]{1,0:T(8,128)(2,1)S(1)}, bf16[48,8192]{1,0:T(8,128)(2,1)S(1)}, u32[]{:S(2)}, u32[]{:S(2)}) collective-permute-start(bf16[48,8192]{1,0:T(8,128)(2,1)S(1)} %collective-permute-done.9.refs_3_.refs_5_.refs_13_), channel_id=1, source_target_pairs={{0,96},{1,25},{2,98},{3,27},{4,100},{5,29},{6,102},{7,31},{8,104},... | collective-permute-start | bytes 2359304 | tf_op jit(solution)/shard_map/ppermute | solution.py:43
  48.7 3.2 %collective-permute-done.11 = f32[128,1024]{1,0:T(8,128)S(1)} collective-permute-done((f32[128,1024]{1,0:T(8,128)S(1)}, f32[128,1024]{1,0:T(8,128)S(1)}, u32[]{:S(2)}, u32[]{:S(2)}) %collective-permute-start.11) | collective-permute-done | bytes 524320 | tf_op jit(solution)/shard_map/ppermute | solution.py:57
  52.3 3.1 %ladder.4 = (f32[256,1024]{1,0:T(8,128)S(1)}, f32[256,1024]{1,0:T(8,128)S(1)}) custom-call(s32[256]{0:T(256)S(1)} %select_n.429.tab, bf16[80,8192]{1,0:T(8,128)(2,1)S(1)} %collective-permute-done.3.refs_0_.refs_2_.refs_10_, bf16[48,8192]{1,0:T(8,128)(2,1)S(1)} %collective-permute-done.10.refs_1_.refs_3_.refs_11_, ...), custom_call_target="tpu_custom_call" | custom-call | flops 1024 | bytes 1024 | tf_op jit(solution)/shard_map/ladder/pallas_call | solution.py:120
  55.5 2.6 %collective-permute-start.13 = (f16[256,1024]{1,0:T(8,128)(2,1)S(1)}, f16[256,1024]{1,0:T(8,128)(2,1)S(1)}, u32[]{:S(2)}, u32[]{:S(2)}) collective-permute-start(f16[256,1024]{1,0:T(8,128)(2,1)S(1)} %multiply_convert_fusion), channel_id=1, source_target_pairs={{0,2},{1,7},{2,0},{3,5},{4,6},{5,3},{6,4},{7,1},{8,10},{9,15},{10,... | collective-permute-start | bytes 1572872 | tf_op jit(solution)/shard_map/ppermute | solution.py:57
  58.1 4.4 %collective-permute-done.14.refs_0_.refs_6_.refs_14_ = bf16[80,8192]{1,0:T(8,128)(2,1)S(1)} collective-permute-done((bf16[80,8192]{1,0:T(8,128)(2,1)S(1)}, bf16[80,8192]{1,0:T(8,128)(2,1)S(1)}, u32[]{:S(2)}, u32[]{:S(2)}) %collective-permute-start.14) | collective-permute-done | bytes 1310752 | tf_op jit(solution)/shard_map/ppermute | solution.py:43
  64.9 2.6 %collective-permute-start.20 = (f16[128,512]{1,0:T(8,128)(2,1)S(1)}, f16[128,512]{1,0:T(8,128)(2,1)S(1)}, u32[]{:S(2)}, u32[]{:S(2)}) collective-permute-start(f16[128,512]{1,0:T(8,128)(2,1)S(1)} %get-tuple-element.81), channel_id=1, source_target_pairs={{0,2},{1,7},{2,0},{3,5},{4,6},{5,3},{6,4},{7,1},{8,10},{9,15},{10,... | collective-permute-start | bytes 393224 | tf_op jit(solution)/shard_map/ppermute | solution.py:57
  69.6 3.6 %hole.1 = (f32[64,4096]{1,0:T(8,128)S(1)}, f32[64,4096]{1,0:T(8,128)}) custom-call(bf16[64,512]{1,0:T(8,128)(2,1)S(1)} %fusion.2.h_ref, bf16[80,8192]{1,0:T(8,128)(2,1)S(1)} %pad_maximum_fusion.refs_0_.refs_8_, bf16[48,8192]{1,0:T(8,128)(2,1)S(1)} %pad_maximum_fusion.1.refs_1_.refs_9_, bf16[80,8192]{1,0:T(8,128)(2,1)S(1)} %collective-permute-done.3.refs_0_.refs_2_.refs_10_, ...), custom_call_target="tpu_custom_call" | custom-call | flops 68719476736 | bytes 67108864 | tf_op jit(solution)/shard_map/hole/pallas_call | solution.py:144
  76.5 2.6 %collective-permute-start.27 = (f32[64,4096]{1,0:T(8,128)}, f32[64,4096]{1,0:T(8,128)S(1)}, u32[]{:S(2)}, u32[]{:S(2)}) collective-permute-start(f32[64,4096]{1,0:T(8,128)} %get-tuple-element.74), channel_id=1, source_target_pairs={{0,1},{1,0},{2,3},{3,2},{4,5},{5,4},{6,7},{7,6},{8,9},{9,8},{10,11... | collective-permute-start | bytes 3145736 | tf_op jit(solution)/shard_map/ppermute | solution.py:61
  79.4 2.6 %collective-permute-start.17 = (f16[128,512]{1,0:T(8,128)(2,1)S(1)}, f16[128,512]{1,0:T(8,128)(2,1)S(1)}, u32[]{:S(2)}, u32[]{:S(2)}) collective-permute-start(f16[128,512]{1,0:T(8,128)(2,1)S(1)} %get-tuple-element.79), channel_id=1, source_target_pairs={{0,96},{1,25},{2,98},{3,27},{4,100},{5,29},{6,102},{7,31},{8,104},... | collective-permute-start | bytes 393224 | tf_op jit(solution)/shard_map/ppermute | solution.py:43
  82.0 2.6 %collective-permute-done.18 = f16[128,512]{1,0:T(8,128)(2,1)S(1)} collective-permute-done((f16[128,512]{1,0:T(8,128)(2,1)S(1)}, f16[128,512]{1,0:T(8,128)(2,1)S(1)}, u32[]{:S(2)}, u32[]{:S(2)}) %collective-permute-start.18) | collective-permute-done | bytes 131104 | tf_op jit(solution)/shard_map/ppermute | solution.py:43
  86.8 2.3 %collective-permute-start.23 = (f32[128,512]{1,0:T(8,128)S(1)}, f32[128,512]{1,0:T(8,128)S(1)}, u32[]{:S(2)}, u32[]{:S(2)}) collective-permute-start(f32[128,512]{1,0:T(8,128)S(1)} %pad_maximum_fusion.5), channel_id=1, source_target_pairs={{0,24},{1,97},{2,26},{3,99},{4,28},{5,101},{6,30},{7,103},{8,0},{9... | collective-permute-start | bytes 786440 | tf_op jit(solution)/shard_map/ppermute | solution.py:43
  89.1 2.8 %collective-permute-done.25.refs_3_ = f32[128,512]{1,0:T(8,128)S(1)} collective-permute-done((f32[128,512]{1,0:T(8,128)S(1)}, f32[128,512]{1,0:T(8,128)S(1)}, u32[]{:S(2)}, u32[]{:S(2)}) %collective-permute-start.25) | collective-permute-done | bytes 262176 | tf_op jit(solution)/shard_map/ppermute | solution.py:43
  91.9 2.8 %collective-permute-done.24.refs_2_ = f32[128,512]{1,0:T(8,128)S(1)} collective-permute-done((f32[128,512]{1,0:T(8,128)S(1)}, f32[128,512]{1,0:T(8,128)S(1)}, u32[]{:S(2)}, u32[]{:S(2)}) %collective-permute-start.24) | collective-permute-done | bytes 262176 | tf_op jit(solution)/shard_map/ppermute | solution.py:43
  95.6 2.6 %collective-permute-start.26 = (f32[512,256]{1,0:T(8,128)}, f32[512,256]{1,0:T(8,128)}, u32[]{:S(2)}, u32[]{:S(2)}) collective-permute-start(f32[512,256]{1,0:T(8,128)} %pad_maximum_fusion.3), channel_id=1, source_target_pairs={{0,1},{1,0},{2,3},{3,2},{4,5},{5,4},{6,7},{7,6},{8,9},{9,8},{10,11... | collective-permute-start | bytes 1572872 | tf_op jit(solution)/shard_map/ppermute | solution.py:61
  100.0 2.5 %finish.1 = (f32[64,4096]{1,0:T(8,128)}, bf16[64,4096]{1,0:T(8,128)(2,1)}) custom-call(s32[33]{0:T(128)S(1)} %compare_select_fusion.20.where, f32[128,512]{1,0:T(8,128)S(1)} %pad_maximum_fusion.4.refs_0_, f32[128,512]{1,0:T(8,128)S(1)} %collective-permute-done.23.refs_1_, f32[128,512]{1,0:T(8,128)S(1)} %collective-permute-done.24.refs_2_, ...), custom_call_target="tpu_custom_call" | custom-call | flops 1024 | bytes 1024 | tf_op jit(solution)/shard_map/finish/pallas_call | solution.py:174
  (95 shorter events, 25.7 us)
Async XLA Ops:
  5.0 10.5 %collective-permute-start.1 = (bf16[32,8192]{1,0:T(8,128)(2,1)S(1)}, bf16[32,8192]{1,0:T(8,128)(2,1)S(1)}, u32[]{:S(2)}, u32[]{:S(2)}) collective-permute-start(bf16[32,8192]{1,0:T(8,128)(2,1)S(1)} %pad_maximum_fusion.2), channel_id=1, source_target_pairs={{0,8},{1,33},{2,10},{3,35},{4,12},{5,37},{6,14},{7,39},{8,16},{9,4... | collective-permute-start | bytes 1572872 | tf_op jit(solution)/shard_map/ppermute | solution.py:43
  6.8 8.7 %collective-permute-start.2 = (bf16[32,8192]{1,0:T(8,128)(2,1)S(1)}, bf16[32,8192]{1,0:T(8,128)(2,1)S(1)}, u32[]{:S(2)}, u32[]{:S(2)}) collective-permute-start(bf16[32,8192]{1,0:T(8,128)(2,1)S(1)} %pad_maximum_fusion.2), channel_id=1, source_target_pairs={{0,24},{1,97},{2,26},{3,99},{4,28},{5,101},{6,30},{7,103},{8,0},{9... | collective-permute-start | bytes 1572872 | tf_op jit(solution)/shard_map/ppermute | solution.py:43
  15.6 11.4 %collective-permute-start.7 = (bf16[16,8192]{1,0:T(8,128)(2,1)S(1)}, bf16[16,8192]{1,0:T(8,128)(2,1)S(1)}, u32[]{:S(2)}, u32[]{:S(2)}) collective-permute-start(bf16[16,8192]{1,0:T(8,128)(2,1)S(1)} %get-tuple-element.82), channel_id=1, source_target_pairs={{0,24},{1,97},{2,26},{3,99},{4,28},{5,101},{6,30},{7,103},{8,0},{9... | collective-permute-start | bytes 786440 | tf_op jit(solution)/shard_map/ppermute | solution.py:43
  18.7 8.3 %collective-permute-start.6 = (bf16[16,8192]{1,0:T(8,128)(2,1)S(1)}, bf16[16,8192]{1,0:T(8,128)(2,1)S(1)}, u32[]{:S(2)}, u32[]{:S(2)}) collective-permute-start(bf16[16,8192]{1,0:T(8,128)(2,1)S(1)} %slice.107), channel_id=1, source_target_pairs={{0,8},{1,33},{2,10},{3,35},{4,12},{5,37},{6,14},{7,39},{8,16},{9,4... | collective-permute-start | bytes 786440 | tf_op jit(solution)/shard_map/ppermute | solution.py:43
  18.8 12.5 %collective-permute-start.5 = (bf16[16,256,128]{2,1,0:T(8,128)(2,1)S(1)}, bf16[16,256,128]{2,1,0:T(8,128)(2,1)S(1)}, u32[]{:S(2)}, u32[]{:S(2)}) collective-permute-start(bf16[16,256,128]{2,1,0:T(8,128)(2,1)S(1)} %select.141.refs_2_.refs_4_), channel_id=1, source_target_pairs={{0,1},{1,0},{2,3},{3,2},{4,5},{5,4},{6,7},{7,6},{8,9},{9,8},{10,11... | collective-permute-start | bytes 3145736 | tf_op jit(solution)/shard_map/ppermute | solution.py:61
  19.2 21.0 %collective-permute-start.3 = (bf16[80,8192]{1,0:T(8,128)(2,1)S(1)}, bf16[80,8192]{1,0:T(8,128)(2,1)S(1)}, u32[]{:S(2)}, u32[]{:S(2)}) collective-permute-start(bf16[80,8192]{1,0:T(8,128)(2,1)S(1)} %pad_maximum_fusion.refs_0_.refs_8_), channel_id=1, source_target_pairs={{0,32},{1,9},{2,34},{3,11},{4,36},{5,13},{6,38},{7,15},{8,40},{9,1... | collective-permute-start | bytes 3932168 | tf_op jit(solution)/shard_map/ppermute | solution.py:43
  20.1 20.2 %collective-permute-start.4 = (bf16[80,8192]{1,0:T(8,128)(2,1)S(1)}, bf16[80,8192]{1,0:T(8,128)(2,1)S(1)}, u32[]{:S(2)}, u32[]{:S(2)}) collective-permute-start(bf16[80,8192]{1,0:T(8,128)(2,1)S(1)} %pad_maximum_fusion.refs_0_.refs_8_), channel_id=1, source_target_pairs={{0,96},{1,25},{2,98},{3,27},{4,100},{5,29},{6,102},{7,31},{8,104},... | collective-permute-start | bytes 3932168 | tf_op jit(solution)/shard_map/ppermute | solution.py:43
  29.5 15.8 %collective-permute-start.9 = (bf16[48,8192]{1,0:T(8,128)(2,1)S(1)}, bf16[48,8192]{1,0:T(8,128)(2,1)S(1)}, u32[]{:S(2)}, u32[]{:S(2)}) collective-permute-start(bf16[48,8192]{1,0:T(8,128)(2,1)S(1)} %pad_maximum_fusion.1.refs_1_.refs_9_), channel_id=1, source_target_pairs={{0,96},{1,25},{2,98},{3,27},{4,100},{5,29},{6,102},{7,31},{8,104},... | collective-permute-start | bytes 2359304 | tf_op jit(solution)/shard_map/ppermute | solution.py:43
  31.3 17.3 %collective-permute-start.10 = (bf16[48,8192]{1,0:T(8,128)(2,1)S(1)}, bf16[48,8192]{1,0:T(8,128)(2,1)S(1)}, u32[]{:S(2)}, u32[]{:S(2)}) collective-permute-start(bf16[48,8192]{1,0:T(8,128)(2,1)S(1)} %pad_maximum_fusion.1.refs_1_.refs_9_), channel_id=1, source_target_pairs={{0,32},{1,9},{2,34},{3,11},{4,36},{5,13},{6,38},{7,15},{8,40},{9,1... | collective-permute-start | bytes 2359304 | tf_op jit(solution)/shard_map/ppermute | solution.py:43
  42.2 9.6 %collective-permute-start.11 = (f32[128,1024]{1,0:T(8,128)S(1)}, f32[128,1024]{1,0:T(8,128)S(1)}, u32[]{:S(2)}, u32[]{:S(2)}) collective-permute-start(f32[128,1024]{1,0:T(8,128)S(1)} %get-tuple-element.52), channel_id=1, source_target_pairs={{0,2},{1,7},{2,0},{3,5},{4,6},{5,3},{6,4},{7,1},{8,10},{9,15},{10,... | collective-permute-start | bytes 1572872 | tf_op jit(solution)/shard_map/ppermute | solution.py:57
  44.9 17.7 %collective-permute-start.14 = (bf16[80,8192]{1,0:T(8,128)(2,1)S(1)}, bf16[80,8192]{1,0:T(8,128)(2,1)S(1)}, u32[]{:S(2)}, u32[]{:S(2)}) collective-permute-start(bf16[80,8192]{1,0:T(8,128)(2,1)S(1)} %collective-permute-done.3.refs_0_.refs_2_.refs_10_), channel_id=1, source_target_pairs={{0,32},{1,9},{2,34},{3,11},{4,36},{5,13},{6,38},{7,15},{8,40},{9,1... | collective-permute-start | bytes 3932168 | tf_op jit(solution)/shard_map/ppermute | solution.py:43
  45.2 12.9 %collective-permute-start.15 = (bf16[48,8192]{1,0:T(8,128)(2,1)S(1)}, bf16[48,8192]{1,0:T(8,128)(2,1)S(1)}, u32[]{:S(2)}, u32[]{:S(2)}) collective-permute-start(bf16[48,8192]{1,0:T(8,128)(2,1)S(1)} %collective-permute-done.9.refs_3_.refs_5_.refs_13_), channel_id=1, source_target_pairs={{0,96},{1,25},{2,98},{3,27},{4,100},{5,29},{6,102},{7,31},{8,104},... | collective-permute-start | bytes 2359304 | tf_op jit(solution)/shard_map/ppermute | solution.py:43
  52.0 6.1 %collective-permute-start.12 = (f32[128,512]{1,0:T(8,128)S(1)}, f32[128,512]{1,0:T(8,128)S(1)}, u32[]{:S(2)}, u32[]{:S(2)}) collective-permute-start(f32[128,512]{1,0:T(8,128)S(1)} %slice.141), channel_id=1, source_target_pairs={{0,6},{1,3},{2,4},{3,1},{4,2},{5,7},{6,0},{7,5},{8,14},{9,11},{10,... | collective-permute-start | bytes 786440 | tf_op jit(solution)/shard_map/ppermute | solution.py:57
  55.5 9.3 %collective-permute-start.13 = (f16[256,1024]{1,0:T(8,128)(2,1)S(1)}, f16[256,1024]{1,0:T(8,128)(2,1)S(1)}, u32[]{:S(2)}, u32[]{:S(2)}) collective-permute-start(f16[256,1024]{1,0:T(8,128)(2,1)S(1)} %multiply_convert_fusion), channel_id=1, source_target_pairs={{0,2},{1,7},{2,0},{3,5},{4,6},{5,3},{6,4},{7,1},{8,10},{9,15},{10,... | collective-permute-start | bytes 1572872 | tf_op jit(solution)/shard_map/ppermute | solution.py:57
  64.9 8.3 %collective-permute-start.20 = (f16[128,512]{1,0:T(8,128)(2,1)S(1)}, f16[128,512]{1,0:T(8,128)(2,1)S(1)}, u32[]{:S(2)}, u32[]{:S(2)}) collective-permute-start(f16[128,512]{1,0:T(8,128)(2,1)S(1)} %get-tuple-element.81), channel_id=1, source_target_pairs={{0,2},{1,7},{2,0},{3,5},{4,6},{5,3},{6,4},{7,1},{8,10},{9,15},{10,... | collective-permute-start | bytes 393224 | tf_op jit(solution)/shard_map/ppermute | solution.py:57
  67.4 6.9 %collective-permute-start.21 = (f16[128,512]{1,0:T(8,128)(2,1)S(1)}, f16[128,512]{1,0:T(8,128)(2,1)S(1)}, u32[]{:S(2)}, u32[]{:S(2)}) collective-permute-start(f16[128,512]{1,0:T(8,128)(2,1)S(1)} %get-tuple-element.80), channel_id=1, source_target_pairs={{0,4},{2,6},{4,0},{6,2},{1,5},{3,7},{5,1},{7,3},{8,12},{10,14},{12... | collective-permute-start | bytes 393224 | tf_op jit(solution)/shard_map/ppermute | solution.py:284
  67.7 6.8 %collective-permute-start.19 = (f16[128,512]{1,0:T(8,128)(2,1)S(1)}, f16[128,512]{1,0:T(8,128)(2,1)S(1)}, u32[]{:S(2)}, u32[]{:S(2)}) collective-permute-start(f16[128,512]{1,0:T(8,128)(2,1)S(1)} %multiply_convert_fusion.4), channel_id=1, source_target_pairs={{0,6},{1,3},{2,4},{3,1},{4,2},{5,7},{6,0},{7,5},{8,14},{9,11},{10,... | collective-permute-start | bytes 393224 | tf_op jit(solution)/shard_map/ppermute | solution.py:57
  68.6 10.5 %collective-permute-start.16 = (f16[256,512]{1,0:T(8,128)(2,1)S(1)}, f16[256,512]{1,0:T(8,128)(2,1)S(1)}, u32[]{:S(2)}, u32[]{:S(2)}) collective-permute-start(f16[256,512]{1,0:T(8,128)(2,1)S(1)} %fusion.4), channel_id=1, source_target_pairs={{0,6},{1,3},{2,4},{3,1},{4,2},{5,7},{6,0},{7,5},{8,14},{9,11},{10,... | collective-permute-start | bytes 786440 | tf_op jit(solution)/shard_map/ppermute | solution.py:57
  74.6 7.4 %collective-permute-start.22 = (f16[128,512]{1,0:T(8,128)(2,1)S(1)}, f16[128,512]{1,0:T(8,128)(2,1)S(1)}, u32[]{:S(2)}, u32[]{:S(2)}) collective-permute-start(f16[128,512]{1,0:T(8,128)(2,1)S(1)} %multiply_convert_fusion.1), channel_id=1, source_target_pairs={{0,64},{1,17},{2,66},{3,19},{4,68},{5,21},{6,70},{7,23},{8,72},{9,... | collective-permute-start | bytes 393224 | tf_op jit(solution)/shard_map/ppermute | solution.py:43
  76.5 23.5 %collective-permute-start.27 = (f32[64,4096]{1,0:T(8,128)}, f32[64,4096]{1,0:T(8,128)S(1)}, u32[]{:S(2)}, u32[]{:S(2)}) collective-permute-start(f32[64,4096]{1,0:T(8,128)} %get-tuple-element.74), channel_id=1, source_target_pairs={{0,1},{1,0},{2,3},{3,2},{4,5},{5,4},{6,7},{7,6},{8,9},{9,8},{10,11... | collective-permute-start | bytes 3145736 | tf_op jit(solution)/shard_map/ppermute | solution.py:61
  79.2 5.4 %collective-permute-start.18 = (f16[128,512]{1,0:T(8,128)(2,1)S(1)}, f16[128,512]{1,0:T(8,128)(2,1)S(1)}, u32[]{:S(2)}, u32[]{:S(2)}) collective-permute-start(f16[128,512]{1,0:T(8,128)(2,1)S(1)} %get-tuple-element.78), channel_id=1, source_target_pairs={{0,32},{1,9},{2,34},{3,11},{4,36},{5,13},{6,38},{7,15},{8,40},{9,1... | collective-permute-start | bytes 393224 | tf_op jit(solution)/shard_map/ppermute | solution.py:43
  84.8 7.1 %collective-permute-start.25 = (f32[128,512]{1,0:T(8,128)S(1)}, f32[128,512]{1,0:T(8,128)S(1)}, u32[]{:S(2)}, u32[]{:S(2)}) collective-permute-start(f32[128,512]{1,0:T(8,128)S(1)} %pad_maximum_fusion.7), channel_id=1, source_target_pairs={{0,16},{1,65},{2,18},{3,67},{4,20},{5,69},{6,22},{7,71},{8,24},{9,... | collective-permute-start | bytes 786440 | tf_op jit(solution)/shard_map/ppermute | solution.py:43
  86.2 8.5 %collective-permute-start.24 = (f32[128,512]{1,0:T(8,128)S(1)}, f32[128,512]{1,0:T(8,128)S(1)}, u32[]{:S(2)}, u32[]{:S(2)}) collective-permute-start(f32[128,512]{1,0:T(8,128)S(1)} %pad_maximum_fusion.6), channel_id=1, source_target_pairs={{0,8},{1,33},{2,10},{3,35},{4,12},{5,37},{6,14},{7,39},{8,16},{9,4... | collective-permute-start | bytes 786440 | tf_op jit(solution)/shard_map/ppermute | solution.py:43
  86.8 7.9 %collective-permute-start.23 = (f32[128,512]{1,0:T(8,128)S(1)}, f32[128,512]{1,0:T(8,128)S(1)}, u32[]{:S(2)}, u32[]{:S(2)}) collective-permute-start(f32[128,512]{1,0:T(8,128)S(1)} %pad_maximum_fusion.5), channel_id=1, source_target_pairs={{0,24},{1,97},{2,26},{3,99},{4,28},{5,101},{6,30},{7,103},{8,0},{9... | collective-permute-start | bytes 786440 | tf_op jit(solution)/shard_map/ppermute | solution.py:43
  (8 other events, 79.6 us)

commit v4 on v3

--- a/solution.py
+++ b/solution.py
@@ -153,33 +153,40 @@
     )(h_rel, *a_list, *a_list)
 
 
-def finish_kernel(where, *refs):
-    keeps, (got, hole_a, hole_b, occ, energy, res, upd) = refs[:RING], refs[RING:]
-    core = where[32]
-    mine = pl.multiple_of(core * 32, 32)
-    his = pl.multiple_of((1 - core) * 32, 32)
+def finish_kernel(*refs):
+    keeps, gots, (hole_a, hole_b, occ, energy, res, upd) = refs[:RING], refs[RING:2 * RING], refs[2 * RING:]
+    z, y, core = (lax.axis_index(name) for name in ("z", "y", "core"))
+    rows = occ.shape[1]
+    square = (rows, rows)
+    same = lax.broadcasted_iota(jnp.int32, square, 0) == lax.broadcasted_iota(jnp.int32, square, 1)
+    occ_col = jnp.sum(jnp.where(same, occ[...], 0.0), axis=1, keepdims=True)
+    low, high = occ_col[:32], occ_col[32:]
+    occ_rows = [jnp.where(core == 0, low, high), jnp.where(core == 0, high, low)]
     for i in range(16):
-        own = keeps[i // 4][i % 4 * 32:(i % 4 + 1) * 32, :256]
-        for first, part, at in ((mine, own, i), (his, got[i * 32:(i + 1) * 32], 16 + i)):
-            rows = pl.ds(first, 32)
-            cols = pl.ds(pl.multiple_of(where[at] * 256, 256), 256)
-            total = part + (hole_a[rows, cols] + hole_b[rows, cols])
-            res[rows, cols] = total
-            upd[rows, cols] = (total / (energy[:, cols] - occ[rows, :])).astype(BF)
-
-
-def finish(where, keeps, got, hole_a, hole_b, occ, energy):
+        k, j = i // 4, i % 4
+        for parts, lanes, sender in ((keeps, 0, core), (gots, 256, 1 - core)):
+            kf, ks = -RELS[k] % RING, RELS[j] % RING
+            kz, ky = jnp.where(sender == 0, ks, kf), jnp.where(sender == 0, kf, ks)
+            col = lax.rem(z + kz, RING) * RING + lax.rem(y + ky, RING)
+            at = pl.ds(pl.multiple_of(sender * 32, 32), 32)
+            cols = pl.ds(pl.multiple_of(col * 256, 256), 256)
+            total = parts[k][j * 32:(j + 1) * 32, lanes:lanes + 256] + (hole_a[at, cols] + hole_b[at, cols])
+            res[at, cols] = total
+            upd[at, cols] = (total / (energy[:, cols] - occ_rows[lanes // 256])).astype(BF)
+
+
+def finish(keeps, gots, hole_a, hole_b, occ, energy):
     shape = hole_a.shape
     vm = pl.BlockSpec(memory_space=pltpu.VMEM)
     return pl.pallas_call(
         finish_kernel,
-        in_specs=[pl.BlockSpec(memory_space=pltpu.SMEM)] + [vm] * 9,
+        in_specs=[vm] * 12,
         out_specs=[vm, vm],
         out_shape=[jax.ShapeDtypeStruct(shape, F32), jax.ShapeDtypeStruct(shape, BF)],
         compiler_params=pltpu.CompilerParams(vmem_limit_bytes=VMEM_LIMIT),
         cost_estimate=LIGHT,
         name="finish",
-    )(where, *keeps, got, hole_a, hole_b, occ, energy)
+    )(*keeps, *gots, hole_a, hole_b, occ, energy)
 
 
 def local(amplitudes, ladder_ints, hole_ints, tile_irrep, pair_orbitals, occ_energy, pair_energy):
@@ -212,43 +219,37 @@
     ints2d = ladder_ints.reshape(-1, ladder_ints.shape[2])
 
     quarter = half // 2
-    r_m = along(own, True, 1)
-    r_p = along(own, True, -1)
+    r_m = along(own, True, -1)
+    r_p = along(own, True, 1)
     w_a = select(hold((tab, own))[0], ints2d, 0)
     r_m, r_p, w_a, tab = hold((r_m, r_p, w_a, tab))
     s_a = jnp.concatenate([own, r_m, r_p[:quarter]], axis=0)
-    q_ma = along(s_a, False, 1)
-    q_pa = along(s_a, False, -1)
-    r_2a = along(r_m[:quarter], True, 1)
-    r_2b = along(r_p[quarter:], True, -1)
+    q_ma = along(s_a, False, -1)
+    q_pa = along(s_a, False, 1)
+    r_2a = along(r_m[:quarter], True, -1)
+    r_2b = along(r_p[quarter:], True, 1)
     w_b = select(tab, ints2d, 2)
     r_2a, r_2b, w_b = hold((r_2a, r_2b, w_b))
     s_b = jnp.concatenate([r_p[quarter:], r_2a, r_2b], axis=0)
-    q_mb = along(s_b, False, 1)
-    q_pb = along(s_b, False, -1)
+    q_mb = along(s_b, False, -1)
+    q_pb = along(s_b, False, 1)
     w_own = [w_a, w_b]
     w_other = [other_core(w) for w in w_own]
 
-    i = jnp.arange(33, dtype=jnp.int32)
-    kf = sum(jnp.where(i // 4 % 4 == k, jnp.int32(-RELS[k] % RING), 0) for k in range(RING))
-    ks = sum(jnp.where(i % 4 == k, jnp.int32(RELS[k] % RING), 0) for k in range(RING))
-    flip = (c + i // 16) % 2 == 0
-    kz, ky = jnp.where(flip, ks, kf), jnp.where(flip, kf, ks)
-    where = jnp.where(i == 32, c, (z + kz) % RING * RING + (y + ky) % RING)
     orbital = jnp.arange(occ_energy.shape[0], dtype=jnp.int32)
     picked = (pair_orbitals[:, :, None] == orbital[None, None, :]).astype(F32)
-    occ = jnp.sum(picked * occ_energy[None, None, :], axis=(1, 2))[:, None]
+    occ = jnp.sum(picked * occ_energy[None, None, :], axis=(1, 2))
 
     j = jnp.arange(16 * half, dtype=jnp.int32)
     ds = sum(jnp.where(j // (4 * half) == k, jnp.int32(RELS[k] % RING), 0) for k in range(RING))
-    df = sum(jnp.where(j // half % 4 == k, jnp.int32(RELS[k] % RING), 0) for k in range(RING))
+    df = sum(jnp.where(j // half % 4 == k, jnp.int32(-RELS[k] % RING), 0) for k in range(RING))
     dz, dy = jnp.where(c == 0, ds, df), jnp.where(c == 0, df, ds)
     source = ((z + dz) % RING * RING + (y + dy) % RING) * rows + c * half + j % half
     onehot = (jnp.arange(hole_ints.shape[1], dtype=jnp.int32)[:, None] == source[None, :]).astype(BF)
     h_rel = jnp.dot(hole_ints, onehot, preferred_element_type=F32).astype(BF)
 
-    q_ma, q_pa, w_other, where, occ, h_rel = hold((q_ma, q_pa, w_other, where, occ, h_rel))
-    q_2a = along(q_ma, False, 1)
+    q_ma, q_pa, w_other, occ, h_rel = hold((q_ma, q_pa, w_other, occ, h_rel))
+    q_2a = along(q_ma, False, -1)
 
     mid = 4 * TW
     block = RING * half
@@ -266,11 +267,11 @@
     keep_0, send_0 = ladder(tab, [s_a, s_b], w_own, w_other)
     got_0 = across_x(send_0, True)
     q_pb, keep_0 = hold((q_pb, keep_0))
-    q_2b = along(q_pb, False, -1)
+    q_2b = along(q_pb, False, 1)
     q_mb, got_0 = hold((q_mb, got_0))
     sum_0 = keep_0 + got_0
     end_0 = across_x(sum_0[:, mid:], False)
-    a_list = [s_a, s_b, q_ma, q_mb, q_pa, q_pb, q_2a, q_2b]
+    a_list = [s_a, s_b, q_pa, q_pb, q_ma, q_mb, q_2a, q_2b]
     keep_1, send_1 = ladder(tab, a_list[2:6], w_own, w_other)
     got_1 = across_x(coded(send_1), True)
     keep_2, send_2 = ladder(tab, a_list[6:], w_own, w_other)
@@ -296,12 +297,13 @@
     from_p, from_m, from_2 = hold((from_p, from_m, from_2))
     hole_got = other_core(hole_send)
     back = [t_0, from_m, from_p, from_2]
-    keeps = []
-    for k in range(RING):
-        u = jnp.concatenate([part[k * half:(k + 1) * half] for part in back], axis=0)
-        keeps.append(u if k == 0 else along(u, True, RELS[k]))
-    got = other_core(jnp.concatenate([u[:, mid // 2:] for u in keeps], axis=0))
-    return finish(where, keeps, got, hole_own, hole_got, occ, pair_energy[None, :])
+    keeps = [jnp.concatenate([part[m * half:(m + 1) * half] for part in back], axis=0) for m in (0, 2, 1, 3)]
+    gots = [other_core(keeps[0])]
+    keeps[1], gots[0] = hold((keeps[1], gots[0]))
+    for k in range(1, RING):
+        keeps[k] = along(keeps[k], True, RELS[k])
+        gots.append(other_core(keeps[k]))
+    return finish(keeps, gots, hole_own, hole_got, occ[None, :], pair_energy[None, :])
 
 
 def solution(mesh):

time: 103 us -> 102 us (level)
  waiting for transfers between devices: 29 us -> 35.2 us
  starting transfers between devices: 43.7 us -> 39.2 us
  Pallas kernels: 22.5 us -> 20.8 us
    ppermute x6, waiting for transfers between devices: 3.62 us -> 8.88 us  [across_x(): return lax.ppermute(value, AXES, pairs)]
    ppermute x6, starting transfers between devices: 9.77 us -> 6.8 us  [across_x(): return lax.ppermute(value, AXES, pairs)]
    ppermute x16, waiting for transfers between devices: 22.5 us -> 25.1 us  [along(): return lax.ppermute(value, AXES, perm_of(first, step))]
    ppermute x16, starting transfers between devices: 24.3 us -> 21.7 us  [along(): return lax.ppermute(value, AXES, perm_of(first, step))]
    ppermute x1, starting transfers between devices: 0.25 us -> 2.79 us  [local(): lax.ppermute(far_parts[2], 'x', [(i, (i + 2) % RING) for i in range(RING)])]
    ppermute x5 -> x8, starting transfers between devices: 9.43 us -> 7.83 us  [other_core(): return lax.ppermute(value, 'core', [(0, 1), (1, 0)])]
    ppermute x1, waiting for transfers between devices: 1.16 us -> 0.06 us  [local(): lax.ppermute(far_parts[2], 'x', [(i, (i + 2) % RING) for i in range(RING)])]
  transfers between devices with their start and end apart: 28 -> 31, of which waited for: 13 -> 14; matrix products, arithmetic and copies ran while one was open for 5% -> 4% of each run, Pallas kernels for 20% -> 19%
where the time goes in v4:
time: 102 us; the launch traced here: 101 us
  starting transfers between devices  39.2 us (38%)
  waiting for transfers between devices  35.2 us (35%)
  Pallas kernels  20.8 us (20%)
  other arithmetic  3.4 us (3%)
  local copies, waits for them, and re-layouts  1.37 us (1%)
  between operations  1.02 us (1%)
    ppermute x16, waiting for transfers between devices, along(): return lax.ppermute(value, AXES, perm_of(first, step))  25.1 us
    ppermute x16, starting transfers between devices, along(): return lax.ppermute(value, AXES, perm_of(first, step))  21.7 us
    pallas_call x2, Pallas kernels, select(): pl.pallas_call(functools.partial(select_kernel, first_block=first_block),...  9.45 us
    ppermute x6, waiting for transfers between devices, across_x(): return lax.ppermute(value, AXES, pairs)  8.88 us
    ppermute x8, starting transfers between devices, other_core(): return lax.ppermute(value, 'core', [(0, 1), (1, 0)])  7.83 us
    pallas_call x3, Pallas kernels, ladder(): pl.pallas_call(functools.partial(ladder_kernel, n=n), in_specs=[pl.BlockS...  7.02 us
    ppermute x6, starting transfers between devices, across_x(): return lax.ppermute(value, AXES, pairs)  6.8 us
    pallas_call x1, Pallas kernels, hole_part(): pl.pallas_call(hole_kernel, grid=(steps,), in_specs=[pl.BlockSpec(h_rel.s...  2.89 us
  transfers between devices with their start and end apart: 31, of which 14 were waited for; matrix products, arithmetic and copies ran while one was open for 4% of the time, Pallas kernels for 19%

profile of v4, /device:TPU:1, one launch (start us, length us, event | category | flops | bytes accessed | tf_op | source)
XLA Modules:
  0.0 101.4 jit_solution(6524756683306581294)
XLA Ops:
  6.8 2.2 %collective-permute-start.1 = (bf16[32,8192]{1,0:T(8,128)(2,1)S(1)}, bf16[32,8192]{1,0:T(8,128)(2,1)S(1)}, u32[]{:S(2)}, u32[]{:S(2)}) collective-permute-start(bf16[32,8192]{1,0:T(8,128)(2,1)S(1)} %pad_maximum_fusion.2), channel_id=1, source_target_pairs={{0,24},{1,97},{2,26},{3,99},{4,28},{5,101},{6,30},{7,103},{8,0},{9... | collective-permute-start | bytes 1572872 | tf_op jit(solution)/shard_map/ppermute | solution.py:43
  9.6 4.7 %select.123.refs_2_.refs_4_ = bf16[16,256,128]{2,1,0:T(8,128)(2,1)S(1)} custom-call(s32[256]{0:T(256)S(1)} %select_n.335.tab, bf16[32768,256]{1,0:T(8,128)(2,1)} %bitcast.8), custom_call_target="tpu_custom_call" | custom-call | flops 1024 | bytes 1024 | tf_op jit(solution)/shard_map/select/pallas_call | solution.py:88
  15.6 3.1 %collective-permute-start.3 = (bf16[16,8192]{1,0:T(8,128)(2,1)S(1)}, bf16[16,8192]{1,0:T(8,128)(2,1)S(1)}, u32[]{:S(2)}, u32[]{:S(2)}) collective-permute-start(bf16[16,8192]{1,0:T(8,128)(2,1)S(1)} %slice.95), channel_id=1, source_target_pairs={{0,24},{1,97},{2,26},{3,99},{4,28},{5,101},{6,30},{7,103},{8,0},{9... | collective-permute-start | bytes 786440 | tf_op jit(solution)/shard_map/ppermute | solution.py:43
  19.9 2.3 %collective-permute-start.6 = (bf16[80,8192]{1,0:T(8,128)(2,1)S(1)}, bf16[80,8192]{1,0:T(8,128)(2,1)S(1)}, u32[]{:S(2)}, u32[]{:S(2)}) collective-permute-start(bf16[80,8192]{1,0:T(8,128)(2,1)S(1)} %pad_maximum_fusion.refs_0_.refs_8_), channel_id=1, source_target_pairs={{0,96},{1,25},{2,98},{3,27},{4,100},{5,29},{6,102},{7,31},{8,104},... | collective-permute-start | bytes 3932168 | tf_op jit(solution)/shard_map/ppermute | solution.py:43
  22.3 4.7 %select.124.refs_3_.refs_5_ = bf16[16,256,128]{2,1,0:T(8,128)(2,1)S(1)} custom-call(s32[256]{0:T(256)S(1)} %select_n.335.tab, bf16[32768,256]{1,0:T(8,128)(2,1)} %bitcast.9), custom_call_target="tpu_custom_call" | custom-call | flops 1024 | bytes 1024 | tf_op jit(solution)/shard_map/select/pallas_call | solution.py:88
  27.1 2.2 %collective-permute-start.9 = (bf16[16,256,128]{2,1,0:T(8,128)(2,1)S(1)}, bf16[16,256,128]{2,1,0:T(8,128)(2,1)S(1)}, u32[]{:S(2)}, u32[]{:S(2)}) collective-permute-start(bf16[16,256,128]{2,1,0:T(8,128)(2,1)S(1)} %select.124.refs_3_.refs_5_), channel_id=1, source_target_pairs={{0,1},{1,0},{2,3},{3,2},{4,5},{5,4},{6,7},{7,6},{8,9},{9,8},{10,11... | collective-permute-start | bytes 3145736 | tf_op jit(solution)/shard_map/ppermute | solution.py:61
  29.4 2.0 %collective-permute-start.10 = (bf16[48,8192]{1,0:T(8,128)(2,1)S(1)}, bf16[48,8192]{1,0:T(8,128)(2,1)S(1)}, u32[]{:S(2)}, u32[]{:S(2)}) collective-permute-start(bf16[48,8192]{1,0:T(8,128)(2,1)S(1)} %pad_maximum_fusion.1.refs_1_.refs_9_), channel_id=1, source_target_pairs={{0,96},{1,25},{2,98},{3,27},{4,100},{5,29},{6,102},{7,31},{8,104},... | collective-permute-start | bytes 2359304 | tf_op jit(solution)/shard_map/ppermute | solution.py:43
  31.9 8.2 %collective-permute-done.7.refs_0_.refs_2_.refs_10_ = bf16[80,8192]{1,0:T(8,128)(2,1)S(1)} collective-permute-done((bf16[80,8192]{1,0:T(8,128)(2,1)S(1)}, bf16[80,8192]{1,0:T(8,128)(2,1)S(1)}, u32[]{:S(2)}, u32[]{:S(2)}) %collective-permute-start.7) | collective-permute-done | bytes 1310752 | tf_op jit(solution)/shard_map/ppermute | solution.py:43
  40.1 2.0 %ladder.3 = (f32[128,1024]{1,0:T(8,128)S(1)}, f32[128,1024]{1,0:T(8,128)S(1)}) custom-call(s32[256]{0:T(256)S(1)} %select_n.335.tab, bf16[80,8192]{1,0:T(8,128)(2,1)S(1)} %pad_maximum_fusion.refs_0_.refs_8_, bf16[48,8192]{1,0:T(8,128)(2,1)S(1)} %pad_maximum_fusion.1.refs_1_.refs_9_, bf16[16,256,128]{2,1,0:T(8,128)(2,1)S(1)} %select.123.refs_2_.refs_4_, ...), custom_call_target="tpu_custom_call" | custom-call | flops 1024 | bytes 1024 | tf_op jit(solution)/shard_map/ladder/pallas_call | solution.py:120
  42.1 2.7 %collective-permute-start.11 = (f32[128,1024]{1,0:T(8,128)S(1)}, f32[128,1024]{1,0:T(8,128)S(1)}, u32[]{:S(2)}, u32[]{:S(2)}) collective-permute-start(f32[128,1024]{1,0:T(8,128)S(1)} %get-tuple-element.52), channel_id=1, source_target_pairs={{0,2},{1,7},{2,0},{3,5},{4,6},{5,3},{6,4},{7,1},{8,10},{9,15},{10,... | collective-permute-start | bytes 1572872 | tf_op jit(solution)/shard_map/ppermute | solution.py:57
  44.8 3.5 %collective-permute-done.5.refs_1_.refs_3_.refs_11_ = bf16[48,8192]{1,0:T(8,128)(2,1)S(1)} collective-permute-done((bf16[48,8192]{1,0:T(8,128)(2,1)S(1)}, bf16[48,8192]{1,0:T(8,128)(2,1)S(1)}, u32[]{:S(2)}, u32[]{:S(2)}) %collective-permute-start.5) | collective-permute-done | bytes 786464 | tf_op jit(solution)/shard_map/ppermute | solution.py:43
  48.3 3.2 %collective-permute-done.11 = f32[128,1024]{1,0:T(8,128)S(1)} collective-permute-done((f32[128,1024]{1,0:T(8,128)S(1)}, f32[128,1024]{1,0:T(8,128)S(1)}, u32[]{:S(2)}, u32[]{:S(2)}) %collective-permute-start.11) | collective-permute-done | bytes 524320 | tf_op jit(solution)/shard_map/ppermute | solution.py:57
  52.2 3.1 %ladder.4 = (f32[256,1024]{1,0:T(8,128)S(1)}, f32[256,1024]{1,0:T(8,128)S(1)}) custom-call(s32[256]{0:T(256)S(1)} %select_n.335.tab, bf16[80,8192]{1,0:T(8,128)(2,1)S(1)} %collective-permute-done.7.refs_0_.refs_2_.refs_10_, bf16[48,8192]{1,0:T(8,128)(2,1)S(1)} %collective-permute-done.5.refs_1_.refs_3_.refs_11_, ...), custom_call_target="tpu_custom_call" | custom-call | flops 1024 | bytes 1024 | tf_op jit(solution)/shard_map/ladder/pallas_call | solution.py:120
  55.4 2.3 %collective-permute-start.13 = (f16[256,1024]{1,0:T(8,128)(2,1)S(1)}, f16[256,1024]{1,0:T(8,128)(2,1)S(1)}, u32[]{:S(2)}, u32[]{:S(2)}) collective-permute-start(f16[256,1024]{1,0:T(8,128)(2,1)S(1)} %multiply_convert_fusion), channel_id=1, source_target_pairs={{0,2},{1,7},{2,0},{3,5},{4,6},{5,3},{6,4},{7,1},{8,10},{9,15},{10,... | collective-permute-start | bytes 1572872 | tf_op jit(solution)/shard_map/ppermute | solution.py:57
  57.7 2.9 %collective-permute-done.15.refs_1_.refs_7_.refs_15_ = bf16[48,8192]{1,0:T(8,128)(2,1)S(1)} collective-permute-done((bf16[48,8192]{1,0:T(8,128)(2,1)S(1)}, bf16[48,8192]{1,0:T(8,128)(2,1)S(1)}, u32[]{:S(2)}, u32[]{:S(2)}) %collective-permute-start.15) | collective-permute-done | bytes 786464 | tf_op jit(solution)/shard_map/ppermute | solution.py:43
  65.8 2.8 %collective-permute-start.21 = (f16[128,512]{1,0:T(8,128)(2,1)S(1)}, f16[128,512]{1,0:T(8,128)(2,1)S(1)}, u32[]{:S(2)}, u32[]{:S(2)}) collective-permute-start(f16[128,512]{1,0:T(8,128)(2,1)S(1)} %get-tuple-element.82), channel_id=1, source_target_pairs={{0,4},{2,6},{4,0},{6,2},{1,5},{3,7},{5,1},{7,3},{8,12},{10,14},{12... | collective-permute-start | bytes 393224 | tf_op jit(solution)/shard_map/ppermute | solution.py:285
  69.1 2.9 %hole.1 = (f32[64,4096]{1,0:T(8,128)S(1)}, f32[64,4096]{1,0:T(8,128)S(1)}) custom-call(bf16[64,512]{1,0:T(8,128)(2,1)S(1)} %fusion.2.h_ref, bf16[80,8192]{1,0:T(8,128)(2,1)S(1)} %pad_maximum_fusion.refs_0_.refs_8_, bf16[48,8192]{1,0:T(8,128)(2,1)S(1)} %pad_maximum_fusion.1.refs_1_.refs_9_, ...), custom_call_target="tpu_custom_call" | custom-call | flops 68719476736 | bytes 67108864 | tf_op jit(solution)/shard_map/hole/pallas_call | solution.py:144
  72.0 4.5 %collective-permute-done.20 = f16[128,512]{1,0:T(8,128)(2,1)S(1)} collective-permute-done((f16[128,512]{1,0:T(8,128)(2,1)S(1)}, f16[128,512]{1,0:T(8,128)(2,1)S(1)}, u32[]{:S(2)}, u32[]{:S(2)}) %collective-permute-start.20) | collective-permute-done | bytes 131104 | tf_op jit(solution)/shard_map/ppermute | solution.py:57
  76.6 2.4 %collective-permute-start.22 = (f16[128,512]{1,0:T(8,128)(2,1)S(1)}, f16[128,512]{1,0:T(8,128)(2,1)S(1)}, u32[]{:S(2)}, u32[]{:S(2)}) collective-permute-start(f16[128,512]{1,0:T(8,128)(2,1)S(1)} %multiply_convert_fusion.1), channel_id=1, source_target_pairs={{0,64},{1,17},{2,66},{3,19},{4,68},{5,21},{6,70},{7,23},{8,72},{9,... | collective-permute-start | bytes 393224 | tf_op jit(solution)/shard_map/ppermute | solution.py:43
  80.8 2.7 %collective-permute-start.17 = (f16[128,512]{1,0:T(8,128)(2,1)S(1)}, f16[128,512]{1,0:T(8,128)(2,1)S(1)}, u32[]{:S(2)}, u32[]{:S(2)}) collective-permute-start(f16[128,512]{1,0:T(8,128)(2,1)S(1)} %get-tuple-element.81), channel_id=1, source_target_pairs={{0,96},{1,25},{2,98},{3,27},{4,100},{5,29},{6,102},{7,31},{8,104},... | collective-permute-start | bytes 393224 | tf_op jit(solution)/shard_map/ppermute | solution.py:43
  83.5 2.6 %collective-permute-done.18 = f16[128,512]{1,0:T(8,128)(2,1)S(1)} collective-permute-done((f16[128,512]{1,0:T(8,128)(2,1)S(1)}, f16[128,512]{1,0:T(8,128)(2,1)S(1)}, u32[]{:S(2)}, u32[]{:S(2)}) %collective-permute-start.18) | collective-permute-done | bytes 131104 | tf_op jit(solution)/shard_map/ppermute | solution.py:43
  87.6 4.0 %collective-permute-start.26 = (f32[128,512]{1,0:T(8,128)S(1)}, f32[128,512]{1,0:T(8,128)S(1)}, u32[]{:S(2)}, u32[]{:S(2)}) collective-permute-start(f32[128,512]{1,0:T(8,128)S(1)} %pad_maximum_fusion.6), channel_id=1, source_target_pairs={{0,16},{1,65},{2,18},{3,67},{4,20},{5,69},{6,22},{7,71},{8,24},{9,... | collective-permute-start | bytes 786440 | tf_op jit(solution)/shard_map/ppermute | solution.py:43
  91.7 2.7 %collective-permute-done.25.refs_2_ = f32[128,512]{1,0:T(8,128)S(1)} collective-permute-done((f32[128,512]{1,0:T(8,128)S(1)}, f32[128,512]{1,0:T(8,128)S(1)}, u32[]{:S(2)}, u32[]{:S(2)}) %collective-permute-start.25) | collective-permute-done | bytes 262176 | tf_op jit(solution)/shard_map/ppermute | solution.py:43
  94.9 3.1 %collective-permute-done.26.refs_3_ = f32[128,512]{1,0:T(8,128)S(1)} collective-permute-done((f32[128,512]{1,0:T(8,128)S(1)}, f32[128,512]{1,0:T(8,128)S(1)}, u32[]{:S(2)}, u32[]{:S(2)}) %collective-permute-start.26) | collective-permute-done | bytes 262176 | tf_op jit(solution)/shard_map/ppermute | solution.py:43
  (94 shorter events, 23.7 us)
Async XLA Ops:
  5.0 10.5 %collective-permute-start.2 = (bf16[32,8192]{1,0:T(8,128)(2,1)S(1)}, bf16[32,8192]{1,0:T(8,128)(2,1)S(1)}, u32[]{:S(2)}, u32[]{:S(2)}) collective-permute-start(bf16[32,8192]{1,0:T(8,128)(2,1)S(1)} %pad_maximum_fusion.2), channel_id=1, source_target_pairs={{0,8},{1,33},{2,10},{3,35},{4,12},{5,37},{6,14},{7,39},{8,16},{9,4... | collective-permute-start | bytes 1572872 | tf_op jit(solution)/shard_map/ppermute | solution.py:43
  6.8 8.7 %collective-permute-start.1 = (bf16[32,8192]{1,0:T(8,128)(2,1)S(1)}, bf16[32,8192]{1,0:T(8,128)(2,1)S(1)}, u32[]{:S(2)}, u32[]{:S(2)}) collective-permute-start(bf16[32,8192]{1,0:T(8,128)(2,1)S(1)} %pad_maximum_fusion.2), channel_id=1, source_target_pairs={{0,24},{1,97},{2,26},{3,99},{4,28},{5,101},{6,30},{7,103},{8,0},{9... | collective-permute-start | bytes 1572872 | tf_op jit(solution)/shard_map/ppermute | solution.py:43
  15.6 11.5 %collective-permute-start.3 = (bf16[16,8192]{1,0:T(8,128)(2,1)S(1)}, bf16[16,8192]{1,0:T(8,128)(2,1)S(1)}, u32[]{:S(2)}, u32[]{:S(2)}) collective-permute-start(bf16[16,8192]{1,0:T(8,128)(2,1)S(1)} %slice.95), channel_id=1, source_target_pairs={{0,24},{1,97},{2,26},{3,99},{4,28},{5,101},{6,30},{7,103},{8,0},{9... | collective-permute-start | bytes 786440 | tf_op jit(solution)/shard_map/ppermute | solution.py:43
  18.7 8.4 %collective-permute-start.4 = (bf16[16,8192]{1,0:T(8,128)(2,1)S(1)}, bf16[16,8192]{1,0:T(8,128)(2,1)S(1)}, u32[]{:S(2)}, u32[]{:S(2)}) collective-permute-start(bf16[16,8192]{1,0:T(8,128)(2,1)S(1)} %get-tuple-element.84), channel_id=1, source_target_pairs={{0,8},{1,33},{2,10},{3,35},{4,12},{5,37},{6,14},{7,39},{8,16},{9,4... | collective-permute-start | bytes 786440 | tf_op jit(solution)/shard_map/ppermute | solution.py:43
  18.7 12.7 %collective-permute-start.8 = (bf16[16,256,128]{2,1,0:T(8,128)(2,1)S(1)}, bf16[16,256,128]{2,1,0:T(8,128)(2,1)S(1)}, u32[]{:S(2)}, u32[]{:S(2)}) collective-permute-start(bf16[16,256,128]{2,1,0:T(8,128)(2,1)S(1)} %select.123.refs_2_.refs_4_), channel_id=1, source_target_pairs={{0,1},{1,0},{2,3},{3,2},{4,5},{5,4},{6,7},{7,6},{8,9},{9,8},{10,11... | collective-permute-start | bytes 3145736 | tf_op jit(solution)/shard_map/ppermute | solution.py:61
  19.0 21.1 %collective-permute-start.7 = (bf16[80,8192]{1,0:T(8,128)(2,1)S(1)}, bf16[80,8192]{1,0:T(8,128)(2,1)S(1)}, u32[]{:S(2)}, u32[]{:S(2)}) collective-permute-start(bf16[80,8192]{1,0:T(8,128)(2,1)S(1)} %pad_maximum_fusion.refs_0_.refs_8_), channel_id=1, source_target_pairs={{0,32},{1,9},{2,34},{3,11},{4,36},{5,13},{6,38},{7,15},{8,40},{9,1... | collective-permute-start | bytes 3932168 | tf_op jit(solution)/shard_map/ppermute | solution.py:43
  19.9 20.3 %collective-permute-start.6 = (bf16[80,8192]{1,0:T(8,128)(2,1)S(1)}, bf16[80,8192]{1,0:T(8,128)(2,1)S(1)}, u32[]{:S(2)}, u32[]{:S(2)}) collective-permute-start(bf16[80,8192]{1,0:T(8,128)(2,1)S(1)} %pad_maximum_fusion.refs_0_.refs_8_), channel_id=1, source_target_pairs={{0,96},{1,25},{2,98},{3,27},{4,100},{5,29},{6,102},{7,31},{8,104},... | collective-permute-start | bytes 3932168 | tf_op jit(solution)/shard_map/ppermute | solution.py:43
  29.4 18.9 %collective-permute-start.10 = (bf16[48,8192]{1,0:T(8,128)(2,1)S(1)}, bf16[48,8192]{1,0:T(8,128)(2,1)S(1)}, u32[]{:S(2)}, u32[]{:S(2)}) collective-permute-start(bf16[48,8192]{1,0:T(8,128)(2,1)S(1)} %pad_maximum_fusion.1.refs_1_.refs_9_), channel_id=1, source_target_pairs={{0,96},{1,25},{2,98},{3,27},{4,100},{5,29},{6,102},{7,31},{8,104},... | collective-permute-start | bytes 2359304 | tf_op jit(solution)/shard_map/ppermute | solution.py:43
  31.4 16.9 %collective-permute-start.5 = (bf16[48,8192]{1,0:T(8,128)(2,1)S(1)}, bf16[48,8192]{1,0:T(8,128)(2,1)S(1)}, u32[]{:S(2)}, u32[]{:S(2)}) collective-permute-start(bf16[48,8192]{1,0:T(8,128)(2,1)S(1)} %pad_maximum_fusion.1.refs_1_.refs_9_), channel_id=1, source_target_pairs={{0,32},{1,9},{2,34},{3,11},{4,36},{5,13},{6,38},{7,15},{8,40},{9,1... | collective-permute-start | bytes 2359304 | tf_op jit(solution)/shard_map/ppermute | solution.py:43
  42.1 9.3 %collective-permute-start.11 = (f32[128,1024]{1,0:T(8,128)S(1)}, f32[128,1024]{1,0:T(8,128)S(1)}, u32[]{:S(2)}, u32[]{:S(2)}) collective-permute-start(f32[128,1024]{1,0:T(8,128)S(1)} %get-tuple-element.52), channel_id=1, source_target_pairs={{0,2},{1,7},{2,0},{3,5},{4,6},{5,3},{6,4},{7,1},{8,10},{9,15},{10,... | collective-permute-start | bytes 1572872 | tf_op jit(solution)/shard_map/ppermute | solution.py:57
  44.8 16.8 %collective-permute-start.14 = (bf16[80,8192]{1,0:T(8,128)(2,1)S(1)}, bf16[80,8192]{1,0:T(8,128)(2,1)S(1)}, u32[]{:S(2)}, u32[]{:S(2)}) collective-permute-start(bf16[80,8192]{1,0:T(8,128)(2,1)S(1)} %collective-permute-done.6.refs_2_.refs_4_.refs_12_), channel_id=1, source_target_pairs={{0,96},{1,25},{2,98},{3,27},{4,100},{5,29},{6,102},{7,31},{8,104},... | collective-permute-start | bytes 3932168 | tf_op jit(solution)/shard_map/ppermute | solution.py:43
  48.3 12.3 %collective-permute-start.15 = (bf16[48,8192]{1,0:T(8,128)(2,1)S(1)}, bf16[48,8192]{1,0:T(8,128)(2,1)S(1)}, u32[]{:S(2)}, u32[]{:S(2)}) collective-permute-start(bf16[48,8192]{1,0:T(8,128)(2,1)S(1)} %collective-permute-done.5.refs_1_.refs_3_.refs_11_), channel_id=1, source_target_pairs={{0,32},{1,9},{2,34},{3,11},{4,36},{5,13},{6,38},{7,15},{8,40},{9,1... | collective-permute-start | bytes 2359304 | tf_op jit(solution)/shard_map/ppermute | solution.py:43
  51.5 6.1 %collective-permute-start.12 = (f32[128,512]{1,0:T(8,128)S(1)}, f32[128,512]{1,0:T(8,128)S(1)}, u32[]{:S(2)}, u32[]{:S(2)}) collective-permute-start(f32[128,512]{1,0:T(8,128)S(1)} %slice.125), channel_id=1, source_target_pairs={{0,6},{1,3},{2,4},{3,1},{4,2},{5,7},{6,0},{7,5},{8,14},{9,11},{10,... | collective-permute-start | bytes 786440 | tf_op jit(solution)/shard_map/ppermute | solution.py:57
  55.4 9.3 %collective-permute-start.13 = (f16[256,1024]{1,0:T(8,128)(2,1)S(1)}, f16[256,1024]{1,0:T(8,128)(2,1)S(1)}, u32[]{:S(2)}, u32[]{:S(2)}) collective-permute-start(f16[256,1024]{1,0:T(8,128)(2,1)S(1)} %multiply_convert_fusion), channel_id=1, source_target_pairs={{0,2},{1,7},{2,0},{3,5},{4,6},{5,3},{6,4},{7,1},{8,10},{9,15},{10,... | collective-permute-start | bytes 1572872 | tf_op jit(solution)/shard_map/ppermute | solution.py:57
  64.7 7.3 %collective-permute-start.19 = (f16[128,512]{1,0:T(8,128)(2,1)S(1)}, f16[128,512]{1,0:T(8,128)(2,1)S(1)}, u32[]{:S(2)}, u32[]{:S(2)}) collective-permute-start(f16[128,512]{1,0:T(8,128)(2,1)S(1)} %multiply_convert_fusion.4), channel_id=1, source_target_pairs={{0,6},{1,3},{2,4},{3,1},{4,2},{5,7},{6,0},{7,5},{8,14},{9,11},{10,... | collective-permute-start | bytes 393224 | tf_op jit(solution)/shard_map/ppermute | solution.py:57
  65.8 6.2 %collective-permute-start.21 = (f16[128,512]{1,0:T(8,128)(2,1)S(1)}, f16[128,512]{1,0:T(8,128)(2,1)S(1)}, u32[]{:S(2)}, u32[]{:S(2)}) collective-permute-start(f16[128,512]{1,0:T(8,128)(2,1)S(1)} %get-tuple-element.82), channel_id=1, source_target_pairs={{0,4},{2,6},{4,0},{6,2},{1,5},{3,7},{5,1},{7,3},{8,12},{10,14},{12... | collective-permute-start | bytes 393224 | tf_op jit(solution)/shard_map/ppermute | solution.py:285
  68.6 8.0 %collective-permute-start.20 = (f16[128,512]{1,0:T(8,128)(2,1)S(1)}, f16[128,512]{1,0:T(8,128)(2,1)S(1)}, u32[]{:S(2)}, u32[]{:S(2)}) collective-permute-start(f16[128,512]{1,0:T(8,128)(2,1)S(1)} %get-tuple-element.83), channel_id=1, source_target_pairs={{0,2},{1,7},{2,0},{3,5},{4,6},{5,3},{6,4},{7,1},{8,10},{9,15},{10,... | collective-permute-start | bytes 393224 | tf_op jit(solution)/shard_map/ppermute | solution.py:57
  69.1 11.6 %collective-permute-start.16 = (f16[256,512]{1,0:T(8,128)(2,1)S(1)}, f16[256,512]{1,0:T(8,128)(2,1)S(1)}, u32[]{:S(2)}, u32[]{:S(2)}) collective-permute-start(f16[256,512]{1,0:T(8,128)(2,1)S(1)} %fusion.4), channel_id=1, source_target_pairs={{0,6},{1,3},{2,4},{3,1},{4,2},{5,7},{6,0},{7,5},{8,14},{9,11},{10,... | collective-permute-start | bytes 786440 | tf_op jit(solution)/shard_map/ppermute | solution.py:57
  76.6 6.8 %collective-permute-start.22 = (f16[128,512]{1,0:T(8,128)(2,1)S(1)}, f16[128,512]{1,0:T(8,128)(2,1)S(1)}, u32[]{:S(2)}, u32[]{:S(2)}) collective-permute-start(f16[128,512]{1,0:T(8,128)(2,1)S(1)} %multiply_convert_fusion.1), channel_id=1, source_target_pairs={{0,64},{1,17},{2,66},{3,19},{4,68},{5,21},{6,70},{7,23},{8,72},{9,... | collective-permute-start | bytes 393224 | tf_op jit(solution)/shard_map/ppermute | solution.py:43
  79.1 20.5 %collective-permute-start.30 = (f32[64,4096]{1,0:T(8,128)S(1)}, f32[64,4096]{1,0:T(8,128)S(1)}, u32[]{:S(2)}, u32[]{:S(2)}) collective-permute-start(f32[64,4096]{1,0:T(8,128)S(1)} %get-tuple-element.76), channel_id=1, source_target_pairs={{0,1},{1,0},{2,3},{3,2},{4,5},{5,4},{6,7},{7,6},{8,9},{9,8},{10,11... | collective-permute-start | bytes 3145736 | tf_op jit(solution)/shard_map/ppermute | solution.py:61
  80.7 5.4 %collective-permute-start.18 = (f16[128,512]{1,0:T(8,128)(2,1)S(1)}, f16[128,512]{1,0:T(8,128)(2,1)S(1)}, u32[]{:S(2)}, u32[]{:S(2)}) collective-permute-start(f16[128,512]{1,0:T(8,128)(2,1)S(1)} %get-tuple-element.80), channel_id=1, source_target_pairs={{0,32},{1,9},{2,34},{3,11},{4,36},{5,13},{6,38},{7,15},{8,40},{9,1... | collective-permute-start | bytes 393224 | tf_op jit(solution)/shard_map/ppermute | solution.py:43
  87.3 7.0 %collective-permute-start.25 = (f32[128,512]{1,0:T(8,128)S(1)}, f32[128,512]{1,0:T(8,128)S(1)}, u32[]{:S(2)}, u32[]{:S(2)}) collective-permute-start(f32[128,512]{1,0:T(8,128)S(1)} %pad_maximum_fusion.5), channel_id=1, source_target_pairs={{0,8},{1,33},{2,10},{3,35},{4,12},{5,37},{6,14},{7,39},{8,16},{9,4... | collective-permute-start | bytes 786440 | tf_op jit(solution)/shard_map/ppermute | solution.py:43
  87.6 10.4 %collective-permute-start.26 = (f32[128,512]{1,0:T(8,128)S(1)}, f32[128,512]{1,0:T(8,128)S(1)}, u32[]{:S(2)}, u32[]{:S(2)}) collective-permute-start(f32[128,512]{1,0:T(8,128)S(1)} %pad_maximum_fusion.6), channel_id=1, source_target_pairs={{0,16},{1,65},{2,18},{3,67},{4,20},{5,69},{6,22},{7,71},{8,24},{9,... | collective-permute-start | bytes 786440 | tf_op jit(solution)/shard_map/ppermute | solution.py:43
  91.6 6.7 %collective-permute-start.24 = (f32[128,512]{1,0:T(8,128)S(1)}, f32[128,512]{1,0:T(8,128)S(1)}, u32[]{:S(2)}, u32[]{:S(2)}) collective-permute-start(f32[128,512]{1,0:T(8,128)S(1)} %pad_maximum_fusion.4), channel_id=1, source_target_pairs={{0,24},{1,97},{2,26},{3,99},{4,28},{5,101},{6,30},{7,103},{8,0},{9... | collective-permute-start | bytes 786440 | tf_op jit(solution)/shard_map/ppermute | solution.py:43
  (11 other events, 83.9 us)

commit v5 on v4

--- a/solution.py
+++ b/solution.py
@@ -14,7 +14,7 @@
 BF = jnp.bfloat16
 F32 = jnp.float32
 VMEM_LIMIT = 24 * 1024 * 1024
-SCALE = 64.0
+SCALE = 16.0
 F16 = jnp.float16
 HEAVY = pl.CostEstimate(flops=2**36, bytes_accessed=2**26, transcendentals=0)
 LIGHT = pl.CostEstimate(flops=1024, bytes_accessed=1024, transcendentals=0)

time: 102 us -> 102 us (level)
  no operation moved by 1% of the time
where the time goes in v5:
time: 102 us; the launch traced here: 101 us
  starting transfers between devices  39.1 us (38%)
  waiting for transfers between devices  35.2 us (35%)
  Pallas kernels  20.8 us (20%)
  other arithmetic  3.4 us (3%)
  local copies, waits for them, and re-layouts  1.37 us (1%)
  between operations  1.02 us (1%)
    ppermute x16, waiting for transfers between devices, along(): return lax.ppermute(value, AXES, perm_of(first, step))  25 us
    ppermute x16, starting transfers between devices, along(): return lax.ppermute(value, AXES, perm_of(first, step))  21.7 us
    pallas_call x2, Pallas kernels, select(): pl.pallas_call(functools.partial(select_kernel, first_block=first_block),...  9.45 us
    ppermute x6, waiting for transfers between devices, across_x(): return lax.ppermute(value, AXES, pairs)  8.87 us
    ppermute x8, starting transfers between devices, other_core(): return lax.ppermute(value, 'core', [(0, 1), (1, 0)])  7.79 us
    pallas_call x3, Pallas kernels, ladder(): pl.pallas_call(functools.partial(ladder_kernel, n=n), in_specs=[pl.BlockS...  7.04 us
    ppermute x6, starting transfers between devices, across_x(): return lax.ppermute(value, AXES, pairs)  6.81 us
    pallas_call x1, Pallas kernels, hole_part(): pl.pallas_call(hole_kernel, grid=(steps,), in_specs=[pl.BlockSpec(h_rel.s...  2.89 us
  transfers between devices with their start and end apart: 31, of which 14 were waited for; matrix products, arithmetic and copies ran while one was open for 4% of the time, Pallas kernels for 19%

profile of v5, /device:TPU:1, one launch (start us, length us, event | category | flops | bytes accessed | tf_op | source)
XLA Modules:
  0.0 101.3 jit_solution(12812381094418936496)
XLA Ops:
  6.8 2.2 %collective-permute-start.1 = (bf16[32,8192]{1,0:T(8,128)(2,1)S(1)}, bf16[32,8192]{1,0:T(8,128)(2,1)S(1)}, u32[]{:S(2)}, u32[]{:S(2)}) collective-permute-start(bf16[32,8192]{1,0:T(8,128)(2,1)S(1)} %pad_maximum_fusion.2), channel_id=1, source_target_pairs={{0,24},{1,97},{2,26},{3,99},{4,28},{5,101},{6,30},{7,103},{8,0},{9... | collective-permute-start | bytes 1572872 | tf_op jit(solution)/shard_map/ppermute | solution.py:43
  9.6 4.7 %select.123.refs_2_.refs_4_ = bf16[16,256,128]{2,1,0:T(8,128)(2,1)S(1)} custom-call(s32[256]{0:T(256)S(1)} %select_n.335.tab, bf16[32768,256]{1,0:T(8,128)(2,1)} %bitcast.8), custom_call_target="tpu_custom_call" | custom-call | flops 1024 | bytes 1024 | tf_op jit(solution)/shard_map/select/pallas_call | solution.py:88
  15.6 3.1 %collective-permute-start.3 = (bf16[16,8192]{1,0:T(8,128)(2,1)S(1)}, bf16[16,8192]{1,0:T(8,128)(2,1)S(1)}, u32[]{:S(2)}, u32[]{:S(2)}) collective-permute-start(bf16[16,8192]{1,0:T(8,128)(2,1)S(1)} %slice.95), channel_id=1, source_target_pairs={{0,24},{1,97},{2,26},{3,99},{4,28},{5,101},{6,30},{7,103},{8,0},{9... | collective-permute-start | bytes 786440 | tf_op jit(solution)/shard_map/ppermute | solution.py:43
  19.9 2.3 %collective-permute-start.6 = (bf16[80,8192]{1,0:T(8,128)(2,1)S(1)}, bf16[80,8192]{1,0:T(8,128)(2,1)S(1)}, u32[]{:S(2)}, u32[]{:S(2)}) collective-permute-start(bf16[80,8192]{1,0:T(8,128)(2,1)S(1)} %pad_maximum_fusion.refs_0_.refs_8_), channel_id=1, source_target_pairs={{0,96},{1,25},{2,98},{3,27},{4,100},{5,29},{6,102},{7,31},{8,104},... | collective-permute-start | bytes 3932168 | tf_op jit(solution)/shard_map/ppermute | solution.py:43
  22.3 4.7 %select.124.refs_3_.refs_5_ = bf16[16,256,128]{2,1,0:T(8,128)(2,1)S(1)} custom-call(s32[256]{0:T(256)S(1)} %select_n.335.tab, bf16[32768,256]{1,0:T(8,128)(2,1)} %bitcast.9), custom_call_target="tpu_custom_call" | custom-call | flops 1024 | bytes 1024 | tf_op jit(solution)/shard_map/select/pallas_call | solution.py:88
  27.1 2.2 %collective-permute-start.9 = (bf16[16,256,128]{2,1,0:T(8,128)(2,1)S(1)}, bf16[16,256,128]{2,1,0:T(8,128)(2,1)S(1)}, u32[]{:S(2)}, u32[]{:S(2)}) collective-permute-start(bf16[16,256,128]{2,1,0:T(8,128)(2,1)S(1)} %select.124.refs_3_.refs_5_), channel_id=1, source_target_pairs={{0,1},{1,0},{2,3},{3,2},{4,5},{5,4},{6,7},{7,6},{8,9},{9,8},{10,11... | collective-permute-start | bytes 3145736 | tf_op jit(solution)/shard_map/ppermute | solution.py:61
  29.4 2.0 %collective-permute-start.10 = (bf16[48,8192]{1,0:T(8,128)(2,1)S(1)}, bf16[48,8192]{1,0:T(8,128)(2,1)S(1)}, u32[]{:S(2)}, u32[]{:S(2)}) collective-permute-start(bf16[48,8192]{1,0:T(8,128)(2,1)S(1)} %pad_maximum_fusion.1.refs_1_.refs_9_), channel_id=1, source_target_pairs={{0,96},{1,25},{2,98},{3,27},{4,100},{5,29},{6,102},{7,31},{8,104},... | collective-permute-start | bytes 2359304 | tf_op jit(solution)/shard_map/ppermute | solution.py:43
  31.9 8.2 %collective-permute-done.7.refs_0_.refs_2_.refs_10_ = bf16[80,8192]{1,0:T(8,128)(2,1)S(1)} collective-permute-done((bf16[80,8192]{1,0:T(8,128)(2,1)S(1)}, bf16[80,8192]{1,0:T(8,128)(2,1)S(1)}, u32[]{:S(2)}, u32[]{:S(2)}) %collective-permute-start.7) | collective-permute-done | bytes 1310752 | tf_op jit(solution)/shard_map/ppermute | solution.py:43
  40.1 2.0 %ladder.3 = (f32[128,1024]{1,0:T(8,128)S(1)}, f32[128,1024]{1,0:T(8,128)S(1)}) custom-call(s32[256]{0:T(256)S(1)} %select_n.335.tab, bf16[80,8192]{1,0:T(8,128)(2,1)S(1)} %pad_maximum_fusion.refs_0_.refs_8_, bf16[48,8192]{1,0:T(8,128)(2,1)S(1)} %pad_maximum_fusion.1.refs_1_.refs_9_, bf16[16,256,128]{2,1,0:T(8,128)(2,1)S(1)} %select.123.refs_2_.refs_4_, ...), custom_call_target="tpu_custom_call" | custom-call | flops 1024 | bytes 1024 | tf_op jit(solution)/shard_map/ladder/pallas_call | solution.py:120
  42.1 2.6 %collective-permute-start.11 = (f32[128,1024]{1,0:T(8,128)S(1)}, f32[128,1024]{1,0:T(8,128)S(1)}, u32[]{:S(2)}, u32[]{:S(2)}) collective-permute-start(f32[128,1024]{1,0:T(8,128)S(1)} %get-tuple-element.52), channel_id=1, source_target_pairs={{0,2},{1,7},{2,0},{3,5},{4,6},{5,3},{6,4},{7,1},{8,10},{9,15},{10,... | collective-permute-start | bytes 1572872 | tf_op jit(solution)/shard_map/ppermute | solution.py:57
  44.8 3.5 %collective-permute-done.5.refs_1_.refs_3_.refs_11_ = bf16[48,8192]{1,0:T(8,128)(2,1)S(1)} collective-permute-done((bf16[48,8192]{1,0:T(8,128)(2,1)S(1)}, bf16[48,8192]{1,0:T(8,128)(2,1)S(1)}, u32[]{:S(2)}, u32[]{:S(2)}) %collective-permute-start.5) | collective-permute-done | bytes 786464 | tf_op jit(solution)/shard_map/ppermute | solution.py:43
  48.3 3.2 %collective-permute-done.11 = f32[128,1024]{1,0:T(8,128)S(1)} collective-permute-done((f32[128,1024]{1,0:T(8,128)S(1)}, f32[128,1024]{1,0:T(8,128)S(1)}, u32[]{:S(2)}, u32[]{:S(2)}) %collective-permute-start.11) | collective-permute-done | bytes 524320 | tf_op jit(solution)/shard_map/ppermute | solution.py:57
  52.2 3.1 %ladder.4 = (f32[256,1024]{1,0:T(8,128)S(1)}, f32[256,1024]{1,0:T(8,128)S(1)}) custom-call(s32[256]{0:T(256)S(1)} %select_n.335.tab, bf16[80,8192]{1,0:T(8,128)(2,1)S(1)} %collective-permute-done.7.refs_0_.refs_2_.refs_10_, bf16[48,8192]{1,0:T(8,128)(2,1)S(1)} %collective-permute-done.5.refs_1_.refs_3_.refs_11_, ...), custom_call_target="tpu_custom_call" | custom-call | flops 1024 | bytes 1024 | tf_op jit(solution)/shard_map/ladder/pallas_call | solution.py:120
  55.4 2.3 %collective-permute-start.13 = (f16[256,1024]{1,0:T(8,128)(2,1)S(1)}, f16[256,1024]{1,0:T(8,128)(2,1)S(1)}, u32[]{:S(2)}, u32[]{:S(2)}) collective-permute-start(f16[256,1024]{1,0:T(8,128)(2,1)S(1)} %multiply_convert_fusion), channel_id=1, source_target_pairs={{0,2},{1,7},{2,0},{3,5},{4,6},{5,3},{6,4},{7,1},{8,10},{9,15},{10,... | collective-permute-start | bytes 1572872 | tf_op jit(solution)/shard_map/ppermute | solution.py:57
  57.7 2.9 %collective-permute-done.15.refs_1_.refs_7_.refs_15_ = bf16[48,8192]{1,0:T(8,128)(2,1)S(1)} collective-permute-done((bf16[48,8192]{1,0:T(8,128)(2,1)S(1)}, bf16[48,8192]{1,0:T(8,128)(2,1)S(1)}, u32[]{:S(2)}, u32[]{:S(2)}) %collective-permute-start.15) | collective-permute-done | bytes 786464 | tf_op jit(solution)/shard_map/ppermute | solution.py:43
  65.8 2.8 %collective-permute-start.21 = (f16[128,512]{1,0:T(8,128)(2,1)S(1)}, f16[128,512]{1,0:T(8,128)(2,1)S(1)}, u32[]{:S(2)}, u32[]{:S(2)}) collective-permute-start(f16[128,512]{1,0:T(8,128)(2,1)S(1)} %get-tuple-element.82), channel_id=1, source_target_pairs={{0,4},{2,6},{4,0},{6,2},{1,5},{3,7},{5,1},{7,3},{8,12},{10,14},{12... | collective-permute-start | bytes 393224 | tf_op jit(solution)/shard_map/ppermute | solution.py:285
  69.1 2.9 %hole.1 = (f32[64,4096]{1,0:T(8,128)S(1)}, f32[64,4096]{1,0:T(8,128)S(1)}) custom-call(bf16[64,512]{1,0:T(8,128)(2,1)S(1)} %fusion.2.h_ref, bf16[80,8192]{1,0:T(8,128)(2,1)S(1)} %pad_maximum_fusion.refs_0_.refs_8_, bf16[48,8192]{1,0:T(8,128)(2,1)S(1)} %pad_maximum_fusion.1.refs_1_.refs_9_, ...), custom_call_target="tpu_custom_call" | custom-call | flops 68719476736 | bytes 67108864 | tf_op jit(solution)/shard_map/hole/pallas_call | solution.py:144
  72.0 4.5 %collective-permute-done.20 = f16[128,512]{1,0:T(8,128)(2,1)S(1)} collective-permute-done((f16[128,512]{1,0:T(8,128)(2,1)S(1)}, f16[128,512]{1,0:T(8,128)(2,1)S(1)}, u32[]{:S(2)}, u32[]{:S(2)}) %collective-permute-start.20) | collective-permute-done | bytes 131104 | tf_op jit(solution)/shard_map/ppermute | solution.py:57
  76.7 2.4 %collective-permute-start.22 = (f16[128,512]{1,0:T(8,128)(2,1)S(1)}, f16[128,512]{1,0:T(8,128)(2,1)S(1)}, u32[]{:S(2)}, u32[]{:S(2)}) collective-permute-start(f16[128,512]{1,0:T(8,128)(2,1)S(1)} %multiply_convert_fusion.1), channel_id=1, source_target_pairs={{0,64},{1,17},{2,66},{3,19},{4,68},{5,21},{6,70},{7,23},{8,72},{9,... | collective-permute-start | bytes 393224 | tf_op jit(solution)/shard_map/ppermute | solution.py:43
  80.8 2.7 %collective-permute-start.17 = (f16[128,512]{1,0:T(8,128)(2,1)S(1)}, f16[128,512]{1,0:T(8,128)(2,1)S(1)}, u32[]{:S(2)}, u32[]{:S(2)}) collective-permute-start(f16[128,512]{1,0:T(8,128)(2,1)S(1)} %get-tuple-element.81), channel_id=1, source_target_pairs={{0,96},{1,25},{2,98},{3,27},{4,100},{5,29},{6,102},{7,31},{8,104},... | collective-permute-start | bytes 393224 | tf_op jit(solution)/shard_map/ppermute | solution.py:43
  83.5 2.6 %collective-permute-done.18 = f16[128,512]{1,0:T(8,128)(2,1)S(1)} collective-permute-done((f16[128,512]{1,0:T(8,128)(2,1)S(1)}, f16[128,512]{1,0:T(8,128)(2,1)S(1)}, u32[]{:S(2)}, u32[]{:S(2)}) %collective-permute-start.18) | collective-permute-done | bytes 131104 | tf_op jit(solution)/shard_map/ppermute | solution.py:43
  87.6 3.9 %collective-permute-start.26 = (f32[128,512]{1,0:T(8,128)S(1)}, f32[128,512]{1,0:T(8,128)S(1)}, u32[]{:S(2)}, u32[]{:S(2)}) collective-permute-start(f32[128,512]{1,0:T(8,128)S(1)} %pad_maximum_fusion.6), channel_id=1, source_target_pairs={{0,16},{1,65},{2,18},{3,67},{4,20},{5,69},{6,22},{7,71},{8,24},{9,... | collective-permute-start | bytes 786440 | tf_op jit(solution)/shard_map/ppermute | solution.py:43
  91.6 2.7 %collective-permute-done.25.refs_2_ = f32[128,512]{1,0:T(8,128)S(1)} collective-permute-done((f32[128,512]{1,0:T(8,128)S(1)}, f32[128,512]{1,0:T(8,128)S(1)}, u32[]{:S(2)}, u32[]{:S(2)}) %collective-permute-start.25) | collective-permute-done | bytes 262176 | tf_op jit(solution)/shard_map/ppermute | solution.py:43
  94.9 3.1 %collective-permute-done.26.refs_3_ = f32[128,512]{1,0:T(8,128)S(1)} collective-permute-done((f32[128,512]{1,0:T(8,128)S(1)}, f32[128,512]{1,0:T(8,128)S(1)}, u32[]{:S(2)}, u32[]{:S(2)}) %collective-permute-start.26) | collective-permute-done | bytes 262176 | tf_op jit(solution)/shard_map/ppermute | solution.py:43
  (94 shorter events, 23.7 us)
Async XLA Ops:
  5.0 10.5 %collective-permute-start.2 = (bf16[32,8192]{1,0:T(8,128)(2,1)S(1)}, bf16[32,8192]{1,0:T(8,128)(2,1)S(1)}, u32[]{:S(2)}, u32[]{:S(2)}) collective-permute-start(bf16[32,8192]{1,0:T(8,128)(2,1)S(1)} %pad_maximum_fusion.2), channel_id=1, source_target_pairs={{0,8},{1,33},{2,10},{3,35},{4,12},{5,37},{6,14},{7,39},{8,16},{9,4... | collective-permute-start | bytes 1572872 | tf_op jit(solution)/shard_map/ppermute | solution.py:43
  6.8 8.7 %collective-permute-start.1 = (bf16[32,8192]{1,0:T(8,128)(2,1)S(1)}, bf16[32,8192]{1,0:T(8,128)(2,1)S(1)}, u32[]{:S(2)}, u32[]{:S(2)}) collective-permute-start(bf16[32,8192]{1,0:T(8,128)(2,1)S(1)} %pad_maximum_fusion.2), channel_id=1, source_target_pairs={{0,24},{1,97},{2,26},{3,99},{4,28},{5,101},{6,30},{7,103},{8,0},{9... | collective-permute-start | bytes 1572872 | tf_op jit(solution)/shard_map/ppermute | solution.py:43
  15.6 11.5 %collective-permute-start.3 = (bf16[16,8192]{1,0:T(8,128)(2,1)S(1)}, bf16[16,8192]{1,0:T(8,128)(2,1)S(1)}, u32[]{:S(2)}, u32[]{:S(2)}) collective-permute-start(bf16[16,8192]{1,0:T(8,128)(2,1)S(1)} %slice.95), channel_id=1, source_target_pairs={{0,24},{1,97},{2,26},{3,99},{4,28},{5,101},{6,30},{7,103},{8,0},{9... | collective-permute-start | bytes 786440 | tf_op jit(solution)/shard_map/ppermute | solution.py:43
  18.7 8.4 %collective-permute-start.4 = (bf16[16,8192]{1,0:T(8,128)(2,1)S(1)}, bf16[16,8192]{1,0:T(8,128)(2,1)S(1)}, u32[]{:S(2)}, u32[]{:S(2)}) collective-permute-start(bf16[16,8192]{1,0:T(8,128)(2,1)S(1)} %get-tuple-element.84), channel_id=1, source_target_pairs={{0,8},{1,33},{2,10},{3,35},{4,12},{5,37},{6,14},{7,39},{8,16},{9,4... | collective-permute-start | bytes 786440 | tf_op jit(solution)/shard_map/ppermute | solution.py:43
  18.7 12.7 %collective-permute-start.8 = (bf16[16,256,128]{2,1,0:T(8,128)(2,1)S(1)}, bf16[16,256,128]{2,1,0:T(8,128)(2,1)S(1)}, u32[]{:S(2)}, u32[]{:S(2)}) collective-permute-start(bf16[16,256,128]{2,1,0:T(8,128)(2,1)S(1)} %select.123.refs_2_.refs_4_), channel_id=1, source_target_pairs={{0,1},{1,0},{2,3},{3,2},{4,5},{5,4},{6,7},{7,6},{8,9},{9,8},{10,11... | collective-permute-start | bytes 3145736 | tf_op jit(solution)/shard_map/ppermute | solution.py:61
  19.0 21.1 %collective-permute-start.7 = (bf16[80,8192]{1,0:T(8,128)(2,1)S(1)}, bf16[80,8192]{1,0:T(8,128)(2,1)S(1)}, u32[]{:S(2)}, u32[]{:S(2)}) collective-permute-start(bf16[80,8192]{1,0:T(8,128)(2,1)S(1)} %pad_maximum_fusion.refs_0_.refs_8_), channel_id=1, source_target_pairs={{0,32},{1,9},{2,34},{3,11},{4,36},{5,13},{6,38},{7,15},{8,40},{9,1... | collective-permute-start | bytes 3932168 | tf_op jit(solution)/shard_map/ppermute | solution.py:43
  19.9 20.3 %collective-permute-start.6 = (bf16[80,8192]{1,0:T(8,128)(2,1)S(1)}, bf16[80,8192]{1,0:T(8,128)(2,1)S(1)}, u32[]{:S(2)}, u32[]{:S(2)}) collective-permute-start(bf16[80,8192]{1,0:T(8,128)(2,1)S(1)} %pad_maximum_fusion.refs_0_.refs_8_), channel_id=1, source_target_pairs={{0,96},{1,25},{2,98},{3,27},{4,100},{5,29},{6,102},{7,31},{8,104},... | collective-permute-start | bytes 3932168 | tf_op jit(solution)/shard_map/ppermute | solution.py:43
  29.4 18.9 %collective-permute-start.10 = (bf16[48,8192]{1,0:T(8,128)(2,1)S(1)}, bf16[48,8192]{1,0:T(8,128)(2,1)S(1)}, u32[]{:S(2)}, u32[]{:S(2)}) collective-permute-start(bf16[48,8192]{1,0:T(8,128)(2,1)S(1)} %pad_maximum_fusion.1.refs_1_.refs_9_), channel_id=1, source_target_pairs={{0,96},{1,25},{2,98},{3,27},{4,100},{5,29},{6,102},{7,31},{8,104},... | collective-permute-start | bytes 2359304 | tf_op jit(solution)/shard_map/ppermute | solution.py:43
  31.4 16.9 %collective-permute-start.5 = (bf16[48,8192]{1,0:T(8,128)(2,1)S(1)}, bf16[48,8192]{1,0:T(8,128)(2,1)S(1)}, u32[]{:S(2)}, u32[]{:S(2)}) collective-permute-start(bf16[48,8192]{1,0:T(8,128)(2,1)S(1)} %pad_maximum_fusion.1.refs_1_.refs_9_), channel_id=1, source_target_pairs={{0,32},{1,9},{2,34},{3,11},{4,36},{5,13},{6,38},{7,15},{8,40},{9,1... | collective-permute-start | bytes 2359304 | tf_op jit(solution)/shard_map/ppermute | solution.py:43
  42.1 9.3 %collective-permute-start.11 = (f32[128,1024]{1,0:T(8,128)S(1)}, f32[128,1024]{1,0:T(8,128)S(1)}, u32[]{:S(2)}, u32[]{:S(2)}) collective-permute-start(f32[128,1024]{1,0:T(8,128)S(1)} %get-tuple-element.52), channel_id=1, source_target_pairs={{0,2},{1,7},{2,0},{3,5},{4,6},{5,3},{6,4},{7,1},{8,10},{9,15},{10,... | collective-permute-start | bytes 1572872 | tf_op jit(solution)/shard_map/ppermute | solution.py:57
  44.8 16.8 %collective-permute-start.14 = (bf16[80,8192]{1,0:T(8,128)(2,1)S(1)}, bf16[80,8192]{1,0:T(8,128)(2,1)S(1)}, u32[]{:S(2)}, u32[]{:S(2)}) collective-permute-start(bf16[80,8192]{1,0:T(8,128)(2,1)S(1)} %collective-permute-done.6.refs_2_.refs_4_.refs_12_), channel_id=1, source_target_pairs={{0,96},{1,25},{2,98},{3,27},{4,100},{5,29},{6,102},{7,31},{8,104},... | collective-permute-start | bytes 3932168 | tf_op jit(solution)/shard_map/ppermute | solution.py:43
  48.3 12.3 %collective-permute-start.15 = (bf16[48,8192]{1,0:T(8,128)(2,1)S(1)}, bf16[48,8192]{1,0:T(8,128)(2,1)S(1)}, u32[]{:S(2)}, u32[]{:S(2)}) collective-permute-start(bf16[48,8192]{1,0:T(8,128)(2,1)S(1)} %collective-permute-done.5.refs_1_.refs_3_.refs_11_), channel_id=1, source_target_pairs={{0,32},{1,9},{2,34},{3,11},{4,36},{5,13},{6,38},{7,15},{8,40},{9,1... | collective-permute-start | bytes 2359304 | tf_op jit(solution)/shard_map/ppermute | solution.py:43
  51.5 6.1 %collective-permute-start.12 = (f32[128,512]{1,0:T(8,128)S(1)}, f32[128,512]{1,0:T(8,128)S(1)}, u32[]{:S(2)}, u32[]{:S(2)}) collective-permute-start(f32[128,512]{1,0:T(8,128)S(1)} %slice.125), channel_id=1, source_target_pairs={{0,6},{1,3},{2,4},{3,1},{4,2},{5,7},{6,0},{7,5},{8,14},{9,11},{10,... | collective-permute-start | bytes 786440 | tf_op jit(solution)/shard_map/ppermute | solution.py:57
  55.4 9.3 %collective-permute-start.13 = (f16[256,1024]{1,0:T(8,128)(2,1)S(1)}, f16[256,1024]{1,0:T(8,128)(2,1)S(1)}, u32[]{:S(2)}, u32[]{:S(2)}) collective-permute-start(f16[256,1024]{1,0:T(8,128)(2,1)S(1)} %multiply_convert_fusion), channel_id=1, source_target_pairs={{0,2},{1,7},{2,0},{3,5},{4,6},{5,3},{6,4},{7,1},{8,10},{9,15},{10,... | collective-permute-start | bytes 1572872 | tf_op jit(solution)/shard_map/ppermute | solution.py:57
  64.7 7.3 %collective-permute-start.19 = (f16[128,512]{1,0:T(8,128)(2,1)S(1)}, f16[128,512]{1,0:T(8,128)(2,1)S(1)}, u32[]{:S(2)}, u32[]{:S(2)}) collective-permute-start(f16[128,512]{1,0:T(8,128)(2,1)S(1)} %multiply_convert_fusion.4), channel_id=1, source_target_pairs={{0,6},{1,3},{2,4},{3,1},{4,2},{5,7},{6,0},{7,5},{8,14},{9,11},{10,... | collective-permute-start | bytes 393224 | tf_op jit(solution)/shard_map/ppermute | solution.py:57
  65.8 6.2 %collective-permute-start.21 = (f16[128,512]{1,0:T(8,128)(2,1)S(1)}, f16[128,512]{1,0:T(8,128)(2,1)S(1)}, u32[]{:S(2)}, u32[]{:S(2)}) collective-permute-start(f16[128,512]{1,0:T(8,128)(2,1)S(1)} %get-tuple-element.82), channel_id=1, source_target_pairs={{0,4},{2,6},{4,0},{6,2},{1,5},{3,7},{5,1},{7,3},{8,12},{10,14},{12... | collective-permute-start | bytes 393224 | tf_op jit(solution)/shard_map/ppermute | solution.py:285
  68.6 8.0 %collective-permute-start.20 = (f16[128,512]{1,0:T(8,128)(2,1)S(1)}, f16[128,512]{1,0:T(8,128)(2,1)S(1)}, u32[]{:S(2)}, u32[]{:S(2)}) collective-permute-start(f16[128,512]{1,0:T(8,128)(2,1)S(1)} %get-tuple-element.83), channel_id=1, source_target_pairs={{0,2},{1,7},{2,0},{3,5},{4,6},{5,3},{6,4},{7,1},{8,10},{9,15},{10,... | collective-permute-start | bytes 393224 | tf_op jit(solution)/shard_map/ppermute | solution.py:57
  69.1 11.5 %collective-permute-start.16 = (f16[256,512]{1,0:T(8,128)(2,1)S(1)}, f16[256,512]{1,0:T(8,128)(2,1)S(1)}, u32[]{:S(2)}, u32[]{:S(2)}) collective-permute-start(f16[256,512]{1,0:T(8,128)(2,1)S(1)} %fusion.4), channel_id=1, source_target_pairs={{0,6},{1,3},{2,4},{3,1},{4,2},{5,7},{6,0},{7,5},{8,14},{9,11},{10,... | collective-permute-start | bytes 786440 | tf_op jit(solution)/shard_map/ppermute | solution.py:57
  76.7 6.8 %collective-permute-start.22 = (f16[128,512]{1,0:T(8,128)(2,1)S(1)}, f16[128,512]{1,0:T(8,128)(2,1)S(1)}, u32[]{:S(2)}, u32[]{:S(2)}) collective-permute-start(f16[128,512]{1,0:T(8,128)(2,1)S(1)} %multiply_convert_fusion.1), channel_id=1, source_target_pairs={{0,64},{1,17},{2,66},{3,19},{4,68},{5,21},{6,70},{7,23},{8,72},{9,... | collective-permute-start | bytes 393224 | tf_op jit(solution)/shard_map/ppermute | solution.py:43
  79.1 20.4 %collective-permute-start.30 = (f32[64,4096]{1,0:T(8,128)S(1)}, f32[64,4096]{1,0:T(8,128)S(1)}, u32[]{:S(2)}, u32[]{:S(2)}) collective-permute-start(f32[64,4096]{1,0:T(8,128)S(1)} %get-tuple-element.76), channel_id=1, source_target_pairs={{0,1},{1,0},{2,3},{3,2},{4,5},{5,4},{6,7},{7,6},{8,9},{9,8},{10,11... | collective-permute-start | bytes 3145736 | tf_op jit(solution)/shard_map/ppermute | solution.py:61
  80.7 5.4 %collective-permute-start.18 = (f16[128,512]{1,0:T(8,128)(2,1)S(1)}, f16[128,512]{1,0:T(8,128)(2,1)S(1)}, u32[]{:S(2)}, u32[]{:S(2)}) collective-permute-start(f16[128,512]{1,0:T(8,128)(2,1)S(1)} %get-tuple-element.80), channel_id=1, source_target_pairs={{0,32},{1,9},{2,34},{3,11},{4,36},{5,13},{6,38},{7,15},{8,40},{9,1... | collective-permute-start | bytes 393224 | tf_op jit(solution)/shard_map/ppermute | solution.py:43
  87.2 7.0 %collective-permute-start.25 = (f32[128,512]{1,0:T(8,128)S(1)}, f32[128,512]{1,0:T(8,128)S(1)}, u32[]{:S(2)}, u32[]{:S(2)}) collective-permute-start(f32[128,512]{1,0:T(8,128)S(1)} %pad_maximum_fusion.5), channel_id=1, source_target_pairs={{0,8},{1,33},{2,10},{3,35},{4,12},{5,37},{6,14},{7,39},{8,16},{9,4... | collective-permute-start | bytes 786440 | tf_op jit(solution)/shard_map/ppermute | solution.py:43
  87.6 10.4 %collective-permute-start.26 = (f32[128,512]{1,0:T(8,128)S(1)}, f32[128,512]{1,0:T(8,128)S(1)}, u32[]{:S(2)}, u32[]{:S(2)}) collective-permute-start(f32[128,512]{1,0:T(8,128)S(1)} %pad_maximum_fusion.6), channel_id=1, source_target_pairs={{0,16},{1,65},{2,18},{3,67},{4,20},{5,69},{6,22},{7,71},{8,24},{9,... | collective-permute-start | bytes 786440 | tf_op jit(solution)/shard_map/ppermute | solution.py:43
  91.5 6.8 %collective-permute-start.24 = (f32[128,512]{1,0:T(8,128)S(1)}, f32[128,512]{1,0:T(8,128)S(1)}, u32[]{:S(2)}, u32[]{:S(2)}) collective-permute-start(f32[128,512]{1,0:T(8,128)S(1)} %pad_maximum_fusion.4), channel_id=1, source_target_pairs={{0,24},{1,97},{2,26},{3,99},{4,28},{5,101},{6,30},{7,103},{8,0},{9... | collective-permute-start | bytes 786440 | tf_op jit(solution)/shard_map/ppermute | solution.py:43
  (11 other events, 83.8 us)

commit v6 on v5

--- a/solution.py
+++ b/solution.py
@@ -275,7 +275,7 @@
     keep_1, send_1 = ladder(tab, a_list[2:6], w_own, w_other)
     got_1 = across_x(coded(send_1), True)
     keep_2, send_2 = ladder(tab, a_list[6:], w_own, w_other)
-    got_1, keep_2, send_2 = hold((got_1, keep_2, send_2))
+    got_1 = hold((got_1, keep_2, send_2))[0]
     sum_1, fwd_1 = halves(keep_1, got_1)
     end_1 = across_x(fwd_1, False)
     far_parts = [coded(keep_2[:, mid:]), coded(send_2[:, :mid]), coded(send_2[:, mid:])]

time: 102 us -> 105 us (1.029)
  starting transfers between devices: 39.1 us -> 49.3 us
  waiting for transfers between devices: 35.2 us -> 29 us
    ppermute x8, starting transfers between devices: 7.79 us -> 16.4 us  [other_core(): return lax.ppermute(value, 'core', [(0, 1), (1, 0)])]
    ppermute x16, waiting for transfers between devices: 25 us -> 19.3 us  [along(): return lax.ppermute(value, AXES, perm_of(first, step))]
    ppermute x6, waiting for transfers between devices: 8.87 us -> 6.79 us  [across_x(): return lax.ppermute(value, AXES, pairs)]
    ppermute x1, waiting for transfers between devices: 0.07 us -> 1.34 us  [local(): lax.ppermute(far_parts[2], 'x', [(i, (i + 2) % RING) for i in range(RING)])]
    ppermute x16, starting transfers between devices: 21.7 us -> 23 us  [along(): return lax.ppermute(value, AXES, perm_of(first, step))]
  transfers between devices with their start and end apart: 31 -> 31, of which waited for: 14 -> 11; matrix products, arithmetic and copies ran while one was open for 4% -> 4% of each run, Pallas kernels for 19% -> 18%
where the time goes in v6:
time: 105 us
  starting transfers between devices  49.3 us (47%)
  waiting for transfers between devices  29 us (28%)
  Pallas kernels  20.8 us (20%)
  other arithmetic  3.37 us (3%)
  local copies, waits for them, and re-layouts  1.37 us (1%)
    ppermute x16, starting transfers between devices, along(): return lax.ppermute(value, AXES, perm_of(first, step))  23 us
    ppermute x16, waiting for transfers between devices, along(): return lax.ppermute(value, AXES, perm_of(first, step))  19.3 us
    ppermute x8, starting transfers between devices, other_core(): return lax.ppermute(value, 'core', [(0, 1), (1, 0)])  16.4 us
    pallas_call x2, Pallas kernels, select(): pl.pallas_call(functools.partial(select_kernel, first_block=first_block),...  9.44 us
    ppermute x6, starting transfers between devices, across_x(): return lax.ppermute(value, AXES, pairs)  7.31 us
    pallas_call x3, Pallas kernels, ladder(): pl.pallas_call(functools.partial(ladder_kernel, n=n), in_specs=[pl.BlockS...  7.05 us
    ppermute x6, waiting for transfers between devices, across_x(): return lax.ppermute(value, AXES, pairs)  6.79 us
    pallas_call x1, Pallas kernels, hole_part(): pl.pallas_call(hole_kernel, grid=(steps,), in_specs=[pl.BlockSpec(h_rel.s...  2.89 us
  transfers between devices with their start and end apart: 31, of which 11 were waited for; matrix products, arithmetic and copies ran while one was open for 4% of the time, Pallas kernels for 18%

profile of v6, /device:TPU:1, one launch (start us, length us, event | category | flops | bytes accessed | tf_op | source)
XLA Modules:
  0.0 105.3 jit_solution(5360397072372915086)
XLA Ops:
  6.8 2.2 %collective-permute-start.1 = (bf16[32,8192]{1,0:T(8,128)(2,1)S(1)}, bf16[32,8192]{1,0:T(8,128)(2,1)S(1)}, u32[]{:S(2)}, u32[]{:S(2)}) collective-permute-start(bf16[32,8192]{1,0:T(8,128)(2,1)S(1)} %pad_maximum_fusion.2), channel_id=1, source_target_pairs={{0,24},{1,97},{2,26},{3,99},{4,28},{5,101},{6,30},{7,103},{8,0},{9... | collective-permute-start | bytes 1572872 | tf_op jit(solution)/shard_map/ppermute | solution.py:43
  9.6 4.7 %select.123.refs_2_.refs_4_ = bf16[16,256,128]{2,1,0:T(8,128)(2,1)S(1)} custom-call(s32[256]{0:T(256)S(1)} %select_n.335.tab, bf16[32768,256]{1,0:T(8,128)(2,1)} %bitcast.8), custom_call_target="tpu_custom_call" | custom-call | flops 1024 | bytes 1024 | tf_op jit(solution)/shard_map/select/pallas_call | solution.py:88
  15.6 3.1 %collective-permute-start.3 = (bf16[16,8192]{1,0:T(8,128)(2,1)S(1)}, bf16[16,8192]{1,0:T(8,128)(2,1)S(1)}, u32[]{:S(2)}, u32[]{:S(2)}) collective-permute-start(bf16[16,8192]{1,0:T(8,128)(2,1)S(1)} %slice.95), channel_id=1, source_target_pairs={{0,24},{1,97},{2,26},{3,99},{4,28},{5,101},{6,30},{7,103},{8,0},{9... | collective-permute-start | bytes 786440 | tf_op jit(solution)/shard_map/ppermute | solution.py:43
  23.5 4.7 %select.124.refs_3_.refs_5_ = bf16[16,256,128]{2,1,0:T(8,128)(2,1)S(1)} custom-call(s32[256]{0:T(256)S(1)} %select_n.335.tab, bf16[32768,256]{1,0:T(8,128)(2,1)} %bitcast.9), custom_call_target="tpu_custom_call" | custom-call | flops 1024 | bytes 1024 | tf_op jit(solution)/shard_map/select/pallas_call | solution.py:88
  29.4 2.7 %collective-permute-start.10 = (bf16[48,8192]{1,0:T(8,128)(2,1)S(1)}, bf16[48,8192]{1,0:T(8,128)(2,1)S(1)}, u32[]{:S(2)}, u32[]{:S(2)}) collective-permute-start(bf16[48,8192]{1,0:T(8,128)(2,1)S(1)} %pad_maximum_fusion.1.refs_1_.refs_9_), channel_id=1, source_target_pairs={{0,96},{1,25},{2,98},{3,27},{4,100},{5,29},{6,102},{7,31},{8,104},... | collective-permute-start | bytes 2359304 | tf_op jit(solution)/shard_map/ppermute | solution.py:43
  32.6 7.1 %collective-permute-done.7.refs_0_.refs_2_.refs_10_ = bf16[80,8192]{1,0:T(8,128)(2,1)S(1)} collective-permute-done((bf16[80,8192]{1,0:T(8,128)(2,1)S(1)}, bf16[80,8192]{1,0:T(8,128)(2,1)S(1)}, u32[]{:S(2)}, u32[]{:S(2)}) %collective-permute-start.7) | collective-permute-done | bytes 1310752 | tf_op jit(solution)/shard_map/ppermute | solution.py:43
  39.9 2.0 %ladder.3 = (f32[128,1024]{1,0:T(8,128)S(1)}, f32[128,1024]{1,0:T(8,128)S(1)}) custom-call(s32[256]{0:T(256)S(1)} %select_n.335.tab, bf16[80,8192]{1,0:T(8,128)(2,1)S(1)} %pad_maximum_fusion.refs_0_.refs_8_, bf16[48,8192]{1,0:T(8,128)(2,1)S(1)} %pad_maximum_fusion.1.refs_1_.refs_9_, bf16[16,256,128]{2,1,0:T(8,128)(2,1)S(1)} %select.123.refs_2_.refs_4_, ...), custom_call_target="tpu_custom_call" | custom-call | flops 1024 | bytes 1024 | tf_op jit(solution)/shard_map/ladder/pallas_call | solution.py:120
  41.9 2.6 %collective-permute-start.11 = (f32[128,1024]{1,0:T(8,128)S(1)}, f32[128,1024]{1,0:T(8,128)S(1)}, u32[]{:S(2)}, u32[]{:S(2)}) collective-permute-start(f32[128,1024]{1,0:T(8,128)S(1)} %get-tuple-element.50), channel_id=1, source_target_pairs={{0,2},{1,7},{2,0},{3,5},{4,6},{5,3},{6,4},{7,1},{8,10},{9,15},{10,... | collective-permute-start | bytes 1572872 | tf_op jit(solution)/shard_map/ppermute | solution.py:57
  44.5 3.4 %collective-permute-done.5.refs_1_.refs_3_.refs_11_ = bf16[48,8192]{1,0:T(8,128)(2,1)S(1)} collective-permute-done((bf16[48,8192]{1,0:T(8,128)(2,1)S(1)}, bf16[48,8192]{1,0:T(8,128)(2,1)S(1)}, u32[]{:S(2)}, u32[]{:S(2)}) %collective-permute-start.5) | collective-permute-done | bytes 786464 | tf_op jit(solution)/shard_map/ppermute | solution.py:43
  47.9 3.3 %collective-permute-done.11 = f32[128,1024]{1,0:T(8,128)S(1)} collective-permute-done((f32[128,1024]{1,0:T(8,128)S(1)}, f32[128,1024]{1,0:T(8,128)S(1)}, u32[]{:S(2)}, u32[]{:S(2)}) %collective-permute-start.11) | collective-permute-done | bytes 524320 | tf_op jit(solution)/shard_map/ppermute | solution.py:57
  51.9 3.1 %ladder.4 = (f32[256,1024]{1,0:T(8,128)S(1)}, f32[256,1024]{1,0:T(8,128)S(1)}) custom-call(s32[256]{0:T(256)S(1)} %select_n.335.tab, bf16[80,8192]{1,0:T(8,128)(2,1)S(1)} %collective-permute-done.7.refs_0_.refs_2_.refs_10_, bf16[48,8192]{1,0:T(8,128)(2,1)S(1)} %collective-permute-done.5.refs_1_.refs_3_.refs_11_, ...), custom_call_target="tpu_custom_call" | custom-call | flops 1024 | bytes 1024 | tf_op jit(solution)/shard_map/ladder/pallas_call | solution.py:120
  55.1 2.3 %collective-permute-start.13 = (f16[256,1024]{1,0:T(8,128)(2,1)S(1)}, f16[256,1024]{1,0:T(8,128)(2,1)S(1)}, u32[]{:S(2)}, u32[]{:S(2)}) collective-permute-start(f16[256,1024]{1,0:T(8,128)(2,1)S(1)} %multiply_convert_fusion), channel_id=1, source_target_pairs={{0,2},{1,7},{2,0},{3,5},{4,6},{5,3},{6,4},{7,1},{8,10},{9,15},{10,... | collective-permute-start | bytes 1572872 | tf_op jit(solution)/shard_map/ppermute | solution.py:57
  57.5 2.8 %collective-permute-done.15.refs_1_.refs_7_.refs_15_ = bf16[48,8192]{1,0:T(8,128)(2,1)S(1)} collective-permute-done((bf16[48,8192]{1,0:T(8,128)(2,1)S(1)}, bf16[48,8192]{1,0:T(8,128)(2,1)S(1)}, u32[]{:S(2)}, u32[]{:S(2)}) %collective-permute-start.15) | collective-permute-done | bytes 786464 | tf_op jit(solution)/shard_map/ppermute | solution.py:43
  60.2 2.0 %ladder.5 = (f32[128,1024]{1,0:T(8,128)S(1)}, f32[128,1024]{1,0:T(8,128)S(1)}) custom-call(s32[256]{0:T(256)S(1)} %select_n.335.tab, bf16[80,8192]{1,0:T(8,128)(2,1)S(1)} %collective-permute-done.14.refs_0_.refs_6_.refs_14_, bf16[48,8192]{1,0:T(8,128)(2,1)S(1)} %collective-permute-done.15.refs_1_.refs_7_.refs_15_, ...), custom_call_target="tpu_custom_call" | custom-call | flops 1024 | bytes 1024 | tf_op jit(solution)/shard_map/ladder/pallas_call | solution.py:120
  63.6 2.5 %collective-permute-start.21 = (f16[128,512]{1,0:T(8,128)(2,1)S(1)}, f16[128,512]{1,0:T(8,128)(2,1)S(1)}, u32[]{:S(2)}, u32[]{:S(2)}) collective-permute-start(f16[128,512]{1,0:T(8,128)(2,1)S(1)} %get-tuple-element.78), channel_id=1, source_target_pairs={{0,4},{2,6},{4,0},{6,2},{1,5},{3,7},{5,1},{7,3},{8,12},{10,14},{12... | collective-permute-start | bytes 393224 | tf_op jit(solution)/shard_map/ppermute | solution.py:285
  66.8 2.9 %hole.1 = (f32[64,4096]{1,0:T(8,128)S(1)}, f32[64,4096]{1,0:T(8,128)S(1)}) custom-call(bf16[64,512]{1,0:T(8,128)(2,1)S(1)} %fusion.2.h_ref, bf16[80,8192]{1,0:T(8,128)(2,1)S(1)} %pad_maximum_fusion.refs_0_.refs_8_, bf16[48,8192]{1,0:T(8,128)(2,1)S(1)} %pad_maximum_fusion.1.refs_1_.refs_9_, ...), custom_call_target="tpu_custom_call" | custom-call | flops 68719476736 | bytes 67108864 | tf_op jit(solution)/shard_map/hole/pallas_call | solution.py:144
  71.1 3.5 %collective-permute-done.20 = f16[128,512]{1,0:T(8,128)(2,1)S(1)} collective-permute-done((f16[128,512]{1,0:T(8,128)(2,1)S(1)}, f16[128,512]{1,0:T(8,128)(2,1)S(1)}, u32[]{:S(2)}, u32[]{:S(2)}) %collective-permute-start.20) | collective-permute-done | bytes 131104 | tf_op jit(solution)/shard_map/ppermute | solution.py:57
  76.1 2.1 %collective-permute-start.30 = (f32[64,4096]{1,0:T(8,128)S(1)}, f32[64,4096]{1,0:T(8,128)S(1)}, u32[]{:S(2)}, u32[]{:S(2)}) collective-permute-start(f32[64,4096]{1,0:T(8,128)S(1)} %get-tuple-element.72), channel_id=1, source_target_pairs={{0,1},{1,0},{2,3},{3,2},{4,5},{5,4},{6,7},{7,6},{8,9},{9,8},{10,11... | collective-permute-start | bytes 3145736 | tf_op jit(solution)/shard_map/ppermute | solution.py:61
  78.8 3.8 %collective-permute-start.17 = (f16[128,512]{1,0:T(8,128)(2,1)S(1)}, f16[128,512]{1,0:T(8,128)(2,1)S(1)}, u32[]{:S(2)}, u32[]{:S(2)}) collective-permute-start(f16[128,512]{1,0:T(8,128)(2,1)S(1)} %get-tuple-element.77), channel_id=1, source_target_pairs={{0,96},{1,25},{2,98},{3,27},{4,100},{5,29},{6,102},{7,31},{8,104},... | collective-permute-start | bytes 393224 | tf_op jit(solution)/shard_map/ppermute | solution.py:43
  82.6 2.5 %collective-permute-done.18 = f16[128,512]{1,0:T(8,128)(2,1)S(1)} collective-permute-done((f16[128,512]{1,0:T(8,128)(2,1)S(1)}, f16[128,512]{1,0:T(8,128)(2,1)S(1)}, u32[]{:S(2)}, u32[]{:S(2)}) %collective-permute-start.18) | collective-permute-done | bytes 131104 | tf_op jit(solution)/shard_map/ppermute | solution.py:43
  87.0 4.2 %collective-permute-start.26 = (f32[128,512]{1,0:T(8,128)S(1)}, f32[128,512]{1,0:T(8,128)S(1)}, u32[]{:S(2)}, u32[]{:S(2)}) collective-permute-start(f32[128,512]{1,0:T(8,128)S(1)} %pad_maximum_fusion.6), channel_id=1, source_target_pairs={{0,16},{1,65},{2,18},{3,67},{4,20},{5,69},{6,22},{7,71},{8,24},{9,... | collective-permute-start | bytes 786440 | tf_op jit(solution)/shard_map/ppermute | solution.py:43
  91.2 2.4 %collective-permute-done.25.refs_2_ = f32[128,512]{1,0:T(8,128)S(1)} collective-permute-done((f32[128,512]{1,0:T(8,128)S(1)}, f32[128,512]{1,0:T(8,128)S(1)}, u32[]{:S(2)}, u32[]{:S(2)}) %collective-permute-start.25) | collective-permute-done | bytes 262176 | tf_op jit(solution)/shard_map/ppermute | solution.py:43
  93.6 4.4 %collective-permute-start.28 = (f32[128,512]{1,0:T(8,128)S(1)}, f32[128,512]{1,0:T(8,128)S(1)}, u32[]{:S(2)}, u32[]{:S(2)}) collective-permute-start(f32[128,512]{1,0:T(8,128)S(1)} %collective-permute-done.25.refs_2_), channel_id=1, source_target_pairs={{0,1},{1,0},{2,3},{3,2},{4,5},{5,4},{6,7},{7,6},{8,9},{9,8},{10,11... | collective-permute-start | bytes 786440 | tf_op jit(solution)/shard_map/ppermute | solution.py:61
  98.1 4.3 %collective-permute-start.29 = (f32[128,512]{1,0:T(8,128)S(1)}, f32[128,512]{1,0:T(8,128)S(1)}, u32[]{:S(2)}, u32[]{:S(2)}) collective-permute-start(f32[128,512]{1,0:T(8,128)S(1)} %collective-permute-done.26.refs_3_), channel_id=1, source_target_pairs={{0,1},{1,0},{2,3},{3,2},{4,5},{5,4},{6,7},{7,6},{8,9},{9,8},{10,11... | collective-permute-start | bytes 786440 | tf_op jit(solution)/shard_map/ppermute | solution.py:61
  (94 shorter events, 25.7 us)
Async XLA Ops:
  5.0 10.5 %collective-permute-start.2 = (bf16[32,8192]{1,0:T(8,128)(2,1)S(1)}, bf16[32,8192]{1,0:T(8,128)(2,1)S(1)}, u32[]{:S(2)}, u32[]{:S(2)}) collective-permute-start(bf16[32,8192]{1,0:T(8,128)(2,1)S(1)} %pad_maximum_fusion.2), channel_id=1, source_target_pairs={{0,8},{1,33},{2,10},{3,35},{4,12},{5,37},{6,14},{7,39},{8,16},{9,4... | collective-permute-start | bytes 1572872 | tf_op jit(solution)/shard_map/ppermute | solution.py:43
  6.8 8.7 %collective-permute-start.1 = (bf16[32,8192]{1,0:T(8,128)(2,1)S(1)}, bf16[32,8192]{1,0:T(8,128)(2,1)S(1)}, u32[]{:S(2)}, u32[]{:S(2)}) collective-permute-start(bf16[32,8192]{1,0:T(8,128)(2,1)S(1)} %pad_maximum_fusion.2), channel_id=1, source_target_pairs={{0,24},{1,97},{2,26},{3,99},{4,28},{5,101},{6,30},{7,103},{8,0},{9... | collective-permute-start | bytes 1572872 | tf_op jit(solution)/shard_map/ppermute | solution.py:43
  15.6 12.6 %collective-permute-start.3 = (bf16[16,8192]{1,0:T(8,128)(2,1)S(1)}, bf16[16,8192]{1,0:T(8,128)(2,1)S(1)}, u32[]{:S(2)}, u32[]{:S(2)}) collective-permute-start(bf16[16,8192]{1,0:T(8,128)(2,1)S(1)} %slice.95), channel_id=1, source_target_pairs={{0,24},{1,97},{2,26},{3,99},{4,28},{5,101},{6,30},{7,103},{8,0},{9... | collective-permute-start | bytes 786440 | tf_op jit(solution)/shard_map/ppermute | solution.py:43
  18.7 9.5 %collective-permute-start.4 = (bf16[16,8192]{1,0:T(8,128)(2,1)S(1)}, bf16[16,8192]{1,0:T(8,128)(2,1)S(1)}, u32[]{:S(2)}, u32[]{:S(2)}) collective-permute-start(bf16[16,8192]{1,0:T(8,128)(2,1)S(1)} %get-tuple-element.80), channel_id=1, source_target_pairs={{0,8},{1,33},{2,10},{3,35},{4,12},{5,37},{6,14},{7,39},{8,16},{9,4... | collective-permute-start | bytes 786440 | tf_op jit(solution)/shard_map/ppermute | solution.py:43
  18.8 20.9 %collective-permute-start.7 = (bf16[80,8192]{1,0:T(8,128)(2,1)S(1)}, bf16[80,8192]{1,0:T(8,128)(2,1)S(1)}, u32[]{:S(2)}, u32[]{:S(2)}) collective-permute-start(bf16[80,8192]{1,0:T(8,128)(2,1)S(1)} %pad_maximum_fusion.refs_0_.refs_8_), channel_id=1, source_target_pairs={{0,32},{1,9},{2,34},{3,11},{4,36},{5,13},{6,38},{7,15},{8,40},{9,1... | collective-permute-start | bytes 3932168 | tf_op jit(solution)/shard_map/ppermute | solution.py:43
  19.8 19.8 %collective-permute-start.6 = (bf16[80,8192]{1,0:T(8,128)(2,1)S(1)}, bf16[80,8192]{1,0:T(8,128)(2,1)S(1)}, u32[]{:S(2)}, u32[]{:S(2)}) collective-permute-start(bf16[80,8192]{1,0:T(8,128)(2,1)S(1)} %pad_maximum_fusion.refs_0_.refs_8_), channel_id=1, source_target_pairs={{0,96},{1,25},{2,98},{3,27},{4,100},{5,29},{6,102},{7,31},{8,104},... | collective-permute-start | bytes 3932168 | tf_op jit(solution)/shard_map/ppermute | solution.py:43
  21.7 7.7 %collective-permute-start.8 = (bf16[16,256,128]{2,1,0:T(8,128)(2,1)S(1)}, bf16[16,256,128]{2,1,0:T(8,128)(2,1)S(1)}, u32[]{:S(2)}, u32[]{:S(2)}) collective-permute-start(bf16[16,256,128]{2,1,0:T(8,128)(2,1)S(1)} %select.123.refs_2_.refs_4_), channel_id=1, source_target_pairs={{0,1},{1,0},{2,3},{3,2},{4,5},{5,4},{6,7},{7,6},{8,9},{9,8},{10,11... | collective-permute-start | bytes 3145736 | tf_op jit(solution)/shard_map/ppermute | solution.py:61
  29.3 18.6 %collective-permute-start.5 = (bf16[48,8192]{1,0:T(8,128)(2,1)S(1)}, bf16[48,8192]{1,0:T(8,128)(2,1)S(1)}, u32[]{:S(2)}, u32[]{:S(2)}) collective-permute-start(bf16[48,8192]{1,0:T(8,128)(2,1)S(1)} %pad_maximum_fusion.1.refs_1_.refs_9_), channel_id=1, source_target_pairs={{0,32},{1,9},{2,34},{3,11},{4,36},{5,13},{6,38},{7,15},{8,40},{9,1... | collective-permute-start | bytes 2359304 | tf_op jit(solution)/shard_map/ppermute | solution.py:43
  29.4 18.5 %collective-permute-start.10 = (bf16[48,8192]{1,0:T(8,128)(2,1)S(1)}, bf16[48,8192]{1,0:T(8,128)(2,1)S(1)}, u32[]{:S(2)}, u32[]{:S(2)}) collective-permute-start(bf16[48,8192]{1,0:T(8,128)(2,1)S(1)} %pad_maximum_fusion.1.refs_1_.refs_9_), channel_id=1, source_target_pairs={{0,96},{1,25},{2,98},{3,27},{4,100},{5,29},{6,102},{7,31},{8,104},... | collective-permute-start | bytes 2359304 | tf_op jit(solution)/shard_map/ppermute | solution.py:43
  39.7 20.5 %collective-permute-start.14 = (bf16[80,8192]{1,0:T(8,128)(2,1)S(1)}, bf16[80,8192]{1,0:T(8,128)(2,1)S(1)}, u32[]{:S(2)}, u32[]{:S(2)}) collective-permute-start(bf16[80,8192]{1,0:T(8,128)(2,1)S(1)} %collective-permute-done.6.refs_2_.refs_4_.refs_12_), channel_id=1, source_target_pairs={{0,96},{1,25},{2,98},{3,27},{4,100},{5,29},{6,102},{7,31},{8,104},... | collective-permute-start | bytes 3932168 | tf_op jit(solution)/shard_map/ppermute | solution.py:43
  41.9 9.3 %collective-permute-start.11 = (f32[128,1024]{1,0:T(8,128)S(1)}, f32[128,1024]{1,0:T(8,128)S(1)}, u32[]{:S(2)}, u32[]{:S(2)}) collective-permute-start(f32[128,1024]{1,0:T(8,128)S(1)} %get-tuple-element.50), channel_id=1, source_target_pairs={{0,2},{1,7},{2,0},{3,5},{4,6},{5,3},{6,4},{7,1},{8,10},{9,15},{10,... | collective-permute-start | bytes 1572872 | tf_op jit(solution)/shard_map/ppermute | solution.py:57
  47.9 12.3 %collective-permute-start.15 = (bf16[48,8192]{1,0:T(8,128)(2,1)S(1)}, bf16[48,8192]{1,0:T(8,128)(2,1)S(1)}, u32[]{:S(2)}, u32[]{:S(2)}) collective-permute-start(bf16[48,8192]{1,0:T(8,128)(2,1)S(1)} %collective-permute-done.5.refs_1_.refs_3_.refs_11_), channel_id=1, source_target_pairs={{0,32},{1,9},{2,34},{3,11},{4,36},{5,13},{6,38},{7,15},{8,40},{9,1... | collective-permute-start | bytes 2359304 | tf_op jit(solution)/shard_map/ppermute | solution.py:43
  55.1 11.2 %collective-permute-start.13 = (f16[256,1024]{1,0:T(8,128)(2,1)S(1)}, f16[256,1024]{1,0:T(8,128)(2,1)S(1)}, u32[]{:S(2)}, u32[]{:S(2)}) collective-permute-start(f16[256,1024]{1,0:T(8,128)(2,1)S(1)} %multiply_convert_fusion), channel_id=1, source_target_pairs={{0,2},{1,7},{2,0},{3,5},{4,6},{5,3},{6,4},{7,1},{8,10},{9,15},{10,... | collective-permute-start | bytes 1572872 | tf_op jit(solution)/shard_map/ppermute | solution.py:57
  62.3 7.5 %collective-permute-start.19 = (f16[128,512]{1,0:T(8,128)(2,1)S(1)}, f16[128,512]{1,0:T(8,128)(2,1)S(1)}, u32[]{:S(2)}, u32[]{:S(2)}) collective-permute-start(f16[128,512]{1,0:T(8,128)(2,1)S(1)} %multiply_convert_fusion.4), channel_id=1, source_target_pairs={{0,6},{1,3},{2,4},{3,1},{4,2},{5,7},{6,0},{7,5},{8,14},{9,11},{10,... | collective-permute-start | bytes 393224 | tf_op jit(solution)/shard_map/ppermute | solution.py:57
  63.6 7.5 %collective-permute-start.21 = (f16[128,512]{1,0:T(8,128)(2,1)S(1)}, f16[128,512]{1,0:T(8,128)(2,1)S(1)}, u32[]{:S(2)}, u32[]{:S(2)}) collective-permute-start(f16[128,512]{1,0:T(8,128)(2,1)S(1)} %get-tuple-element.78), channel_id=1, source_target_pairs={{0,4},{2,6},{4,0},{6,2},{1,5},{3,7},{5,1},{7,3},{8,12},{10,14},{12... | collective-permute-start | bytes 393224 | tf_op jit(solution)/shard_map/ppermute | solution.py:285
  66.1 8.4 %collective-permute-start.20 = (f16[128,512]{1,0:T(8,128)(2,1)S(1)}, f16[128,512]{1,0:T(8,128)(2,1)S(1)}, u32[]{:S(2)}, u32[]{:S(2)}) collective-permute-start(f16[128,512]{1,0:T(8,128)(2,1)S(1)} %get-tuple-element.79), channel_id=1, source_target_pairs={{0,2},{1,7},{2,0},{3,5},{4,6},{5,3},{6,4},{7,1},{8,10},{9,15},{10,... | collective-permute-start | bytes 393224 | tf_op jit(solution)/shard_map/ppermute | solution.py:57
  66.6 11.6 %collective-permute-start.16 = (f16[256,512]{1,0:T(8,128)(2,1)S(1)}, f16[256,512]{1,0:T(8,128)(2,1)S(1)}, u32[]{:S(2)}, u32[]{:S(2)}) collective-permute-start(f16[256,512]{1,0:T(8,128)(2,1)S(1)} %fusion.4), channel_id=1, source_target_pairs={{0,6},{1,3},{2,4},{3,1},{4,2},{5,7},{6,0},{7,5},{8,14},{9,11},{10,... | collective-permute-start | bytes 786440 | tf_op jit(solution)/shard_map/ppermute | solution.py:57
  74.6 8.0 %collective-permute-start.22 = (f16[128,512]{1,0:T(8,128)(2,1)S(1)}, f16[128,512]{1,0:T(8,128)(2,1)S(1)}, u32[]{:S(2)}, u32[]{:S(2)}) collective-permute-start(f16[128,512]{1,0:T(8,128)(2,1)S(1)} %multiply_convert_fusion.1), channel_id=1, source_target_pairs={{0,64},{1,17},{2,66},{3,19},{4,68},{5,21},{6,70},{7,23},{8,72},{9,... | collective-permute-start | bytes 393224 | tf_op jit(solution)/shard_map/ppermute | solution.py:43
  76.1 27.4 %collective-permute-start.30 = (f32[64,4096]{1,0:T(8,128)S(1)}, f32[64,4096]{1,0:T(8,128)S(1)}, u32[]{:S(2)}, u32[]{:S(2)}) collective-permute-start(f32[64,4096]{1,0:T(8,128)S(1)} %get-tuple-element.72), channel_id=1, source_target_pairs={{0,1},{1,0},{2,3},{3,2},{4,5},{5,4},{6,7},{7,6},{8,9},{9,8},{10,11... | collective-permute-start | bytes 3145736 | tf_op jit(solution)/shard_map/ppermute | solution.py:61
  78.3 6.9 %collective-permute-start.18 = (f16[128,512]{1,0:T(8,128)(2,1)S(1)}, f16[128,512]{1,0:T(8,128)(2,1)S(1)}, u32[]{:S(2)}, u32[]{:S(2)}) collective-permute-start(f16[128,512]{1,0:T(8,128)(2,1)S(1)} %get-tuple-element.76), channel_id=1, source_target_pairs={{0,32},{1,9},{2,34},{3,11},{4,36},{5,13},{6,38},{7,15},{8,40},{9,1... | collective-permute-start | bytes 393224 | tf_op jit(solution)/shard_map/ppermute | solution.py:43
  86.9 6.7 %collective-permute-start.25 = (f32[128,512]{1,0:T(8,128)S(1)}, f32[128,512]{1,0:T(8,128)S(1)}, u32[]{:S(2)}, u32[]{:S(2)}) collective-permute-start(f32[128,512]{1,0:T(8,128)S(1)} %pad_maximum_fusion.5), channel_id=1, source_target_pairs={{0,8},{1,33},{2,10},{3,35},{4,12},{5,37},{6,14},{7,39},{8,16},{9,4... | collective-permute-start | bytes 786440 | tf_op jit(solution)/shard_map/ppermute | solution.py:43
  87.0 11.1 %collective-permute-start.26 = (f32[128,512]{1,0:T(8,128)S(1)}, f32[128,512]{1,0:T(8,128)S(1)}, u32[]{:S(2)}, u32[]{:S(2)}) collective-permute-start(f32[128,512]{1,0:T(8,128)S(1)} %pad_maximum_fusion.6), channel_id=1, source_target_pairs={{0,16},{1,65},{2,18},{3,67},{4,20},{5,69},{6,22},{7,71},{8,24},{9,... | collective-permute-start | bytes 786440 | tf_op jit(solution)/shard_map/ppermute | solution.py:43
  91.2 11.2 %collective-permute-start.24 = (f32[128,512]{1,0:T(8,128)S(1)}, f32[128,512]{1,0:T(8,128)S(1)}, u32[]{:S(2)}, u32[]{:S(2)}) collective-permute-start(f32[128,512]{1,0:T(8,128)S(1)} %pad_maximum_fusion.4), channel_id=1, source_target_pairs={{0,24},{1,97},{2,26},{3,99},{4,28},{5,101},{6,30},{7,103},{8,0},{9... | collective-permute-start | bytes 786440 | tf_op jit(solution)/shard_map/ppermute | solution.py:43
  93.6 8.7 %collective-permute-start.28 = (f32[128,512]{1,0:T(8,128)S(1)}, f32[128,512]{1,0:T(8,128)S(1)}, u32[]{:S(2)}, u32[]{:S(2)}) collective-permute-start(f32[128,512]{1,0:T(8,128)S(1)} %collective-permute-done.25.refs_2_), channel_id=1, source_target_pairs={{0,1},{1,0},{2,3},{3,2},{4,5},{5,4},{6,7},{7,6},{8,9},{9,8},{10,11... | collective-permute-start | bytes 786440 | tf_op jit(solution)/shard_map/ppermute | solution.py:61
  (11 other events, 98.4 us)
